TPU v7x, 128 devices: a whole 4x4x4 slice. The times are simulated.
128 devices in a mesh: section: 8 (over y, x_hi), dp: 4 (over x_lo, core), tensor: 4 (over z).
Axes of the slice: x: 4 (x_hi: 2, x_lo: 2; x = x_hi * 2 + x_lo), y: 4, z: 4, core: 2. Of those that a mesh axis runs over, the one named last changes fastest.
Arguments:
- earlier_inputs: bfloat16 [8, 2048, 12288], P('section', 'dp'), may hold values from -6 to 6
- earlier_grads: bfloat16 [8, 2048, 2048], P('section', 'dp', 'tensor'), may hold values from -6 to 6
- current_grads: bfloat16 [8, 2048, 2048], P('section', 'dp', 'tensor'), may hold values from -6 to 6
- key_value_weight: bfloat16 [8, 12288, 2048], P('section', 'dp', 'tensor'), may hold values from -0.078125 to 0.078125
- exponents: int32 [8, 96, 2048], P('section', 'tensor', 'dp'), may hold values from -11 to -9
- sign_bits: int32 [12288], P('tensor'), may hold values from 0 to 1
Outputs:
- upstream_grad: bfloat16 [8, 12288, 2048], P('section', 'tensor', 'dp')
- weight_grad: float32 [8, 12288, 2048], P('section', 'dp', 'tensor')
Inputs may be any that keep to these rules, and one draw needn't show every extreme that they name: exponents of the power-of-two scales.
All inputs are finite; a program needn't handle non-finite values.
Results may differ from a plain program's by a relative error of at most 0.0038.
Values may be sent and summed in bfloat16 or wider, within the bound.
No kernel may reach another device: no remote copies, remote signals or barrier semaphores. Data moves between devices by JAX's collectives and lax.ppermute only.
A program may use at most 192 MiB of HBM per device.

v0:
```python
import jax
import jax.numpy as jnp
from jax import lax
from jax.sharding import PartitionSpec as P

HB = 128


fp8_limit = 448.0


def from_behind(shard, axis, by):
    peers = lax.axis_size(axis)
    pairs = [(i, i + by) for i in range(peers) if 0 <= i + by < peers]
    return lax.ppermute(shard, axis, pairs)


def hadamard_table(order):
    index = jnp.arange(order, dtype=jnp.int32)
    table = jnp.ones((order, order), jnp.float32)
    for bit_pos in range(order.bit_length() - 1):
        both = (index[:, None] >> bit_pos & 1) * (index[None, :] >> bit_pos & 1)
        table = table * (1.0 - 2.0 * both.astype(jnp.float32))
    return table / jnp.sqrt(jnp.float32(order))


def body(earlier_inputs, earlier_grads, current_grads, key_value_weight, exponents, sign_bits):
    inputs_local = earlier_inputs[0]
    grads_before = earlier_grads[0]
    grads_now = current_grads[0]
    weight_local = key_value_weight[0]
    expo_local = exponents[0]
    table = hadamard_table(HB)
    signs = (2 * sign_bits - 1).astype(jnp.float32)
    tokens_here = grads_now.shape[0]
    partial_grad = lax.dot_general(
        lax.all_gather(weight_local, "dp", axis=0, tiled=True),
        grads_now,
        (((1,), (1,)), ((), ())),
        preferred_element_type=jnp.float32,
    )
    input_grad = lax.psum_scatter(partial_grad, "tensor", scatter_dimension=0, tiled=True)
    blocks = (input_grad * signs[:, None]).reshape(-1, HB, tokens_here)
    rotated = jnp.einsum("ij,bjt->bit", table, blocks, precision=lax.Precision.HIGHEST)
    scale = jnp.exp2(-expo_local.astype(jnp.float32))
    coded = jnp.clip(rotated * scale[:, None, :], -fp8_limit, fp8_limit).astype(jnp.bfloat16)
    got_coded, got_expo = from_behind((coded, expo_local), "section", -1)
    values = got_coded.astype(jnp.float32) * jnp.exp2(got_expo.astype(jnp.float32))[:, None, :]
    back = jnp.einsum("ji,bjt->bit", table, values, precision=lax.Precision.HIGHEST).reshape(
        -1, tokens_here
    )
    upstream_grad = (back * signs[:, None]).astype(jnp.bfloat16)
    weight_grad = lax.psum_scatter(
        lax.dot_general(
            inputs_local, grads_before, (((0,), (0,)), ((), ())), preferred_element_type=jnp.float32
        ),
        "dp",
        scatter_dimension=0,
        tiled=True,
    )
    return (upstream_grad[None], weight_grad[None])


def solution(mesh):
    placed = (
        P("section", "dp", None),
        P("section", "dp", "tensor"),
        P("section", "dp", "tensor"),
        P("section", "dp", "tensor"),
        P("section", "tensor", "dp"),
        P("tensor"),
    )
    return jax.shard_map(
        body,
        mesh=mesh,
        in_specs=placed,
        out_specs=(P("section", "tensor", "dp"), P("section", "dp", "tensor")),
        check_vma=False,
    )
```

profile of v0, /device:TPU:20, one launch (start us, length us, event | category | flops | bytes accessed | tf_op | source)
XLA Modules:
  0.0 653.1 jit_solution(16282606772246836653)
XLA Ops:
  7.2 0.0 copy-start
  7.2 0.0 all-gather.3.cloned.1.call-start
  7.2 0.7 all-gather.3.cloned.1.call-update
  7.9 0.0 reduce-scatter.3.cloned.1.call-start
  8.0 118.4 %all-gather.3.cloned.1.call-done = bf16[1,12288,512]{2,1,0:T(8,128)(2,1)} async-done(((bf16[1,3072,512]{2,1,0:T(8,128)(2,1)}), bf16[1,12288,512]{2,1,0:T(8,128)(2,1)}) %all-gather.3.cloned.1.call-update) | async-done | bytes 12582928 | tf_op jit(solution)/shard_map/all_gather | solution.py:37
  126.4 0.0 copy-done
  126.4 16.4 %fusion.2 = f32[12288,512]{1,0:T(8,128)} fusion(bf16[1,12288,512]{2,1,0:T(8,128)(2,1)} %all-gather.3.cloned.1.call-done, bf16[1,512,512]{2,1,0:T(8,128)(2,1)S(1)} %copy-done), kind=kOutput, calls=%fused_computation.2 | convolution fusion | flops 6442450944 | bytes 38273024 | tf_op jit(solution)/shard_map/dot_general | solution.py:36
  142.8 0.0 copy-start.2
  142.8 0.0 reduce-scatter.3.cloned.1.call-update
  142.8 0.0 reduce-scatter.5.cloned.1.call-start
  142.9 1.0 copy-done.2
  143.8 17.2 %fusion = f32[12288,512]{1,0:T(8,128)} fusion(bf16[1,512,12288]{2,1,0:T(8,128)(2,1)} %param.6, bf16[1,512,512]{2,1,0:T(8,128)(2,1)S(1)} %copy-done.2), kind=kOutput, calls=%fused_computation | convolution fusion | flops 6442450944 | bytes 38273024 | tf_op jit(solution)/shard_map/dot_general | solution.py:54
  161.0 0.0 copy-start.4
  161.0 0.0 copy-start.3
  161.0 0.0 reduce-scatter.5.cloned.1.call-update
  161.1 0.6 copy-done.4
  161.7 0.1 copy-done.3
  161.9 199.5 %reduce-scatter.3.cloned.1.call-done = f32[3072,512]{1,0:T(8,128)} async-done(((f32[12288,512]{1,0:T(8,128)}), f32[3072,512]{1,0:T(8,128)}) %reduce-scatter.3.cloned.1.call-update) | async-done | bytes 6291472 | tf_op jit(solution)/shard_map/reduce_scatter | solution.py:42
  361.4 3.3 broadcast_multiply_fusion
  364.7 6.8 %fusion.8 = bf16[24,128,512]{2,1,0:T(8,128)(2,1)S(1)} fusion(f32[24,512]{1,0:T(8,128)S(1)} %multiply_exponential_fusion.1, f32[24,128,512]{2,1,0:T(8,128)S(1)} %bitcast.30, s32[128]{0:T(128)S(1)} %get-tuple-element.2, s32[128]{0:T(128)S(1)} %get-tuple-element.3, s32[128]{0:T(128)S(1)} %get-tuple-element.4, s32[128]{0:T(128)S(1)} %get-tuple-element.5, ...), kind=kOutput, calls=%fused_computation.10 | convolution fusion | flops 2421211136 | bytes 9489920 | tf_op jit(solution)/shard_map/ij,bjt->bit/dot_general | solution.py:44
  371.5 2.5 collective-permute-start
  374.0 5.0 collective-permute-start.1
  379.0 136.9 %collective-permute-done.1 = s32[24,512]{1,0:T(8,128)S(1)} collective-permute-done((s32[24,512]{1,0:T(8,128)S(1)}, s32[24,512]{1,0:T(8,128)S(1)}, u32[]{:S(2)}, u32[]{:S(2)}) %collective-permute-start.1) | collective-permute-done | bytes 49184 | tf_op jit(solution)/shard_map/ppermute | solution.py:15
  515.9 0.0 collective-permute-done
  515.9 0.0 copy-start.1
  515.9 7.5 %fusion.5 = f32[24,512,128]{1,2,0:T(8,128)S(1)} fusion(bf16[24,128,512]{2,1,0:T(8,128)(2,1)S(1)} %collective-permute-done, f32[24,512]{1,0:T(8,128)S(1)} %multiply_exponential_fusion, s32[128]{0:T(128)S(1)} %get-tuple-element.2, s32[128]{0:T(128)S(1)} %get-tuple-element.3, s32[128]{0:T(128)S(1)} %get-tuple-element.4, s32[128]{0:T(128)S(1)} %get-tuple-element.5, ...), kind=kOutput, calls=%fused_computation.6 | convolution fusion | flops 2419638272 | bytes 9489920 | tf_op jit(solution)/shard_map/ji,bjt->bit/dot_general | solution.py:49
  523.5 2.6 fusion.4
  526.0 120.5 %reduce-scatter.5.cloned.1.call-done = f32[3072,512]{1,0:T(8,128)} async-done(((f32[12288,512]{1,0:T(8,128)}), f32[3072,512]{1,0:T(8,128)}) %reduce-scatter.5.cloned.1.call-update) | async-done | bytes 6291472 | tf_op jit(solution)/shard_map/reduce_scatter | solution.py:53
  646.5 0.0 copy-done.1
  (7 shorter events, 0.1 us)
Async XLA Ops:
  7.2 119.2 %copy-start = (bf16[1,512,512]{2,1,0:T(8,128)(2,1)S(1)}, bf16[1,512,512]{2,1,0:T(8,128)(2,1)}, u32[]{:S(2)}) copy-start(bf16[1,512,512]{2,1,0:T(8,128)(2,1)} %param.8) | copy-start | bytes 1572868
  7.2 119.2 %all-gather.3.cloned.1.call-start = ((), (), s32[]{:S(2)}) async-start(), calls=%async_computation.4 | async-start | bytes 15728640 | tf_op jit(solution)/shard_map/all_gather | solution.py:37
  7.9 353.5 %reduce-scatter.3.cloned.1.call-start = ((), (), s32[]{:S(2)}) async-start(), calls=%async_computation.2 | async-start | bytes 31457280 | tf_op jit(solution)/shard_map/reduce_scatter | solution.py:42
  142.8 1.0 copy-start.2
  142.8 503.7 %reduce-scatter.5.cloned.1.call-start = ((), (), s32[]{:S(2)}) async-start(), calls=%async_computation.3 | async-start | bytes 31457280 | tf_op jit(solution)/shard_map/reduce_scatter | solution.py:53
  161.0 0.7 copy-start.4
  161.0 0.8 copy-start.3
  371.5 144.4 %collective-permute-start = (bf16[24,128,512]{2,1,0:T(8,128)(2,1)S(1)}, bf16[24,128,512]{2,1,0:T(8,128)(2,1)S(1)}, u32[]{:S(2)}, u32[]{:S(2)}) collective-permute-start(bf16[24,128,512]{2,1,0:T(8,128)(2,1)S(1)} %fusion.8), channel_id=1, source_target_pairs={{16,0},{32,16},{48,32},{64,48},{80,64},{96,80},{112,96},{17,1},{33... | collective-permute-start | bytes 9437192 | tf_op jit(solution)/shard_map/ppermute | solution.py:15
  374.0 141.9 %collective-permute-start.1 = (s32[24,512]{1,0:T(8,128)S(1)}, s32[24,512]{1,0:T(8,128)S(1)}, u32[]{:S(2)}, u32[]{:S(2)}) collective-permute-start(s32[24,512]{1,0:T(8,128)S(1)} %bitcast.31), channel_id=1, source_target_pairs={{16,0},{32,16},{48,32},{64,48},{80,64},{96,80},{112,96},{17,1},{33... | collective-permute-start | bytes 147464 | tf_op jit(solution)/shard_map/ppermute | solution.py:15
  515.9 130.6 %copy-start.1 = (bf16[1,512,512]{2,1,0:T(8,128)(2,1)S(1)}, bf16[1,512,512]{2,1,0:T(8,128)(2,1)}, u32[]{:S(2)}) copy-start(bf16[1,512,512]{2,1,0:T(8,128)(2,1)} %param.8) | copy-start | bytes 1572868
Sparse Core Ops, SparseCore 0:
  9.7 116.6 all-gather.2
  143.0 218.4 reduce-scatter.2
  364.6 281.8 reduce-scatter.4
where the time goes:
time: 654 us; the launch traced here: 653 us
  waiting for transfers between devices  576 us (88%)
  matrix products  47.9 us (7%)
  between operations  13.8 us (2%)
  starting transfers between devices  7.62 us (1%)
    reduce_scatter x1, waiting for transfers between devices, body(): lax.psum_scatter(partial_grad, 'tensor', scatter_dimension=0, tiled=True)  200 us
    ppermute x2, waiting for transfers between devices, from_behind(): return lax.ppermute(shard, axis, pairs)  137 us
    reduce_scatter x1, waiting for transfers between devices, body(): lax.psum_scatter(lax.dot_general(inputs_local, grads_before, (((0,), (0,)...  121 us
    all_gather x1, waiting for transfers between devices, body(): lax.all_gather(weight_local, 'dp', axis=0, tiled=True)  118 us
    dot_general x1, matrix products, body(): lax.dot_general(inputs_local, grads_before, (((0,), (0,)), ((), ())), pre...  17.2 us
    dot_general x1, matrix products, body(): lax.dot_general(lax.all_gather(weight_local, 'dp', axis=0, tiled=True), g...  16.4 us
  transfers between devices with their start and end apart: 5, of which 4 were waited for; matrix products, arithmetic and copies ran while one was open for 6% of the time, Pallas kernels for 0%

commit v1 on v0

v1 whole, which is shorter than its diff:
```python
import jax
import jax.numpy as jnp
from jax import lax
from jax.experimental import pallas as pl
from jax.experimental.pallas import tpu as pltpu
from jax.sharding import PartitionSpec as P

HB = 128
FP8_LIMIT = 448.0
AXES = ("section", "dp", "tensor")
VMEM = pl.BlockSpec(memory_space=pltpu.VMEM)
SMEM = pl.BlockSpec(memory_space=pltpu.SMEM)


def send(shard, place):
    sections, dps, tensors = (lax.axis_size(axis) for axis in AXES)
    pairs = []
    for s in range(sections):
        for d in range(dps):
            for t in range(tensors):
                to_s, to_d, to_t = place(s, d, t)
                if 0 <= to_s < sections:
                    pairs.append(((s * dps + d) * tensors + t, (to_s * dps + to_d) * tensors + to_t % tensors))
    return lax.ppermute(shard, AXES, pairs)


def other_core(shard):
    return send(shard, lambda s, d, t: (s, d ^ 1, t))


def other_chip(shard):
    return send(shard, lambda s, d, t: (s, d ^ 2, t))


def hadamard_signs(order):
    index = jnp.arange(order, dtype=jnp.int32)
    table = jnp.ones((order, order), jnp.float32)
    for bit_pos in range(order.bit_length() - 1):
        both = (index[:, None] >> bit_pos & 1) * (index[None, :] >> bit_pos & 1)
        table = table * (1.0 - 2.0 * both.astype(jnp.float32))
    return table


def rotate_kernel(base_ref, w0, w1, w2, w3, table_ref, g0, g1, g2, g3, out_ref):
    base = base_ref[0]
    weights, grads = (w0, w1, w2, w3), (g0, g1, g2, g3)
    rows, depth = w0.shape
    norm = HB ** -0.5
    for k, grad in enumerate(grads):
        slot = jnp.bitwise_xor(base, k)

        @pl.loop(0, rows // (2 * HB))
        def _(m):
            at = pl.multiple_of(m * 2 * HB, 2 * HB)
            total = None
            for r, weight in enumerate(weights):
                term = lax.dot_general(
                    weight[pl.ds(at, 2 * HB), :],
                    grad[:, r * depth : (r + 1) * depth],
                    (((1,), (1,)), ((), ())),
                    preferred_element_type=jnp.float32,
                )
                total = term if total is None else total + term
            high = total.astype(jnp.bfloat16)
            low = (total - high.astype(jnp.float32)).astype(jnp.bfloat16)
            for b in range(2):
                both = jnp.concatenate([high[b * HB : (b + 1) * HB], low[b * HB : (b + 1) * HB]], axis=0)
                turned = jnp.dot(table_ref[m * 2 + b], both, preferred_element_type=jnp.float32) * norm
                out_ref[slot, pl.ds(pl.multiple_of(at + b * HB, HB), HB), :] = turned.astype(jnp.bfloat16)


def rotate(base, weights, table, grads):
    rows, depth = weights[0].shape
    tokens = grads[0].shape[0]
    flops = 2 * rows * len(grads) * tokens * depth * len(weights)
    return pl.pallas_call(
        rotate_kernel,
        out_shape=jax.ShapeDtypeStruct((len(grads), rows, tokens), jnp.bfloat16),
        in_specs=[SMEM] + [VMEM] * 9,
        out_specs=VMEM,
        compiler_params=pltpu.CompilerParams(vmem_limit_bytes=40 * 1024 * 1024),
        cost_estimate=pl.CostEstimate(flops=flops, bytes_accessed=16 << 20, transcendentals=0),
        name="rotate",
    )(base, *weights, table, *grads)


def back_kernel(here_ref, p0, p1, p2, p3, limit_ref, table_ref, out_ref):
    here = here_ref[0]
    pieces = (p0, p1, p2, p3)
    blocks = p0.shape[0] // HB
    norm = HB ** -0.5
    for r, piece in enumerate(pieces):
        first = jnp.bitwise_xor(here, r) * blocks

        @pl.loop(0, blocks)
        def _(b):
            limit = limit_ref[first + b]
            values = piece[pl.ds(pl.multiple_of(b * HB, HB), HB), :].astype(jnp.float32)
            values = jnp.clip(values, -limit, limit).astype(jnp.bfloat16)
            turned = jnp.dot(table_ref[first + b], values, preferred_element_type=jnp.float32) * norm
            out_ref[pl.ds(pl.multiple_of((first + b) * HB, HB), HB), :] = turned.astype(jnp.bfloat16)


def back(here, pieces, limit, table):
    rows, tokens = pieces[0].shape
    return pl.pallas_call(
        back_kernel,
        out_shape=jax.ShapeDtypeStruct((len(pieces) * rows, tokens), jnp.bfloat16),
        in_specs=[SMEM] + [VMEM] * 6,
        out_specs=VMEM,
        compiler_params=pltpu.CompilerParams(vmem_limit_bytes=40 * 1024 * 1024),
        cost_estimate=pl.CostEstimate(flops=2 * 4 * rows * tokens * HB, bytes_accessed=7 << 20, transcendentals=0),
        name="rotate_back",
    )(here, *pieces, limit, table)


def body(earlier_inputs, earlier_grads, current_grads, key_value_weight, exponents, sign_bits):
    dp, tensor = lax.axis_index("dp"), lax.axis_index("tensor")
    parts = lax.axis_size("tensor")
    inputs_local, grads_before = earlier_inputs[0], earlier_grads[0]
    rows_here = key_value_weight.shape[1]
    quarter = rows_here // parts

    def scalar(value):
        return jnp.reshape(value, (1,)).astype(jnp.int32)

    grads_far = send(current_grads[0], lambda s, d, t: (s - 1, d ^ 2, t))
    grads_near = other_chip(grads_far)
    pieces_of = []
    for held in (grads_near, grads_far):
        around = [held] + [send(held, lambda s, d, t, r=r: (s, d, t + r)) for r in range(1, parts)]
        pieces_of.append(jnp.concatenate(around, axis=1))
    near, far = pieces_of
    grads = [near, other_core(near), far, other_core(far)]
    weights = []
    for r in range(parts):
        piece = lax.dynamic_slice_in_dim(key_value_weight[0], (tensor + r) % parts * quarter, quarter, 0)
        weights.append(send(piece, lambda s, d, t, r=r: (s - 1, d ^ 2, t + r)))

    plain = hadamard_signs(HB)
    bits = lax.dynamic_slice_in_dim(sign_bits, dp * quarter, quarter, 0)
    bits = send(bits, lambda s, d, t: (s, t ^ 2, d))
    signs_there = (2 * bits - 1).astype(jnp.float32).reshape(-1, 1, HB)
    table = (plain * signs_there).astype(jnp.bfloat16)
    turned = rotate(
        scalar(jnp.bitwise_xor(dp, tensor)), weights, jnp.concatenate([table, table], axis=2), grads
    )
    pieces = [send(turned[r], lambda s, d, t, r=r: (s, t ^ r, d ^ 2)) for r in range(parts)]
    got_expo = send(exponents[0], lambda s, d, t: (s - 1, d, t))
    limit = (FP8_LIMIT * jnp.exp2(got_expo.astype(jnp.float32)))[:, None, :]
    signs_here = (2 * sign_bits - 1).astype(jnp.float32).reshape(-1, HB, 1)
    upstream_grad = back(scalar(dp), pieces, limit, (plain * signs_here).astype(jnp.bfloat16))

    def features(block):
        return lax.dynamic_slice_in_dim(inputs_local, block * rows_here, rows_here, 1)

    def product(mine, got):
        return lax.dot_general(
            mine, grads_before, (((0,), (0,)), ((), ())), preferred_element_type=jnp.float32
        ) + lax.dot_general(got, grads_other, (((0,), (0,)), ((), ())), preferred_element_type=jnp.float32)

    grads_other = other_core(grads_before)
    got_far = other_core(features(jnp.bitwise_xor(dp, 3)))
    got_near = other_core(features(jnp.bitwise_xor(dp, 1)))
    partial = product(features(jnp.bitwise_xor(dp, 2)), got_far).astype(jnp.bfloat16)
    arrived = other_chip(partial).astype(jnp.float32)
    weight_grad = product(features(dp), got_near) + arrived
    return (upstream_grad[None], weight_grad[None])


def solution(mesh):
    placed = (
        P("section", "dp", None),
        P("section", "dp", "tensor"),
        P("section", "dp", "tensor"),
        P("section", "dp", "tensor"),
        P("section", "tensor", "dp"),
        P("tensor"),
    )
    return jax.shard_map(
        body,
        mesh=mesh,
        in_specs=placed,
        out_specs=(P("section", "tensor", "dp"), P("section", "dp", "tensor")),
        check_vma=False,
    )
```

time: 654 us -> 241 us (0.37)
  waiting for transfers between devices: 576 us -> 119 us
  starting transfers between devices: 7.62 us -> 46 us
  matrix products: 47.9 us -> 19.6 us
  Pallas kernels: 0 us -> 22.3 us
  local copies, waits for them, and re-layouts: 1.72 us -> 22 us
  between operations: 13.8 us -> 1.05 us
    reduce_scatter x2 -> x0, waiting for transfers between devices: 320 us -> none  [the longest x1 200 us: body(): lax.psum_scatter(partial_grad, 'tensor', scatter_dimension=0, tiled=True)]
    all_gather x1 -> x0, waiting for transfers between devices: 118 us -> none  [body(): lax.all_gather(weight_local, 'dp', axis=0, tiled=True)]
    ppermute x2 -> x24, starting transfers between devices: 7.5 us -> 46 us  [send(): return lax.ppermute(shard, AXES, pairs)]
    dot_general x4, matrix products: 47.9 us -> 19.6 us  [the longest x2 10.3 us: product(): lax.dot_general(mine, grads_before, (((0,), (0,)), ((), ())), preferred_e...]
    pallas_call x0 -> x2, Pallas kernels: none -> 22.3 us  [the longest x1 16 us: rotate(): pl.pallas_call(rotate_kernel, out_shape=jax.ShapeDtypeStruct((len(grads),...]
    ppermute x2 -> x24, waiting for transfers between devices: 137 us -> 119 us  [send(): return lax.ppermute(shard, AXES, pairs)]
    unnamed x10 -> x32, local copies, waits for them, and re-layouts: 1.72 us -> 9.93 us
    dynamic_slice x0 -> x3, local copies, waits for them, and re-layouts: none -> 7.94 us  [the longest x1 6.07 us: features(): lax.dynamic_slice_in_dim(inputs_local, block * rows_here, rows_here, 1)]
  transfers between devices with their start and end apart: 5 -> 24, of which waited for: 4 -> 13; matrix products, arithmetic and copies ran while one was open for 6% -> 15% of each run, Pallas kernels for 0% -> 9%
where the time goes in v1:
time: 241 us; the launch traced here: 237 us
  waiting for transfers between devices  119 us (49%)
  starting transfers between devices  46 us (19%)
  Pallas kernels  22.3 us (9%)
  local copies, waits for them, and re-layouts  22 us (9%)
  matrix products  19.6 us (8%)
  other arithmetic  7.14 us (3%)
    ppermute x24, waiting for transfers between devices, send(): return lax.ppermute(shard, AXES, pairs)  119 us
    ppermute x24, starting transfers between devices, send(): return lax.ppermute(shard, AXES, pairs)  46 us
    pallas_call x1, Pallas kernels, rotate(): pl.pallas_call(rotate_kernel, out_shape=jax.ShapeDtypeStruct((len(grads),...  16 us
    dot_general x2, matrix products, product(): lax.dot_general(mine, grads_before, (((0,), (0,)), ((), ())), preferred_e...  10.3 us
    unnamed x32, local copies, waits for them, and re-layouts  9.93 us
    dot_general x2, matrix products, product(): lax.dot_general(got, grads_other, (((0,), (0,)), ((), ())), preferred_ele...  9.34 us
    broadcast_in_dim x1, other arithmetic, body(): return (upstream_grad[None], weight_grad[None])  6.38 us
    pallas_call x1, Pallas kernels, back(): pl.pallas_call(back_kernel, out_shape=jax.ShapeDtypeStruct((len(pieces) *...  6.31 us
  transfers between devices with their start and end apart: 24, of which 13 were waited for; matrix products, arithmetic and copies ran while one was open for 15% of the time, Pallas kernels for 9%

profile of v1, /device:TPU:20, one launch (start us, length us, event | category | flops | bytes accessed | tf_op | source)
XLA Modules:
  0.0 236.7 jit_solution(10784057022427459117)
XLA Ops:
  0.7 6.1 %dynamic-slice_bitcast_fusion.1 = (bf16[512,3072]{1,0:T(8,128)(2,1)}, bf16[512,3072]{1,0:T(8,128)(2,1)}) fusion(bf16[1,512,12288]{2,1,0:T(8,128)(2,1)} %param.6, s32[]{:T(128)S(6)} %select_n.56, s32[]{:T(128)S(6)} %select_n.58), kind=kLoop, calls=%fused_computation.8 | loop fusion | bytes 12582920 | tf_op jit(solution)/shard_map/dynamic_slice | solution.py:155
  6.7 2.4 %collective-permute-start.5 = (bf16[512,512]{1,0:T(8,128)(2,1)S(1)}, bf16[512,512]{1,0:T(8,128)(2,1)}, u32[]{:S(2)}, u32[]{:S(2)}) collective-permute-start(bf16[512,512]{1,0:T(8,128)(2,1)S(1)} %bitcast.48), channel_id=1, source_target_pairs={{16,8},{17,9},{18,10},{19,11},{20,12},{21,13},{22,14},{23,15},{24,... | collective-permute-start | bytes 1572872 | tf_op jit(solution)/shard_map/ppermute | solution.py:24
  9.3 14.7 %collective-permute-done.5 = bf16[512,512]{1,0:T(8,128)(2,1)} collective-permute-done((bf16[512,512]{1,0:T(8,128)(2,1)S(1)}, bf16[512,512]{1,0:T(8,128)(2,1)}, u32[]{:S(2)}, u32[]{:S(2)}) %collective-permute-start.5) | collective-permute-done | bytes 524320 | tf_op jit(solution)/shard_map/ppermute | solution.py:24
  24.0 2.4 %collective-permute-start.6 = (bf16[512,512]{1,0:T(8,128)(2,1)}, bf16[512,512]{1,0:T(8,128)(2,1)}, u32[]{:S(2)}, u32[]{:S(2)}) collective-permute-start(bf16[512,512]{1,0:T(8,128)(2,1)} %collective-permute-done.5), channel_id=1, source_target_pairs={{0,8},{1,9},{2,10},{3,11},{4,12},{5,13},{6,14},{7,15},{8,0},{9,1},... | collective-permute-start | bytes 1572872 | tf_op jit(solution)/shard_map/ppermute | solution.py:24
  26.4 6.4 %fusion = f32[3072,512]{1,0:T(8,128)} fusion(bf16[1,512,12288]{2,1,0:T(8,128)(2,1)} %param.6, s32[]{:T(128)S(6)} %select_n.57, bf16[1,512,512]{2,1,0:T(8,128)(2,1)S(1)} %copy-done.4), kind=kOutput, calls=%fused_computation.2 | convolution fusion | flops 1610612736 | bytes 9961476 | tf_op jit(solution)/shard_map/dot_general | solution.py:158
  32.8 1.9 collective-permute-start.11
  34.7 3.6 %collective-permute-start.12 = (bf16[512,512]{1,0:T(8,128)(2,1)}, bf16[512,512]{1,0:T(8,128)(2,1)}, u32[]{:S(2)}, u32[]{:S(2)}) collective-permute-start(bf16[512,512]{1,0:T(8,128)(2,1)} %collective-permute-done.5), channel_id=1, source_target_pairs={{0,2},{1,3},{2,0},{3,1},{4,6},{5,7},{6,4},{7,5},{8,10},{9,11},{10,... | collective-permute-start | bytes 1572872 | tf_op jit(solution)/shard_map/ppermute | solution.py:24
  38.3 1.8 dynamic-slice_bitcast_fusion.2
  40.1 1.0 collective-permute-start.13
  41.1 1.0 collective-permute-start.7
  42.2 1.9 constant_dynamic-update-slice_fusion.7
  44.2 7.3 %collective-permute-done.11 = bf16[512,512]{1,0:T(8,128)(2,1)S(1)} collective-permute-done((bf16[512,512]{1,0:T(8,128)(2,1)}, bf16[512,512]{1,0:T(8,128)(2,1)S(1)}, u32[]{:S(2)}, u32[]{:S(2)}) %collective-permute-start.11) | collective-permute-done | bytes 524320 | tf_op jit(solution)/shard_map/ppermute | solution.py:24
  51.5 0.8 copy-done.9
  52.3 2.0 collective-permute-start
  54.4 8.4 %collective-permute-done.12 = bf16[512,512]{1,0:T(8,128)(2,1)} collective-permute-done((bf16[512,512]{1,0:T(8,128)(2,1)}, bf16[512,512]{1,0:T(8,128)(2,1)}, u32[]{:S(2)}, u32[]{:S(2)}) %collective-permute-start.12) | collective-permute-done | bytes 524320 | tf_op jit(solution)/shard_map/ppermute | solution.py:24
  62.7 3.2 %collective-permute-start.8 = (bf16[512,512]{1,0:T(8,128)(2,1)}, bf16[512,512]{1,0:T(8,128)(2,1)S(1)}, u32[]{:S(2)}, u32[]{:S(2)}) collective-permute-start(bf16[512,512]{1,0:T(8,128)(2,1)} %collective-permute-done.6), channel_id=1, source_target_pairs={{0,2},{1,3},{2,0},{3,1},{4,6},{5,7},{6,4},{7,5},{8,10},{9,11},{10,... | collective-permute-start | bytes 1572872 | tf_op jit(solution)/shard_map/ppermute | solution.py:24
  66.0 1.1 constant_dynamic-update-slice_fusion.3
  67.3 2.0 constant_dynamic-update-slice_fusion.6
  69.4 2.1 collective-permute-done.7
  71.5 1.9 constant_dynamic-update-slice_fusion.5
  73.4 1.9 constant_dynamic-update-slice_fusion.4.g2
  75.4 1.1 constant_dynamic-update-slice_fusion.2
  76.5 7.1 %collective-permute-done.8 = bf16[512,512]{1,0:T(8,128)(2,1)S(1)} collective-permute-done((bf16[512,512]{1,0:T(8,128)(2,1)}, bf16[512,512]{1,0:T(8,128)(2,1)S(1)}, u32[]{:S(2)}, u32[]{:S(2)}) %collective-permute-start.8) | collective-permute-done | bytes 524320 | tf_op jit(solution)/shard_map/ppermute | solution.py:24
  83.9 6.7 %collective-permute-done.4 = s32[768]{0:T(1024)S(1)} collective-permute-done((s32[768]{0:T(1024)S(1)}, s32[768]{0:T(1024)S(1)}, u32[]{:S(2)}, u32[]{:S(2)}) %collective-permute-start.4) | collective-permute-done | bytes 3104 | tf_op jit(solution)/shard_map/ppermute | solution.py:24
  90.6 1.9 collective-permute-start.1
  92.7 0.6 collective-permute-start.14
  93.4 4.2 %collective-permute-start.2 = (bf16[768,512]{1,0:T(8,128)(2,1)}, bf16[768,512]{1,0:T(8,128)(2,1)}, u32[]{:S(2)}, u32[]{:S(2)}) collective-permute-start(bf16[768,512]{1,0:T(8,128)(2,1)} %get-tuple-element.11), channel_id=1, source_target_pairs={{16,10},{17,11},{18,8},{19,9},{20,14},{21,15},{22,12},{23,13},{24,... | collective-permute-start | bytes 2359304 | tf_op jit(solution)/shard_map/ppermute | solution.py:24
  97.6 5.6 %add_convert_fusion = bf16[3072,512]{1,0:T(8,128)(2,1)} fusion(f32[3072,512]{1,0:T(8,128)S(1)} %copy-done.2, bf16[512,3072]{1,0:T(8,128)(2,1)} %collective-permute-done.22, bf16[512,512]{1,0:T(8,128)(2,1)S(1)} %collective-permute-done.21), kind=kOutput, calls=%fused_computation.1 | convolution fusion | flops 1613758464 | bytes 13107200 | tf_op jit(solution)/shard_map/dot_general | solution.py:160
  103.3 13.4 %collective-permute-done.1.w1 = bf16[768,512]{1,0:T(8,128)(2,1)S(1)} collective-permute-done((bf16[768,512]{1,0:T(8,128)(2,1)S(1)}, bf16[768,512]{1,0:T(8,128)(2,1)S(1)}, u32[]{:S(2)}, u32[]{:S(2)}) %collective-permute-start.1) | collective-permute-done | bytes 786464 | tf_op jit(solution)/shard_map/ppermute | solution.py:24
  116.7 0.9 copy-done
  117.6 1.0 collective-permute-start.23
  118.8 3.8 %fusion.2 = f32[3072,512]{1,0:T(8,128)S(1)} fusion(bf16[1,512,12288]{2,1,0:T(8,128)(2,1)} %param.6, s32[]{:T(128)S(6)} %select_n.55, bf16[1,512,512]{2,1,0:T(8,128)(2,1)S(1)} %copy-done.4), kind=kOutput, calls=%fused_computation.4 | convolution fusion | flops 1610612736 | bytes 9961476 | tf_op jit(solution)/shard_map/dot_general | solution.py:158
  122.7 7.9 %collective-permute-done.2.w2 = bf16[768,512]{1,0:T(8,128)(2,1)} collective-permute-done((bf16[768,512]{1,0:T(8,128)(2,1)}, bf16[768,512]{1,0:T(8,128)(2,1)}, u32[]{:S(2)}, u32[]{:S(2)}) %collective-permute-start.2) | collective-permute-done | bytes 786464 | tf_op jit(solution)/shard_map/ppermute | solution.py:24
  130.5 4.1 %collective-permute-start.3 = (bf16[768,512]{1,0:T(8,128)(2,1)S(1)}, bf16[768,512]{1,0:T(8,128)(2,1)S(1)}, u32[]{:S(2)}, u32[]{:S(2)}) collective-permute-start(bf16[768,512]{1,0:T(8,128)(2,1)S(1)} %copy-done.7), channel_id=1, source_target_pairs={{16,11},{17,8},{18,9},{19,10},{20,15},{21,12},{22,13},{23,14},{24,... | collective-permute-start | bytes 2359304 | tf_op jit(solution)/shard_map/ppermute | solution.py:24
  134.7 17.3 %collective-permute-done.3.w3 = bf16[768,512]{1,0:T(8,128)(2,1)S(1)} collective-permute-done((bf16[768,512]{1,0:T(8,128)(2,1)S(1)}, bf16[768,512]{1,0:T(8,128)(2,1)S(1)}, u32[]{:S(2)}, u32[]{:S(2)}) %collective-permute-start.3) | collective-permute-done | bytes 786464 | tf_op jit(solution)/shard_map/ppermute | solution.py:24
  152.1 2.5 %collective-permute-start.19 = (s32[24,512]{1,0:T(8,128)S(1)}, s32[24,512]{1,0:T(8,128)S(1)}, u32[]{:S(2)}, u32[]{:S(2)}) collective-permute-start(s32[24,512]{1,0:T(8,128)S(1)} %bitcast.49), channel_id=1, source_target_pairs={{16,0},{17,1},{18,2},{19,3},{20,4},{21,5},{22,6},{23,7},{24,8},{25... | collective-permute-start | bytes 147464 | tf_op jit(solution)/shard_map/ppermute | solution.py:24
  154.6 16.0 %rotate.1 = bf16[4,768,512]{2,1,0:T(8,128)(2,1)} custom-call(s32[1]{0:T(128)} %bitcast.1.base_ref, bf16[768,512]{1,0:T(8,128)(2,1)S(1)} %collective-permute-done.w0, bf16[768,512]{1,0:T(8,128)(2,1)S(1)} %copy-done.1, bf16[768,512]{1,0:T(8,128)(2,1)} %collective-permute-done.2.w2, bf16[768,512]{1,0:T(8,128)(2,1)S(1)} %collective-permute-done.3.w3, ...), custom_call_target="tpu_custom_call" | custom-call | flops 6442450944 | bytes 16777216 | tf_op jit(solution)/shard_map/rotate/pallas_call | solution.py:76
  170.6 2.1 slice_bitcast_fusion
  172.7 4.0 %collective-permute-start.15 = (bf16[768,512]{1,0:T(8,128)(2,1)S(1)}, bf16[768,512]{1,0:T(8,128)(2,1)S(1)}, u32[]{:S(2)}, u32[]{:S(2)}) collective-permute-start(bf16[768,512]{1,0:T(8,128)(2,1)S(1)} %get-tuple-element.7), channel_id=1, source_target_pairs={{0,2},{1,6},{2,10},{3,14},{4,3},{5,7},{6,11},{7,15},{8,0},{9,4},{1... | collective-permute-start | bytes 2359304 | tf_op jit(solution)/shard_map/ppermute | solution.py:24
  176.6 2.1 collective-permute-start.16
  178.7 4.9 %collective-permute-done.19 = s32[24,512]{1,0:T(8,128)S(1)} collective-permute-done((s32[24,512]{1,0:T(8,128)S(1)}, s32[24,512]{1,0:T(8,128)S(1)}, u32[]{:S(2)}, u32[]{:S(2)}) %collective-permute-start.19) | collective-permute-done | bytes 49184 | tf_op jit(solution)/shard_map/ppermute | solution.py:24
  183.6 7.2 %collective-permute-start.17 = (bf16[768,512]{1,0:T(8,128)(2,1)S(1)}, bf16[768,512]{1,0:T(8,128)(2,1)S(1)}, u32[]{:S(2)}, u32[]{:S(2)}) collective-permute-start(bf16[768,512]{1,0:T(8,128)(2,1)S(1)} %get-tuple-element.5), channel_id=1, source_target_pairs={{0,10},{1,14},{2,2},{3,6},{4,11},{5,15},{6,3},{7,7},{8,8},{9,12},{... | collective-permute-start | bytes 2359304 | tf_op jit(solution)/shard_map/ppermute | solution.py:24
  191.5 3.7 %fusion.10 = f32[3072,512]{1,0:T(8,128)S(1)} fusion(bf16[512,3072]{1,0:T(8,128)(2,1)} %collective-permute-done.20, bf16[512,512]{1,0:T(8,128)(2,1)S(1)} %copy-done.6), kind=kOutput, calls=%fused_computation.44 | convolution fusion | flops 1610612736 | bytes 9961472 | tf_op jit(solution)/shard_map/dot_general | solution.py:160
  195.3 11.4 %collective-permute-done.15.p0 = bf16[768,512]{1,0:T(8,128)(2,1)S(1)} collective-permute-done((bf16[768,512]{1,0:T(8,128)(2,1)S(1)}, bf16[768,512]{1,0:T(8,128)(2,1)S(1)}, u32[]{:S(2)}, u32[]{:S(2)}) %collective-permute-start.15) | collective-permute-done | bytes 786464 | tf_op jit(solution)/shard_map/ppermute | solution.py:24
  206.7 12.5 %collective-permute-done.16.p1 = bf16[768,512]{1,0:T(8,128)(2,1)S(1)} collective-permute-done((bf16[768,512]{1,0:T(8,128)(2,1)S(1)}, bf16[768,512]{1,0:T(8,128)(2,1)S(1)}, u32[]{:S(2)}, u32[]{:S(2)}) %collective-permute-start.16) | collective-permute-done | bytes 786464 | tf_op jit(solution)/shard_map/ppermute | solution.py:24
  219.3 4.8 %collective-permute-done.18.p3 = bf16[768,512]{1,0:T(8,128)(2,1)S(1)} collective-permute-done((bf16[768,512]{1,0:T(8,128)(2,1)S(1)}, bf16[768,512]{1,0:T(8,128)(2,1)S(1)}, u32[]{:S(2)}, u32[]{:S(2)}) %collective-permute-start.18) | collective-permute-done | bytes 786464 | tf_op jit(solution)/shard_map/ppermute | solution.py:24
  224.1 6.3 %rotate_back.1 = bf16[3072,512]{1,0:T(8,128)(2,1)} custom-call(s32[1]{0:T(128)} %bitcast.here_ref, bf16[768,512]{1,0:T(8,128)(2,1)S(1)} %collective-permute-done.15.p0, bf16[768,512]{1,0:T(8,128)(2,1)S(1)} %collective-permute-done.16.p1, bf16[768,512]{1,0:T(8,128)(2,1)S(1)} %collective-permute-done.17.p2, bf16[768,512]{1,0:T(8,128)(2,1)S(1)} %collective-permute-done.18.p3, ...), custom_call_target="tpu_custom_call" | custom-call | flops 402653184 | bytes 7340032 | tf_op jit(solution)/shard_map/rotate_back/pallas_call | solution.py:106
  230.4 6.4 %add_bitcast_fusion = f32[1,3072,512]{2,1,0:T(8,128)} fusion(bf16[3072,512]{1,0:T(8,128)(2,1)} %collective-permute-done.23, f32[3072,512]{1,0:T(8,128)S(1)} %fusion.2, f32[3072,512]{1,0:T(8,128)S(1)} %fusion.10), kind=kLoop, calls=%fused_computation | loop fusion | flops 4718592 | bytes 22020096 | tf_op jit(solution)/shard_map/broadcast_in_dim | solution.py:168
  (57 shorter events, 1.8 us)
Async XLA Ops:
  0.6 6.1 %copy-start.11 = (bf16[1,512,512]{2,1,0:T(8,128)(2,1)S(1)}, bf16[1,512,512]{2,1,0:T(8,128)(2,1)}, u32[]{:S(2)}) copy-start(bf16[1,512,512]{2,1,0:T(8,128)(2,1)} %param.8) | copy-start | bytes 1572868
  0.7 25.7 %copy-start.4 = (bf16[1,512,512]{2,1,0:T(8,128)(2,1)S(1)}, bf16[1,512,512]{2,1,0:T(8,128)(2,1)}, u32[]{:S(2)}) copy-start(bf16[1,512,512]{2,1,0:T(8,128)(2,1)} %param.7) | copy-start | bytes 1572868
  6.7 86.6 %collective-permute-start.22 = (bf16[512,3072]{1,0:T(8,128)(2,1)}, bf16[512,3072]{1,0:T(8,128)(2,1)}, u32[]{:S(2)}, u32[]{:S(2)}) collective-permute-start(bf16[512,3072]{1,0:T(8,128)(2,1)} %get-tuple-element.3), channel_id=1, source_target_pairs={{0,4},{1,5},{2,6},{3,7},{4,0},{5,1},{6,2},{7,3},{8,12},{9,13},{10,... | collective-permute-start | bytes 9437192 | tf_op jit(solution)/shard_map/ppermute | solution.py:24
  6.7 17.2 %collective-permute-start.5 = (bf16[512,512]{1,0:T(8,128)(2,1)S(1)}, bf16[512,512]{1,0:T(8,128)(2,1)}, u32[]{:S(2)}, u32[]{:S(2)}) collective-permute-start(bf16[512,512]{1,0:T(8,128)(2,1)S(1)} %bitcast.48), channel_id=1, source_target_pairs={{16,8},{17,9},{18,10},{19,11},{20,12},{21,13},{22,14},{23,15},{24,... | collective-permute-start | bytes 1572872 | tf_op jit(solution)/shard_map/ppermute | solution.py:24
  9.3 29.1 %copy-start.3 = (bf16[1,3072,512]{2,1,0:T(8,128)(2,1)S(1)}, bf16[1,3072,512]{2,1,0:T(8,128)(2,1)}, u32[]{:S(2)}) copy-start(bf16[1,3072,512]{2,1,0:T(8,128)(2,1)} %param.9) | copy-start | bytes 9437188
  24.0 17.2 %collective-permute-start.6 = (bf16[512,512]{1,0:T(8,128)(2,1)}, bf16[512,512]{1,0:T(8,128)(2,1)}, u32[]{:S(2)}, u32[]{:S(2)}) collective-permute-start(bf16[512,512]{1,0:T(8,128)(2,1)} %collective-permute-done.5), channel_id=1, source_target_pairs={{0,8},{1,9},{2,10},{3,11},{4,12},{5,13},{6,14},{7,15},{8,0},{9,1},... | collective-permute-start | bytes 1572872 | tf_op jit(solution)/shard_map/ppermute | solution.py:24
  32.8 9.3 %copy-start.10 = (s32[3072]{0:T(1024)S(1)}, s32[3072]{0:T(1024)}, u32[]{:S(2)}) copy-start(s32[3072]{0:T(1024)} %param.11) | copy-start | bytes 36868
  32.8 18.6 %collective-permute-start.11 = (bf16[512,512]{1,0:T(8,128)(2,1)}, bf16[512,512]{1,0:T(8,128)(2,1)S(1)}, u32[]{:S(2)}, u32[]{:S(2)}) collective-permute-start(bf16[512,512]{1,0:T(8,128)(2,1)} %collective-permute-done.5), channel_id=1, source_target_pairs={{0,1},{1,2},{2,3},{3,0},{4,5},{5,6},{6,7},{7,4},{8,9},{9,10},{10,1... | collective-permute-start | bytes 1572872 | tf_op jit(solution)/shard_map/ppermute | solution.py:24
  34.7 28.0 %collective-permute-start.12 = (bf16[512,512]{1,0:T(8,128)(2,1)}, bf16[512,512]{1,0:T(8,128)(2,1)}, u32[]{:S(2)}, u32[]{:S(2)}) collective-permute-start(bf16[512,512]{1,0:T(8,128)(2,1)} %collective-permute-done.5), channel_id=1, source_target_pairs={{0,2},{1,3},{2,0},{3,1},{4,6},{5,7},{6,4},{7,5},{8,10},{9,11},{10,... | collective-permute-start | bytes 1572872 | tf_op jit(solution)/shard_map/ppermute | solution.py:24
  40.1 27.0 %collective-permute-start.13 = (bf16[512,512]{1,0:T(8,128)(2,1)}, bf16[512,512]{1,0:T(8,128)(2,1)}, u32[]{:S(2)}, u32[]{:S(2)}) collective-permute-start(bf16[512,512]{1,0:T(8,128)(2,1)} %collective-permute-done.5), channel_id=1, source_target_pairs={{0,3},{1,0},{2,1},{3,2},{4,7},{5,4},{6,5},{7,6},{8,11},{9,8},{10,9... | collective-permute-start | bytes 1572872 | tf_op jit(solution)/shard_map/ppermute | solution.py:24
  41.1 30.4 %collective-permute-start.7 = (bf16[512,512]{1,0:T(8,128)(2,1)}, bf16[512,512]{1,0:T(8,128)(2,1)}, u32[]{:S(2)}, u32[]{:S(2)}) collective-permute-start(bf16[512,512]{1,0:T(8,128)(2,1)} %collective-permute-done.6), channel_id=1, source_target_pairs={{0,1},{1,2},{2,3},{3,0},{4,5},{5,6},{6,7},{7,4},{8,9},{9,10},{10,1... | collective-permute-start | bytes 1572872 | tf_op jit(solution)/shard_map/ppermute | solution.py:24
  51.5 0.8 copy-start.9
  52.3 38.3 %copy-start.8 = (bf16[768,512]{1,0:T(8,128)(2,1)S(1)}, bf16[768,512]{1,0:T(8,128)(2,1)}, u32[]{:S(2)}) copy-start(bf16[768,512]{1,0:T(8,128)(2,1)} %get-tuple-element.9) | copy-start | bytes 2359300
  52.3 41.0 %collective-permute-start = (bf16[768,512]{1,0:T(8,128)(2,1)}, bf16[768,512]{1,0:T(8,128)(2,1)S(1)}, u32[]{:S(2)}, u32[]{:S(2)}) collective-permute-start(bf16[768,512]{1,0:T(8,128)(2,1)} %get-tuple-element.10), channel_id=1, source_target_pairs={{16,8},{17,9},{18,10},{19,11},{20,12},{21,13},{22,14},{23,15},{24,... | collective-permute-start | bytes 2359304 | tf_op jit(solution)/shard_map/ppermute | solution.py:24
  62.7 20.8 %collective-permute-start.8 = (bf16[512,512]{1,0:T(8,128)(2,1)}, bf16[512,512]{1,0:T(8,128)(2,1)S(1)}, u32[]{:S(2)}, u32[]{:S(2)}) collective-permute-start(bf16[512,512]{1,0:T(8,128)(2,1)} %collective-permute-done.6), channel_id=1, source_target_pairs={{0,2},{1,3},{2,0},{3,1},{4,6},{5,7},{6,4},{7,5},{8,10},{9,11},{10,... | collective-permute-start | bytes 1572872 | tf_op jit(solution)/shard_map/ppermute | solution.py:24
  67.1 30.5 %copy-start.2 = (f32[3072,512]{1,0:T(8,128)S(1)}, f32[3072,512]{1,0:T(8,128)}, u32[]{:S(2)}) copy-start(f32[3072,512]{1,0:T(8,128)} %fusion) | copy-start | bytes 18874372
  67.2 25.4 %collective-permute-start.9 = (bf16[512,512]{1,0:T(8,128)(2,1)}, bf16[512,512]{1,0:T(8,128)(2,1)S(1)}, u32[]{:S(2)}, u32[]{:S(2)}) collective-permute-start(bf16[512,512]{1,0:T(8,128)(2,1)} %collective-permute-done.6), channel_id=1, source_target_pairs={{0,3},{1,0},{2,1},{3,2},{4,7},{5,4},{6,5},{7,6},{8,11},{9,8},{10,9... | collective-permute-start | bytes 1572872 | tf_op jit(solution)/shard_map/ppermute | solution.py:24
  71.5 21.2 %collective-permute-start.21 = (bf16[512,512]{1,0:T(8,128)(2,1)S(1)}, bf16[512,512]{1,0:T(8,128)(2,1)S(1)}, u32[]{:S(2)}, u32[]{:S(2)}) collective-permute-start(bf16[512,512]{1,0:T(8,128)(2,1)S(1)} %bitcast.47), channel_id=1, source_target_pairs={{0,4},{1,5},{2,6},{3,7},{4,0},{5,1},{6,2},{7,3},{8,12},{9,13},{10,... | collective-permute-start | bytes 1572872 | tf_op jit(solution)/shard_map/ppermute | solution.py:24
  83.5 7.1 %collective-permute-start.4 = (s32[768]{0:T(1024)S(1)}, s32[768]{0:T(1024)S(1)}, u32[]{:S(2)}, u32[]{:S(2)}) collective-permute-start(s32[768]{0:T(1024)S(1)} %dynamic_slice.51), channel_id=1, source_target_pairs={{0,8},{1,12},{2,0},{3,4},{4,9},{5,13},{6,1},{7,5},{8,10},{9,14},{1... | collective-permute-start | bytes 9224 | tf_op jit(solution)/shard_map/ppermute | solution.py:24
  90.6 26.1 %collective-permute-start.1 = (bf16[768,512]{1,0:T(8,128)(2,1)S(1)}, bf16[768,512]{1,0:T(8,128)(2,1)S(1)}, u32[]{:S(2)}, u32[]{:S(2)}) collective-permute-start(bf16[768,512]{1,0:T(8,128)(2,1)S(1)} %copy-done.8), channel_id=1, source_target_pairs={{16,9},{17,10},{18,11},{19,8},{20,13},{21,14},{22,15},{23,12},{24,... | collective-permute-start | bytes 2359304 | tf_op jit(solution)/shard_map/ppermute | solution.py:24
  92.5 98.4 %collective-permute-start.20 = (bf16[512,3072]{1,0:T(8,128)(2,1)}, bf16[512,3072]{1,0:T(8,128)(2,1)}, u32[]{:S(2)}, u32[]{:S(2)}) collective-permute-start(bf16[512,3072]{1,0:T(8,128)(2,1)} %get-tuple-element.2), channel_id=1, source_target_pairs={{0,4},{1,5},{2,6},{3,7},{4,0},{5,1},{6,2},{7,3},{8,12},{9,13},{10,... | collective-permute-start | bytes 9437192 | tf_op jit(solution)/shard_map/ppermute | solution.py:24
  92.7 10.6 %copy-start.5 = (bf16[512,512]{1,0:T(8,128)(2,1)}, bf16[512,512]{1,0:T(8,128)(2,1)S(1)}, u32[]{:S(2)}) copy-start(bf16[512,512]{1,0:T(8,128)(2,1)S(1)} %collective-permute-done.21) | copy-start | bytes 1572868
  92.7 61.9 %collective-permute-start.14 = (bf16[512,2048]{1,0:T(8,128)(2,1)}, bf16[512,2048]{1,0:T(8,128)(2,1)}, u32[]{:S(2)}, u32[]{:S(2)}) collective-permute-start(bf16[512,2048]{1,0:T(8,128)(2,1)} %constant_dynamic-update-slice_fusion.4.g2), channel_id=1, source_target_pairs={{0,4},{1,5},{2,6},{3,7},{4,0},{5,1},{6,2},{7,3},{8,12},{9,13},{10,... | collective-permute-start | bytes 6291464 | tf_op jit(solution)/shard_map/ppermute | solution.py:24
  93.3 61.3 %collective-permute-start.10 = (bf16[512,2048]{1,0:T(8,128)(2,1)S(1)}, bf16[512,2048]{1,0:T(8,128)(2,1)}, u32[]{:S(2)}, u32[]{:S(2)}) collective-permute-start(bf16[512,2048]{1,0:T(8,128)(2,1)S(1)} %constant_dynamic-update-slice_fusion.g0), channel_id=1, source_target_pairs={{0,4},{1,5},{2,6},{3,7},{4,0},{5,1},{6,2},{7,3},{8,12},{9,13},{10,... | collective-permute-start | bytes 6291464 | tf_op jit(solution)/shard_map/ppermute | solution.py:24
  93.4 37.1 %collective-permute-start.2 = (bf16[768,512]{1,0:T(8,128)(2,1)}, bf16[768,512]{1,0:T(8,128)(2,1)}, u32[]{:S(2)}, u32[]{:S(2)}) collective-permute-start(bf16[768,512]{1,0:T(8,128)(2,1)} %get-tuple-element.11), channel_id=1, source_target_pairs={{16,10},{17,11},{18,8},{19,9},{20,14},{21,15},{22,12},{23,13},{24,... | collective-permute-start | bytes 2359304 | tf_op jit(solution)/shard_map/ppermute | solution.py:24
  116.7 0.9 copy-start
  117.6 112.8 %collective-permute-start.23 = (bf16[3072,512]{1,0:T(8,128)(2,1)}, bf16[3072,512]{1,0:T(8,128)(2,1)}, u32[]{:S(2)}, u32[]{:S(2)}) collective-permute-start(bf16[3072,512]{1,0:T(8,128)(2,1)} %add_convert_fusion), channel_id=1, source_target_pairs={{0,8},{1,9},{2,10},{3,11},{4,12},{5,13},{6,14},{7,15},{8,0},{9,1},... | collective-permute-start | bytes 9437192 | tf_op jit(solution)/shard_map/ppermute | solution.py:24
  118.8 11.8 %copy-start.7 = (bf16[768,512]{1,0:T(8,128)(2,1)S(1)}, bf16[768,512]{1,0:T(8,128)(2,1)}, u32[]{:S(2)}) copy-start(bf16[768,512]{1,0:T(8,128)(2,1)} %get-tuple-element.8) | copy-start | bytes 2359300
  118.8 33.3 %copy-start.12 = (s32[1,24,512]{2,1,0:T(8,128)S(1)}, s32[1,24,512]{2,1,0:T(8,128)}, u32[]{:S(2)}) copy-start(s32[1,24,512]{2,1,0:T(8,128)} %param.10) | copy-start | bytes 147460
  118.8 35.8 %copy-start.1 = (bf16[768,512]{1,0:T(8,128)(2,1)S(1)}, bf16[768,512]{1,0:T(8,128)(2,1)}, u32[]{:S(2)}) copy-start(bf16[768,512]{1,0:T(8,128)(2,1)} %copy-done) | copy-start | bytes 2359300
  130.5 21.5 %collective-permute-start.3 = (bf16[768,512]{1,0:T(8,128)(2,1)S(1)}, bf16[768,512]{1,0:T(8,128)(2,1)S(1)}, u32[]{:S(2)}, u32[]{:S(2)}) collective-permute-start(bf16[768,512]{1,0:T(8,128)(2,1)S(1)} %copy-done.7), channel_id=1, source_target_pairs={{16,11},{17,8},{18,9},{19,10},{20,15},{21,12},{22,13},{23,14},{24,... | collective-permute-start | bytes 2359304 | tf_op jit(solution)/shard_map/ppermute | solution.py:24
  152.1 31.6 %collective-permute-start.19 = (s32[24,512]{1,0:T(8,128)S(1)}, s32[24,512]{1,0:T(8,128)S(1)}, u32[]{:S(2)}, u32[]{:S(2)}) collective-permute-start(s32[24,512]{1,0:T(8,128)S(1)} %bitcast.49), channel_id=1, source_target_pairs={{16,0},{17,1},{18,2},{19,3},{20,4},{21,5},{22,6},{23,7},{24,8},{25... | collective-permute-start | bytes 147464 | tf_op jit(solution)/shard_map/ppermute | solution.py:24
  170.6 21.0 %copy-start.6 = (bf16[512,512]{1,0:T(8,128)(2,1)S(1)}, bf16[512,512]{1,0:T(8,128)(2,1)}, u32[]{:S(2)}) copy-start(bf16[512,512]{1,0:T(8,128)(2,1)} %copy-done.5) | copy-start | bytes 1572868
  172.7 34.1 %collective-permute-start.15 = (bf16[768,512]{1,0:T(8,128)(2,1)S(1)}, bf16[768,512]{1,0:T(8,128)(2,1)S(1)}, u32[]{:S(2)}, u32[]{:S(2)}) collective-permute-start(bf16[768,512]{1,0:T(8,128)(2,1)S(1)} %get-tuple-element.7), channel_id=1, source_target_pairs={{0,2},{1,6},{2,10},{3,14},{4,3},{5,7},{6,11},{7,15},{8,0},{9,4},{1... | collective-permute-start | bytes 2359304 | tf_op jit(solution)/shard_map/ppermute | solution.py:24
  176.6 42.6 %collective-permute-start.16 = (bf16[768,512]{1,0:T(8,128)(2,1)S(1)}, bf16[768,512]{1,0:T(8,128)(2,1)S(1)}, u32[]{:S(2)}, u32[]{:S(2)}) collective-permute-start(bf16[768,512]{1,0:T(8,128)(2,1)S(1)} %get-tuple-element.6), channel_id=1, source_target_pairs={{0,6},{1,2},{2,14},{3,10},{4,7},{5,3},{6,15},{7,11},{8,4},{9,0},{1... | collective-permute-start | bytes 2359304 | tf_op jit(solution)/shard_map/ppermute | solution.py:24
  183.6 35.6 %collective-permute-start.17 = (bf16[768,512]{1,0:T(8,128)(2,1)S(1)}, bf16[768,512]{1,0:T(8,128)(2,1)S(1)}, u32[]{:S(2)}, u32[]{:S(2)}) collective-permute-start(bf16[768,512]{1,0:T(8,128)(2,1)S(1)} %get-tuple-element.5), channel_id=1, source_target_pairs={{0,10},{1,14},{2,2},{3,6},{4,11},{5,15},{6,3},{7,7},{8,8},{9,12},{... | collective-permute-start | bytes 2359304 | tf_op jit(solution)/shard_map/ppermute | solution.py:24
  190.9 33.2 %collective-permute-start.18 = (bf16[768,512]{1,0:T(8,128)(2,1)S(1)}, bf16[768,512]{1,0:T(8,128)(2,1)S(1)}, u32[]{:S(2)}, u32[]{:S(2)}) collective-permute-start(bf16[768,512]{1,0:T(8,128)(2,1)S(1)} %get-tuple-element.4), channel_id=1, source_target_pairs={{0,14},{1,10},{2,6},{3,2},{4,15},{5,11},{6,7},{7,3},{8,12},{9,8},{... | collective-permute-start | bytes 2359304 | tf_op jit(solution)/shard_map/ppermute | solution.py:24

commit v2 on v1

v2 whole, which is shorter than its diff:
```python
import functools

import jax
import jax.numpy as jnp
from jax import lax
from jax.experimental import pallas as pl
from jax.experimental.pallas import tpu as pltpu
from jax.sharding import Mesh
from jax.sharding import PartitionSpec as P

HB = 128
FP8_LIMIT = 448.0
LONG = 100_000_000_000
AXES = ("section", "chip", "core", "tensor")
VMEM = pl.BlockSpec(memory_space=pltpu.VMEM)
SMEM = pl.BlockSpec(memory_space=pltpu.SMEM)


def send(shard, place):
    sections, chips, cores, tensors = (lax.axis_size(axis) for axis in AXES)
    dps = chips * cores
    pairs = []
    for s in range(sections):
        for d in range(dps):
            for t in range(tensors):
                to_s, to_d, to_t = place(s, d, t)
                if 0 <= to_s < sections:
                    pairs.append(((s * dps + d) * tensors + t, (to_s * dps + to_d) * tensors + to_t % tensors))
    return lax.ppermute(shard, AXES, pairs)


def other_core(shard):
    return send(shard, lambda s, d, t: (s, d ^ 1, t))


def other_chip(shard):
    return send(shard, lambda s, d, t: (s, d ^ 2, t))


def signs_kernel(table_ref):
    order = table_ref.shape[0]
    both = lax.broadcasted_iota(jnp.int32, (order, order), 0) & lax.broadcasted_iota(jnp.int32, (order, order), 1)
    odd = jnp.zeros_like(both)
    for bit in range(order.bit_length() - 1):
        odd = odd ^ (both >> bit & 1)
    table_ref[...] = (1 - 2 * odd).astype(jnp.float32)


def hadamard_signs(order):
    return pl.pallas_call(
        signs_kernel,
        out_shape=jax.ShapeDtypeStruct((order, order), jnp.float32),
        out_specs=VMEM,
        cost_estimate=pl.CostEstimate(flops=LONG, bytes_accessed=0, transcendentals=0),
        name="hadamard_signs",
    )()


def sign_table_kernel(plain_ref, signs_ref, out_ref):
    for b in range(out_ref.shape[0]):
        out_ref[b] = (plain_ref[...] * signs_ref[b]).astype(jnp.bfloat16)


def sign_table(plain, bits):
    signs = (2 * bits - 1).astype(jnp.float32).reshape(-1, HB, 1)
    return pl.pallas_call(
        sign_table_kernel,
        out_shape=jax.ShapeDtypeStruct((signs.shape[0], HB, HB), jnp.bfloat16),
        in_specs=[VMEM] * 2,
        out_specs=VMEM,
        cost_estimate=pl.CostEstimate(flops=0, bytes_accessed=0, transcendentals=0),
        name="sign_table",
    )(plain, signs)


def after(value, *others):
    return lax.optimization_barrier((value, *others))[0]


def rotate_kernel(place_ref, *refs):
    base, core = place_ref[0], place_ref[1]
    own, other, (table_ref, held_ref, a_ref, b_ref), outs = refs[:2], refs[2:4], refs[4:8], refs[8:]
    rows = own[0].shape[0] // 2
    tokens = outs[0].shape[1]
    norm = HB ** -0.5
    for k in range(4):
        slot = jnp.bitwise_xor(base, k)
        weights = own if k % 2 == 0 else other
        near = k // 2 * tokens
        total = None
        for x in range(4):
            at = slice(near, near + tokens)
            turn = core if x == 1 else 1 - core
            place = pl.ds(pl.multiple_of(turn * rows, rows), rows) if x % 2 else slice(x // 2 * rows, (x // 2 + 1) * rows)
            weight = weights[(x + 1) % 2][place, :]
            grads = (held_ref[at, :], a_ref[at, :], b_ref[1, at, :], b_ref[0, at, :])[x]
            term = lax.dot_general(weight, grads, (((1,), (1,)), ((), ())), preferred_element_type=jnp.float32)
            total = term if total is None else total + term
        high = total.astype(jnp.bfloat16)
        low = (total - high.astype(jnp.float32)).astype(jnp.bfloat16)
        turned = []
        for b in range(rows // HB):
            rows_at = slice(b * HB, (b + 1) * HB)
            both = jnp.concatenate([high[rows_at], low[rows_at]], axis=0)
            table = table_ref[k % 2 * (rows // HB) + b]
            turned.append((jnp.dot(table, both, preferred_element_type=jnp.float32) * norm).astype(jnp.bfloat16))
        done = jnp.concatenate(turned, axis=0)
        for r, out_ref in enumerate(outs):

            @pl.when(slot == r)
            def _():
                out_ref[...] = done


def rotate(place, weights, table, grads):
    rows = weights[0].shape[0] // 2
    tokens = grads[0].shape[0] // 2
    return pl.pallas_call(
        rotate_kernel,
        out_shape=[jax.ShapeDtypeStruct((rows, tokens), jnp.bfloat16)] * 4,
        in_specs=[SMEM] + [VMEM] * 8,
        out_specs=[VMEM] * 4,
        compiler_params=pltpu.CompilerParams(vmem_limit_bytes=40 * 1024 * 1024),
        cost_estimate=pl.CostEstimate(flops=0, bytes_accessed=0, transcendentals=0),
        name="rotate",
    )(place, *weights, table, *grads)


def back_kernel(here_ref, p0, p1, p2, p3, limit_ref, table_ref, out_ref):
    here = here_ref[0]
    pieces = (p0, p1, p2, p3)
    blocks = p0.shape[0] // HB
    norm = HB ** -0.5
    for r, piece in enumerate(pieces):
        first = jnp.bitwise_xor(here, r) * blocks

        for b in range(blocks):
            limit = limit_ref[first + b]
            values = piece[b * HB : (b + 1) * HB, :].astype(jnp.float32)
            values = jnp.clip(values, -limit, limit).astype(jnp.bfloat16)
            turned = jnp.dot(table_ref[first + b], values, preferred_element_type=jnp.float32) * norm
            out_ref[pl.ds(pl.multiple_of((first + b) * HB, HB), HB), :] = turned.astype(jnp.bfloat16)


def back(here, pieces, limit, table):
    rows, tokens = pieces[0].shape
    return pl.pallas_call(
        back_kernel,
        out_shape=jax.ShapeDtypeStruct((len(pieces) * rows, tokens), jnp.bfloat16),
        in_specs=[SMEM] + [VMEM] * 6,
        out_specs=VMEM,
        compiler_params=pltpu.CompilerParams(vmem_limit_bytes=40 * 1024 * 1024),
        cost_estimate=pl.CostEstimate(flops=2 * 4 * rows * tokens * HB, bytes_accessed=7 << 20, transcendentals=0),
        name="rotate_back",
    )(here, *pieces, limit, table)


def product_kernel(skip, arrived, block_ref, inputs_ref, got_ref, grads_ref, other_ref, *rest):
    arrived, outs, (held, done) = rest[:arrived], rest[arrived:-2], rest[-2:]
    tile = held.shape[2]
    tiles = (got_ref.shape[1] - skip) // tile
    sum_rows = (((0,), (0,)), ((), ()))
    start = block_ref[0] * tiles

    def fetch(i):
        at = pl.ds(pl.multiple_of((start + i) * tile, tile), tile)
        return pltpu.make_async_copy(inputs_ref.at[:, at], held.at[i % 2], done.at[i % 2])

    fetch(0).start()
    for i in range(tiles):
        if i + 1 < tiles:
            fetch(i + 1).start()
        fetch(i).wait()
        got = got_ref[:, skip + i * tile : skip + (i + 1) * tile]
        total = lax.dot_general(held[i % 2], grads_ref[...], sum_rows, preferred_element_type=jnp.float32)
        other = other_ref[:, : grads_ref.shape[1]]
        total += lax.dot_general(got, other, sum_rows, preferred_element_type=jnp.float32)

        def part(refs):
            row = i * tile
            for ref in refs:
                if row < ref.shape[0]:
                    return ref.at[row : row + tile, :]
                row -= ref.shape[0]

        if arrived:
            total += part(arrived)[...].astype(jnp.float32)
        part(outs)[...] = total.astype(outs[0].dtype)


def product(inputs, block, got, grads, other, dtype, outs, skip=0, arrived=()):
    tokens, columns = grads.shape
    rows = got.shape[1] - skip
    return pl.pallas_call(
        functools.partial(product_kernel, skip, len(arrived)),
        out_shape=[jax.ShapeDtypeStruct((rows // 4 * quarters, columns), dtype) for quarters in outs],
        in_specs=[SMEM, pl.BlockSpec(memory_space=pltpu.HBM)] + [VMEM] * (3 + len(arrived)),
        out_specs=[VMEM] * len(outs),
        scratch_shapes=[pltpu.VMEM((2, tokens, rows // 4), inputs.dtype), pltpu.SemaphoreType.DMA((2,))],
        compiler_params=pltpu.CompilerParams(vmem_limit_bytes=40 * 1024 * 1024),
        cost_estimate=pl.CostEstimate(flops=0, bytes_accessed=0, transcendentals=0),
        name="weight_product",
    )(block, inputs, got, grads, other, *arrived)


def body(earlier_inputs, earlier_grads, current_grads, key_value_weight, exponents, sign_bits):
    chip, core, tensor = (lax.axis_index(axis) for axis in AXES[1:])
    dp = chip * lax.axis_size("core") + core
    parts = lax.axis_size("tensor")
    inputs_local, grads_before, weight_local = earlier_inputs[0], earlier_grads[0], key_value_weight[0]
    rows_here = weight_local.shape[0]
    quarter = rows_here // parts

    def scalar(value):
        return jnp.reshape(value, (1,)).astype(jnp.int32)

    def features(inputs, block):
        return lax.dynamic_slice_in_dim(inputs, block * rows_here, rows_here, 1)

    def down(shard, turn=0):
        return send(shard, lambda s, d, t: (s - 1, d ^ 2, t ^ turn))

    def over_z(shard, x):
        return send(shard, lambda s, d, t: (s, d, t ^ x))

    quarters = [
        lax.dynamic_slice_in_dim(weight_local, jnp.bitwise_xor(tensor, x) * quarter, quarter, 0) for x in range(parts)
    ]

    tokens, columns = current_grads.shape[1:]
    plain = hadamard_signs(HB)
    dealt = [quarters[0], over_z(quarters[1], 1), None, over_z(quarters[3], 3)]
    limit = (FP8_LIMIT * jnp.exp2(exponents[0].astype(jnp.float32))).astype(jnp.bfloat16)
    blocks = limit.shape[0]
    limit = jnp.pad(limit, ((0, -blocks % 16), (0, 0)))
    grads_far = down(jnp.concatenate([current_grads[0], limit], axis=0))

    inputs_then = after(inputs_local, quarters[1])
    got_far = other_core(jnp.concatenate([grads_before, features(inputs_then, jnp.bitwise_xor(dp, 3))], axis=1))
    (partial,) = product(
        inputs_local, scalar(jnp.bitwise_xor(dp, 2)), got_far, grads_before, got_far, jnp.bfloat16, (4,), columns
    )
    grads_far, dealt[1], dealt[3], partial, second = lax.optimization_barrier(
        (grads_far, dealt[1], dealt[3], partial, quarters[2])
    )

    dealt[2] = over_z(second, 2)
    grads_near = other_chip(grads_far)
    half = down(jnp.concatenate([dealt[1], dealt[3]], axis=0))
    arrived = other_chip(after(partial, grads_near))
    bits = lax.dynamic_slice_in_dim(sign_bits, dp * quarter, quarter, 0)
    bits = send(bits, lambda s, d, t: (s, t ^ 2, d))
    other_half = down(after(jnp.concatenate([dealt[0], dealt[2]], axis=0), grads_near))
    got_near = other_core(features(after(inputs_local, grads_near), jnp.bitwise_xor(dp, 1)))
    here = sign_table(plain, sign_bits)
    grads_near, plain, bits, here = lax.optimization_barrier((grads_near, plain, bits, here))

    limit = grads_near[tokens : tokens + blocks]
    held = jnp.concatenate([grads_near[:tokens], grads_far[:tokens]], axis=0)
    step_a = send(held, lambda s, d, t: (s, d, t ^ (3 if d & 1 else 1)))
    step_a, half, bits_other = lax.optimization_barrier((step_a, half, other_core(bits)))
    step_b = send(jnp.stack([held, step_a]), lambda s, d, t: (s, d, t ^ (1 if d & 1 else 3)))
    weights = (half, other_half, other_core(half), other_core(other_half))
    bits = jnp.concatenate([bits, bits_other])
    step_b, got_near, *weights = lax.optimization_barrier((step_b, got_near, *weights))

    signs_there = (2 * bits - 1).astype(jnp.float32).reshape(-1, 1, HB)
    table = (plain * signs_there).astype(jnp.bfloat16)
    turned = rotate(
        jnp.stack([jnp.bitwise_xor(dp, tensor), core]).astype(jnp.int32),
        weights,
        jnp.concatenate([table, table], axis=2),
        (held, step_a, step_b),
    )

    arrived, *later = lax.optimization_barrier((arrived, *turned[2:]))
    turned = [*turned[:2], *later]

    pieces = [
        send(turned[r], lambda s, d, t, r=r: (s, (t ^ r) & 2 | d & 1, (d & 2 ^ 2) | (t ^ r) & 1)) for r in range(parts)
    ]
    limit = limit.astype(jnp.float32)[:, None, :]
    (weight_grad,) = product(
        inputs_local, scalar(dp), got_near, grads_before, got_far, jnp.float32, (4,), 0, (arrived,)
    )
    place = scalar(chip * 2 + jnp.bitwise_and(tensor, 1))
    upstream_grad = back(place, pieces, limit, here)
    return (upstream_grad[None], weight_grad[None])


def solution(mesh):
    sections, dps, tensors = (mesh.shape[axis] for axis in ("section", "dp", "tensor"))
    split = Mesh(mesh.devices.reshape(sections, dps // 2, 2, tensors), AXES)
    dp = ("chip", "core")
    placed = (
        P("section", dp, None),
        P("section", dp, "tensor"),
        P("section", dp, "tensor"),
        P("section", dp, "tensor"),
        P("section", "tensor", dp),
        P("tensor"),
    )
    return jax.shard_map(
        body,
        mesh=split,
        in_specs=placed,
        out_specs=(P("section", "tensor", dp), P("section", dp, "tensor")),
        check_vma=False,
    )
```

time: 241 us -> 179 us (0.74); the launches traced: 237 us -> 179 us
  waiting for transfers between devices: 119 us -> 86.9 us
  Pallas kernels: 22.3 us -> 43.5 us
  matrix products: 19.6 us -> 0 us
  starting transfers between devices: 46 us -> 29.7 us
  local copies, waits for them, and re-layouts: 22 us -> 12.8 us
    ppermute x24 -> x20, waiting for transfers between devices: 119 us -> 86.9 us  [send(): return lax.ppermute(shard, AXES, pairs)]
    pallas_call x1 -> x5, Pallas kernels: 16 us -> 39.4 us  [the longest x2 21.9 us: product(): pl.pallas_call(functools.partial(product_kernel, skip, len(arrived)), out...]
    dot_general x4 -> x0, matrix products: 19.6 us -> none  [the longest x2 10.3 us: product(): lax.dot_general(mine, grads_before, (((0,), (0,)), ((), ())), preferred_e...]
    ppermute x24 -> x20, starting transfers between devices: 46 us -> 29.7 us  [send(): return lax.ppermute(shard, AXES, pairs)]
    unnamed x32 -> x14, local copies, waits for them, and re-layouts: 9.93 us -> 0.63 us
    broadcast_in_dim x1, other arithmetic: 6.38 us -> 0.74 us  [body(): limit = limit.astype(jnp.float32)[:, None, :]]
    dynamic_slice x2 -> x3, local copies, waits for them, and re-layouts: 7.87 us -> 9.3 us  [the longest x2 5.91 us: features(): return lax.dynamic_slice_in_dim(inputs, block * rows_here, rows_here, 1)]
  transfers between devices with their start and end apart: 24 -> 20, of which waited for: 13 -> 9; matrix products, arithmetic and copies ran while one was open for 15% -> 5% of each run, Pallas kernels for 9% -> 22%
where the time goes in v2:
time: 179 us
  waiting for transfers between devices  86.9 us (49%)
  Pallas kernels  43.5 us (24%)
  starting transfers between devices  29.7 us (17%)
  local copies, waits for them, and re-layouts  12.8 us (7%)
  other arithmetic  4.94 us (3%)
    ppermute x20, waiting for transfers between devices, send(): return lax.ppermute(shard, AXES, pairs)  86.9 us
    ppermute x20, starting transfers between devices, send(): return lax.ppermute(shard, AXES, pairs)  29.7 us
    pallas_call x2, Pallas kernels, product(): pl.pallas_call(functools.partial(product_kernel, skip, len(arrived)), out...  21.9 us
    pallas_call x1, Pallas kernels, rotate(): pl.pallas_call(rotate_kernel, out_shape=[jax.ShapeDtypeStruct((rows, toke...  14 us
    dynamic_slice x2, local copies, waits for them, and re-layouts, features(): return lax.dynamic_slice_in_dim(inputs, block * rows_here, rows_here, 1)  5.91 us
    pallas_call x1, Pallas kernels, back(): pl.pallas_call(back_kernel, out_shape=jax.ShapeDtypeStruct((len(pieces) *...  4.07 us
  transfers between devices with their start and end apart: 20, of which 9 were waited for; matrix products, arithmetic and copies ran while one was open for 5% of the time, Pallas kernels for 22%

profile of v2, /device:TPU:20, one launch (start us, length us, event | category | flops | bytes accessed | tf_op | source)
XLA Modules:
  0.0 178.7 jit_solution(11814289819477664011)
XLA Ops:
  0.7 3.4 %dynamic-slice_bitcast_fusion = (bf16[768,512]{1,0:T(8,128)(2,1)S(1)}, bf16[768,512]{1,0:T(8,128)(2,1)}, bf16[768,512]{1,0:T(8,128)(2,1)}, bf16[768,512]{1,0:T(8,128)(2,1)}) fusion(bf16[1,3072,512]{2,1,0:T(8,128)(2,1)} %param.9, s32[]{:T(128)S(6)} %select_n.27, s32[]{:T(128)S(6)} %select_n.22, s32[]{:T(128)S(6)} %select_n.21, s32[]{:T(128)S(6)} %select_n.24), kind=kLoop, calls=%fused_computation.9 | loop fusion | bytes 6291472 | tf_op jit(solution)/shard_map/dynamic_slice | solution.py:227
  4.1 2.2 %constant_dynamic-slice_fusion.1 = bf16[512,3072]{1,0:T(8,128)(2,1)S(1)} fusion(bf16[512,12288]{1,0:T(8,128)(2,1)} %bitcast.31, s32[]{:T(128)S(6)} %select_n.23), kind=kLoop, calls=%fused_computation.22 | loop fusion | bytes 6291460 | tf_op jit(solution)/shard_map/dynamic_slice | solution.py:218
  6.2 0.0 copy-start.5
  6.3 2.1 %pad_maximum_fusion = bf16[512,3584]{1,0:T(8,128)(2,1)} fusion(bf16[512,3072]{1,0:T(8,128)(2,1)S(1)} %constant_dynamic-slice_fusion.1, bf16[512,512]{1,0:T(8,128)(2,1)S(1)} %bitcast.27), kind=kLoop, calls=%fused_computation | loop fusion | flops 7340032 | bytes 7340032 | tf_op jit(solution)/shard_map/concatenate | solution.py:239
  8.3 1.9 %collective-permute-start.1 = (bf16[768,512]{1,0:T(8,128)(2,1)}, bf16[768,512]{1,0:T(8,128)(2,1)S(1)}, u32[]{:S(2)}, u32[]{:S(2)}) collective-permute-start(bf16[768,512]{1,0:T(8,128)(2,1)} %get-tuple-element.62), channel_id=1, source_target_pairs={{0,1},{1,0},{2,3},{3,2},{4,5},{5,4},{6,7},{7,6},{8,9},{9,8},{10,11... | collective-permute-start | bytes 2359304 | tf_op jit(solution)/shard_map/ppermute | solution.py:29
  10.2 2.5 %collective-permute-start.2 = (bf16[768,512]{1,0:T(8,128)(2,1)}, bf16[768,512]{1,0:T(8,128)(2,1)S(1)}, u32[]{:S(2)}, u32[]{:S(2)}) collective-permute-start(bf16[768,512]{1,0:T(8,128)(2,1)} %get-tuple-element.61), channel_id=1, source_target_pairs={{0,3},{1,2},{2,1},{3,0},{4,7},{5,6},{6,5},{7,4},{8,11},{9,10},{10,... | collective-permute-start | bytes 2359304 | tf_op jit(solution)/shard_map/ppermute | solution.py:29
  12.8 2.4 %collective-permute-start = (bf16[544,512]{1,0:T(8,128)(2,1)S(1)}, bf16[544,512]{1,0:T(8,128)(2,1)}, u32[]{:S(2)}, u32[]{:S(2)}) collective-permute-start(bf16[544,512]{1,0:T(8,128)(2,1)S(1)} %fusion.1), channel_id=1, source_target_pairs={{16,8},{17,9},{18,10},{19,11},{20,12},{21,13},{22,14},{23,15},{24,... | collective-permute-start | bytes 1671176 | tf_op jit(solution)/shard_map/ppermute | solution.py:29
  15.3 0.1 dynamic_slice.36
  15.4 1.1 collective-permute-start.5
  16.5 10.0 %weight_product.2 = bf16[3072,512]{1,0:T(8,128)(2,1)} custom-call(s32[1]{0:T(128)} %bitcast.7.block_ref, bf16[512,12288]{1,0:T(8,128)(2,1)} %bitcast.32, bf16[512,3584]{1,0:T(8,128)(2,1)} %collective-permute-done.3.got_ref.other_ref, bf16[512,512]{1,0:T(8,128)(2,1)S(1)} %bitcast.28, bf16[512,3584]{1,0:T(8,128)(2,1)} %collective-permute-done.3.got_ref.other_ref), custom_call_target="tpu_custom_call" | custom-call | tf_op jit(solution)/shard_map/weight_product/pallas_call | solution.py:194
  26.6 3.7 %collective-permute-done = bf16[544,512]{1,0:T(8,128)(2,1)} collective-permute-done((bf16[544,512]{1,0:T(8,128)(2,1)S(1)}, bf16[544,512]{1,0:T(8,128)(2,1)}, u32[]{:S(2)}, u32[]{:S(2)}) %collective-permute-start) | collective-permute-done | bytes 557088 | tf_op jit(solution)/shard_map/ppermute | solution.py:29
  30.2 1.1 collective-permute-done.2
  31.3 1.3 collective-permute-start.4
  32.6 0.7 hadamard_signs.1.plain_ref
  33.3 1.7 copy.8.signs_ref
  35.0 2.8 %sign_table.1.table_ref = bf16[24,128,128]{2,1,0:T(8,128)(2,1)} custom-call(f32[128,128]{1,0:T(8,128)} %hadamard_signs.1.plain_ref, f32[24,128,1]{2,1,0:T(8,128)} %copy.8.signs_ref), custom_call_target="tpu_custom_call" | custom-call | tf_op jit(solution)/shard_map/sign_table/pallas_call | solution.py:66
  37.8 2.3 %collective-permute-start.11 = (bf16[768,512]{1,0:T(8,128)(2,1)}, bf16[768,512]{1,0:T(8,128)(2,1)S(1)}, u32[]{:S(2)}, u32[]{:S(2)}) collective-permute-start(bf16[768,512]{1,0:T(8,128)(2,1)} %get-tuple-element.40), channel_id=1, source_target_pairs={{0,2},{1,3},{2,0},{3,1},{4,6},{5,7},{6,4},{7,5},{8,10},{9,11},{10,... | collective-permute-start | bytes 2359304 | tf_op jit(solution)/shard_map/ppermute | solution.py:29
  40.1 0.1 pad_maximum_fusion.2
  40.2 1.1 slice.10
  41.3 1.9 %collective-permute-start.7 = (bf16[1536,512]{1,0:T(8,128)(2,1)S(1)}, bf16[1536,512]{1,0:T(8,128)(2,1)}, u32[]{:S(2)}, u32[]{:S(2)}) collective-permute-start(bf16[1536,512]{1,0:T(8,128)(2,1)S(1)} %pad_maximum_fusion.2), channel_id=1, source_target_pairs={{16,8},{17,9},{18,10},{19,11},{20,12},{21,13},{22,14},{23,15},{24,... | collective-permute-start | bytes 4718600 | tf_op jit(solution)/shard_map/ppermute | solution.py:29
  43.2 2.3 %collective-permute-done.4 = bf16[544,512]{1,0:T(8,128)(2,1)S(1)} collective-permute-done((bf16[544,512]{1,0:T(8,128)(2,1)}, bf16[544,512]{1,0:T(8,128)(2,1)S(1)}, u32[]{:S(2)}, u32[]{:S(2)}) %collective-permute-start.4) | collective-permute-done | bytes 557088 | tf_op jit(solution)/shard_map/ppermute | solution.py:29
  45.6 0.1 fusion.5
  45.7 0.6 copy-done.2
  46.3 0.9 collective-permute-start.6
  47.2 3.8 %constant_dynamic-slice_fusion = bf16[512,3072]{1,0:T(8,128)(2,1)} fusion(bf16[512,12288]{1,0:T(8,128)(2,1)} %bitcast.33, s32[]{:T(128)S(6)} %select_n.26), kind=kLoop, calls=%fused_computation.21 | loop fusion | bytes 6291460 | tf_op jit(solution)/shard_map/dynamic_slice | solution.py:218
  51.0 1.3 collective-permute-start.10
  52.3 5.9 %collective-permute-done.11 = bf16[768,512]{1,0:T(8,128)(2,1)S(1)} collective-permute-done((bf16[768,512]{1,0:T(8,128)(2,1)}, bf16[768,512]{1,0:T(8,128)(2,1)S(1)}, u32[]{:S(2)}, u32[]{:S(2)}) %collective-permute-start.11) | collective-permute-done | bytes 786464 | tf_op jit(solution)/shard_map/ppermute | solution.py:29
  58.2 0.1 pad_maximum_fusion.3
  58.3 1.9 %collective-permute-start.12 = (bf16[1536,512]{1,0:T(8,128)(2,1)S(1)}, bf16[1536,512]{1,0:T(8,128)(2,1)}, u32[]{:S(2)}, u32[]{:S(2)}) collective-permute-start(bf16[1536,512]{1,0:T(8,128)(2,1)S(1)} %pad_maximum_fusion.3), channel_id=1, source_target_pairs={{16,8},{17,9},{18,10},{19,11},{20,12},{21,13},{22,14},{23,15},{24,... | collective-permute-start | bytes 4718600 | tf_op jit(solution)/shard_map/ppermute | solution.py:29
  60.2 1.9 %collective-permute-start.17 = (bf16[3072,512]{1,0:T(8,128)(2,1)}, bf16[3072,512]{1,0:T(8,128)(2,1)}, u32[]{:S(2)}, u32[]{:S(2)}) collective-permute-start(bf16[3072,512]{1,0:T(8,128)(2,1)} %weight_product.2), channel_id=1, source_target_pairs={{0,8},{1,9},{2,10},{3,11},{4,12},{5,13},{6,14},{7,15},{8,0},{9,1},... | collective-permute-start | bytes 9437192 | tf_op jit(solution)/shard_map/ppermute | solution.py:29
  62.2 19.4 %collective-permute-done.7.refs_0_ = bf16[1536,512]{1,0:T(8,128)(2,1)} collective-permute-done((bf16[1536,512]{1,0:T(8,128)(2,1)S(1)}, bf16[1536,512]{1,0:T(8,128)(2,1)}, u32[]{:S(2)}, u32[]{:S(2)}) %collective-permute-start.7) | collective-permute-done | bytes 1572896 | tf_op jit(solution)/shard_map/ppermute | solution.py:29
  81.5 1.5 pad_maximum_fusion.1
  83.0 1.4 collective-permute-start.9
  84.4 28.6 %collective-permute-done.12.refs_1_ = bf16[1536,512]{1,0:T(8,128)(2,1)} collective-permute-done((bf16[1536,512]{1,0:T(8,128)(2,1)S(1)}, bf16[1536,512]{1,0:T(8,128)(2,1)}, u32[]{:S(2)}, u32[]{:S(2)}) %collective-permute-start.12) | collective-permute-done | bytes 1572896 | tf_op jit(solution)/shard_map/ppermute | solution.py:29
  113.0 0.1 pad_add_fusion.place_ref
  113.1 0.1 multiply_convert_fusion
  113.2 0.1 pad_maximum_fusion.5.refs_4_
  113.3 3.5 %collective-permute-done.14.refs_3_ = bf16[1536,512]{1,0:T(8,128)(2,1)} collective-permute-done((bf16[1536,512]{1,0:T(8,128)(2,1)}, bf16[1536,512]{1,0:T(8,128)(2,1)}, u32[]{:S(2)}, u32[]{:S(2)}) %collective-permute-start.14) | collective-permute-done | bytes 1572896 | tf_op jit(solution)/shard_map/ppermute | solution.py:29
  116.8 14.0 %rotate.1 = (bf16[768,512]{1,0:T(8,128)(2,1)}, bf16[768,512]{1,0:T(8,128)(2,1)}, bf16[768,512]{1,0:T(8,128)(2,1)}, bf16[768,512]{1,0:T(8,128)(2,1)}) custom-call(s32[2]{0:T(128)S(1)} %pad_add_fusion.place_ref, bf16[1536,512]{1,0:T(8,128)(2,1)} %collective-permute-done.7.refs_0_, bf16[1536,512]{1,0:T(8,128)(2,1)} %collective-permute-done.12.refs_1_, ...), custom_call_target="tpu_custom_call" | custom-call | tf_op jit(solution)/shard_map/rotate/pallas_call | solution.py:118
  130.8 1.2 collective-permute-start.15
  132.0 2.0 %collective-permute-start.16 = (bf16[768,512]{1,0:T(8,128)(2,1)}, bf16[768,512]{1,0:T(8,128)(2,1)S(1)}, u32[]{:S(2)}, u32[]{:S(2)}) collective-permute-start(bf16[768,512]{1,0:T(8,128)(2,1)} %get-tuple-element.50), channel_id=1, source_target_pairs={{0,3},{1,2},{2,11},{3,10},{4,7},{5,6},{6,15},{7,14},{8,1},{9,0},{1... | collective-permute-start | bytes 2359304 | tf_op jit(solution)/shard_map/ppermute | solution.py:29
  134.0 3.6 %collective-permute-start.18 = (bf16[768,512]{1,0:T(8,128)(2,1)}, bf16[768,512]{1,0:T(8,128)(2,1)S(1)}, u32[]{:S(2)}, u32[]{:S(2)}) collective-permute-start(bf16[768,512]{1,0:T(8,128)(2,1)} %get-tuple-element.55), channel_id=1, source_target_pairs={{0,10},{1,11},{2,2},{3,3},{4,14},{5,15},{6,6},{7,7},{8,8},{9,9},{1... | collective-permute-start | bytes 2359304 | tf_op jit(solution)/shard_map/ppermute | solution.py:29
  137.7 1.8 %collective-permute-start.19 = (bf16[768,512]{1,0:T(8,128)(2,1)}, bf16[768,512]{1,0:T(8,128)(2,1)}, u32[]{:S(2)}, u32[]{:S(2)}) collective-permute-start(bf16[768,512]{1,0:T(8,128)(2,1)} %get-tuple-element.56), channel_id=1, source_target_pairs={{0,11},{1,10},{2,3},{3,2},{4,15},{5,14},{6,7},{7,6},{8,9},{9,8},{1... | collective-permute-start | bytes 2359304 | tf_op jit(solution)/shard_map/ppermute | solution.py:29
  139.5 0.7 slice_convert_fusion
  140.3 11.9 %weight_product.3 = f32[3072,512]{1,0:T(8,128)} custom-call(s32[1]{0:T(128)} %bitcast.18.block_ref, bf16[512,12288]{1,0:T(8,128)(2,1)} %bitcast.34, bf16[512,3072]{1,0:T(8,128)(2,1)} %collective-permute-done.10.got_ref, bf16[512,512]{1,0:T(8,128)(2,1)S(1)} %bitcast.29, bf16[512,3584]{1,0:T(8,128)(2,1)} %collective-permute-done.3.got_ref.other_ref, ...), custom_call_target="tpu_custom_call" | custom-call | tf_op jit(solution)/shard_map/weight_product/pallas_call | solution.py:194
  152.2 16.0 %collective-permute-done.16.p1 = bf16[768,512]{1,0:T(8,128)(2,1)S(1)} collective-permute-done((bf16[768,512]{1,0:T(8,128)(2,1)}, bf16[768,512]{1,0:T(8,128)(2,1)S(1)}, u32[]{:S(2)}, u32[]{:S(2)}) %collective-permute-start.16) | collective-permute-done | bytes 786464 | tf_op jit(solution)/shard_map/ppermute | solution.py:29
  168.1 6.5 %collective-permute-done.19.p3 = bf16[768,512]{1,0:T(8,128)(2,1)} collective-permute-done((bf16[768,512]{1,0:T(8,128)(2,1)}, bf16[768,512]{1,0:T(8,128)(2,1)}, u32[]{:S(2)}, u32[]{:S(2)}) %collective-permute-start.19) | collective-permute-done | bytes 786464 | tf_op jit(solution)/shard_map/ppermute | solution.py:29
  174.6 4.1 %rotate_back.1 = bf16[3072,512]{1,0:T(8,128)(2,1)} custom-call(s32[1]{0:T(128)} %bitcast.here_ref, bf16[768,512]{1,0:T(8,128)(2,1)S(1)} %collective-permute-done.15.p0, bf16[768,512]{1,0:T(8,128)(2,1)S(1)} %collective-permute-done.16.p1, bf16[768,512]{1,0:T(8,128)(2,1)S(1)} %collective-permute-done.18.p2, bf16[768,512]{1,0:T(8,128)(2,1)} %collective-permute-done.19.p3, ...), custom_call_target="tpu_custom_call" | custom-call | flops 402653184 | bytes 7340032 | tf_op jit(solution)/shard_map/rotate_back/pallas_call | solution.py:147
  (33 shorter events, 0.2 us)
Async XLA Ops:
  4.0 2.2 %copy-start = (bf16[1,512,512]{2,1,0:T(8,128)(2,1)S(1)}, bf16[1,512,512]{2,1,0:T(8,128)(2,1)}, u32[]{:S(2)}) copy-start(bf16[1,512,512]{2,1,0:T(8,128)(2,1)} %param.7) | copy-start | bytes 1572868
  6.2 6.6 %copy-start.5 = (s32[1,24,512]{2,1,0:T(8,128)S(1)}, s32[1,24,512]{2,1,0:T(8,128)}, u32[]{:S(2)}) copy-start(s32[1,24,512]{2,1,0:T(8,128)} %param.10) | copy-start | bytes 147460
  6.2 6.6 %copy-start.3 = (bf16[1,512,512]{2,1,0:T(8,128)(2,1)S(1)}, bf16[1,512,512]{2,1,0:T(8,128)(2,1)}, u32[]{:S(2)}) copy-start(bf16[1,512,512]{2,1,0:T(8,128)(2,1)} %param.8) | copy-start | bytes 1572868
  6.2 9.1 %copy-start.6 = (s32[3072]{0:T(1024)S(1)}, s32[3072]{0:T(1024)}, u32[]{:S(2)}) copy-start(s32[3072]{0:T(1024)} %param.11) | copy-start | bytes 36868
  8.3 8.2 %collective-permute-start.3 = (bf16[512,3584]{1,0:T(8,128)(2,1)}, bf16[512,3584]{1,0:T(8,128)(2,1)}, u32[]{:S(2)}, u32[]{:S(2)}) collective-permute-start(bf16[512,3584]{1,0:T(8,128)(2,1)} %pad_maximum_fusion), channel_id=1, source_target_pairs={{0,4},{1,5},{2,6},{3,7},{4,0},{5,1},{6,2},{7,3},{8,12},{9,13},{10,... | collective-permute-start | bytes 11010056 | tf_op jit(solution)/shard_map/ppermute | solution.py:29
  8.3 23.0 %collective-permute-start.1 = (bf16[768,512]{1,0:T(8,128)(2,1)}, bf16[768,512]{1,0:T(8,128)(2,1)S(1)}, u32[]{:S(2)}, u32[]{:S(2)}) collective-permute-start(bf16[768,512]{1,0:T(8,128)(2,1)} %get-tuple-element.62), channel_id=1, source_target_pairs={{0,1},{1,0},{2,3},{3,2},{4,5},{5,4},{6,7},{7,6},{8,9},{9,8},{10,11... | collective-permute-start | bytes 2359304 | tf_op jit(solution)/shard_map/ppermute | solution.py:29
  10.2 21.1 %collective-permute-start.2 = (bf16[768,512]{1,0:T(8,128)(2,1)}, bf16[768,512]{1,0:T(8,128)(2,1)S(1)}, u32[]{:S(2)}, u32[]{:S(2)}) collective-permute-start(bf16[768,512]{1,0:T(8,128)(2,1)} %get-tuple-element.61), channel_id=1, source_target_pairs={{0,3},{1,2},{2,1},{3,0},{4,7},{5,6},{6,5},{7,4},{8,11},{9,10},{10,... | collective-permute-start | bytes 2359304 | tf_op jit(solution)/shard_map/ppermute | solution.py:29
  12.8 17.4 %collective-permute-start = (bf16[544,512]{1,0:T(8,128)(2,1)S(1)}, bf16[544,512]{1,0:T(8,128)(2,1)}, u32[]{:S(2)}, u32[]{:S(2)}) collective-permute-start(bf16[544,512]{1,0:T(8,128)(2,1)S(1)} %fusion.1), channel_id=1, source_target_pairs={{16,8},{17,9},{18,10},{19,11},{20,12},{21,13},{22,14},{23,15},{24,... | collective-permute-start | bytes 1671176 | tf_op jit(solution)/shard_map/ppermute | solution.py:29
  15.4 30.1 %collective-permute-start.5 = (s32[768]{0:T(1024)S(1)}, s32[768]{0:T(1024)S(1)}, u32[]{:S(2)}, u32[]{:S(2)}) collective-permute-start(s32[768]{0:T(1024)S(1)} %dynamic_slice.36), channel_id=1, source_target_pairs={{0,8},{1,12},{2,0},{3,4},{4,9},{5,13},{6,1},{7,5},{8,10},{9,14},{1... | collective-permute-start | bytes 9224 | tf_op jit(solution)/shard_map/ppermute | solution.py:29
  31.3 14.2 %collective-permute-start.4 = (bf16[544,512]{1,0:T(8,128)(2,1)}, bf16[544,512]{1,0:T(8,128)(2,1)S(1)}, u32[]{:S(2)}, u32[]{:S(2)}) collective-permute-start(bf16[544,512]{1,0:T(8,128)(2,1)} %collective-permute-done), channel_id=1, source_target_pairs={{0,8},{1,9},{2,10},{3,11},{4,12},{5,13},{6,14},{7,15},{8,0},{9,1},... | collective-permute-start | bytes 1671176 | tf_op jit(solution)/shard_map/ppermute | solution.py:29
  37.8 20.4 %collective-permute-start.11 = (bf16[768,512]{1,0:T(8,128)(2,1)}, bf16[768,512]{1,0:T(8,128)(2,1)S(1)}, u32[]{:S(2)}, u32[]{:S(2)}) collective-permute-start(bf16[768,512]{1,0:T(8,128)(2,1)} %get-tuple-element.40), channel_id=1, source_target_pairs={{0,2},{1,3},{2,0},{3,1},{4,6},{5,7},{6,4},{7,5},{8,10},{9,11},{10,... | collective-permute-start | bytes 2359304 | tf_op jit(solution)/shard_map/ppermute | solution.py:29
  41.3 40.2 %collective-permute-start.7 = (bf16[1536,512]{1,0:T(8,128)(2,1)S(1)}, bf16[1536,512]{1,0:T(8,128)(2,1)}, u32[]{:S(2)}, u32[]{:S(2)}) collective-permute-start(bf16[1536,512]{1,0:T(8,128)(2,1)S(1)} %pad_maximum_fusion.2), channel_id=1, source_target_pairs={{16,8},{17,9},{18,10},{19,11},{20,12},{21,13},{22,14},{23,15},{24,... | collective-permute-start | bytes 4718600 | tf_op jit(solution)/shard_map/ppermute | solution.py:29
  45.5 0.8 copy-start.2
  45.5 14.7 %collective-permute-start.8 = (s32[768]{0:T(1024)S(1)}, s32[768]{0:T(1024)S(1)}, u32[]{:S(2)}, u32[]{:S(2)}) collective-permute-start(s32[768]{0:T(1024)S(1)} %collective-permute-done.5), channel_id=1, source_target_pairs={{0,4},{1,5},{2,6},{3,7},{4,0},{5,1},{6,2},{7,3},{8,12},{9,13},{10,... | collective-permute-start | bytes 9224 | tf_op jit(solution)/shard_map/ppermute | solution.py:29
  46.3 35.2 %collective-permute-start.6 = (bf16[1024,512]{1,0:T(8,128)(2,1)S(1)}, bf16[1024,512]{1,0:T(8,128)(2,1)S(1)}, u32[]{:S(2)}, u32[]{:S(2)}) collective-permute-start(bf16[1024,512]{1,0:T(8,128)(2,1)S(1)} %get-tuple-element.65.refs_5_), channel_id=1, source_target_pairs={{0,1},{1,0},{2,3},{3,2},{4,7},{5,6},{6,5},{7,4},{8,9},{9,8},{10,11... | collective-permute-start | bytes 3145736 | tf_op jit(solution)/shard_map/ppermute | solution.py:29
  51.0 62.3 %collective-permute-start.10 = (bf16[512,3072]{1,0:T(8,128)(2,1)}, bf16[512,3072]{1,0:T(8,128)(2,1)}, u32[]{:S(2)}, u32[]{:S(2)}) collective-permute-start(bf16[512,3072]{1,0:T(8,128)(2,1)} %constant_dynamic-slice_fusion), channel_id=1, source_target_pairs={{0,4},{1,5},{2,6},{3,7},{4,0},{5,1},{6,2},{7,3},{8,12},{9,13},{10,... | collective-permute-start | bytes 9437192 | tf_op jit(solution)/shard_map/ppermute | solution.py:29
  58.2 54.9 %copy-start.4 = (f32[128,128]{1,0:T(8,128)S(1)}, f32[128,128]{1,0:T(8,128)}, u32[]{:S(2)}) copy-start(f32[128,128]{1,0:T(8,128)} %hadamard_signs.1.plain_ref) | copy-start | bytes 196612
  58.3 54.7 %collective-permute-start.12 = (bf16[1536,512]{1,0:T(8,128)(2,1)S(1)}, bf16[1536,512]{1,0:T(8,128)(2,1)}, u32[]{:S(2)}, u32[]{:S(2)}) collective-permute-start(bf16[1536,512]{1,0:T(8,128)(2,1)S(1)} %pad_maximum_fusion.3), channel_id=1, source_target_pairs={{16,8},{17,9},{18,10},{19,11},{20,12},{21,13},{22,14},{23,15},{24,... | collective-permute-start | bytes 4718600 | tf_op jit(solution)/shard_map/ppermute | solution.py:29
  60.2 73.8 %collective-permute-start.17 = (bf16[3072,512]{1,0:T(8,128)(2,1)}, bf16[3072,512]{1,0:T(8,128)(2,1)}, u32[]{:S(2)}, u32[]{:S(2)}) collective-permute-start(bf16[3072,512]{1,0:T(8,128)(2,1)} %weight_product.2), channel_id=1, source_target_pairs={{0,8},{1,9},{2,10},{3,11},{4,12},{5,13},{6,14},{7,15},{8,0},{9,1},... | collective-permute-start | bytes 9437192 | tf_op jit(solution)/shard_map/ppermute | solution.py:29
  83.0 30.3 %collective-permute-start.9 = (bf16[2,1024,512]{2,1,0:T(8,128)(2,1)}, bf16[2,1024,512]{2,1,0:T(8,128)(2,1)}, u32[]{:S(2)}, u32[]{:S(2)}) collective-permute-start(bf16[2,1024,512]{2,1,0:T(8,128)(2,1)} %pad_maximum_fusion.1), channel_id=1, source_target_pairs={{0,3},{1,2},{2,1},{3,0},{4,5},{5,4},{6,7},{7,6},{8,11},{9,10},{10,... | collective-permute-start | bytes 6291464 | tf_op jit(solution)/shard_map/ppermute | solution.py:29
  84.4 28.9 %collective-permute-start.13 = (bf16[1536,512]{1,0:T(8,128)(2,1)}, bf16[1536,512]{1,0:T(8,128)(2,1)}, u32[]{:S(2)}, u32[]{:S(2)}) collective-permute-start(bf16[1536,512]{1,0:T(8,128)(2,1)} %collective-permute-done.7.refs_0_), channel_id=1, source_target_pairs={{0,4},{1,5},{2,6},{3,7},{4,0},{5,1},{6,2},{7,3},{8,12},{9,13},{10,... | collective-permute-start | bytes 4718600 | tf_op jit(solution)/shard_map/ppermute | solution.py:29
  113.0 3.8 %collective-permute-start.14 = (bf16[1536,512]{1,0:T(8,128)(2,1)}, bf16[1536,512]{1,0:T(8,128)(2,1)}, u32[]{:S(2)}, u32[]{:S(2)}) collective-permute-start(bf16[1536,512]{1,0:T(8,128)(2,1)} %collective-permute-done.12.refs_1_), channel_id=1, source_target_pairs={{0,4},{1,5},{2,6},{3,7},{4,0},{5,1},{6,2},{7,3},{8,12},{9,13},{10,... | collective-permute-start | bytes 4718600 | tf_op jit(solution)/shard_map/ppermute | solution.py:29
  130.8 21.4 %collective-permute-start.15 = (bf16[768,512]{1,0:T(8,128)(2,1)}, bf16[768,512]{1,0:T(8,128)(2,1)S(1)}, u32[]{:S(2)}, u32[]{:S(2)}) collective-permute-start(bf16[768,512]{1,0:T(8,128)(2,1)} %get-tuple-element.49), channel_id=1, source_target_pairs={{0,2},{1,3},{2,10},{3,11},{4,6},{5,7},{6,14},{7,15},{8,0},{9,1},{1... | collective-permute-start | bytes 2359304 | tf_op jit(solution)/shard_map/ppermute | solution.py:29
  132.0 36.1 %collective-permute-start.16 = (bf16[768,512]{1,0:T(8,128)(2,1)}, bf16[768,512]{1,0:T(8,128)(2,1)S(1)}, u32[]{:S(2)}, u32[]{:S(2)}) collective-permute-start(bf16[768,512]{1,0:T(8,128)(2,1)} %get-tuple-element.50), channel_id=1, source_target_pairs={{0,3},{1,2},{2,11},{3,10},{4,7},{5,6},{6,15},{7,14},{8,1},{9,0},{1... | collective-permute-start | bytes 2359304 | tf_op jit(solution)/shard_map/ppermute | solution.py:29
  134.0 34.1 %collective-permute-start.18 = (bf16[768,512]{1,0:T(8,128)(2,1)}, bf16[768,512]{1,0:T(8,128)(2,1)S(1)}, u32[]{:S(2)}, u32[]{:S(2)}) collective-permute-start(bf16[768,512]{1,0:T(8,128)(2,1)} %get-tuple-element.55), channel_id=1, source_target_pairs={{0,10},{1,11},{2,2},{3,3},{4,14},{5,15},{6,6},{7,7},{8,8},{9,9},{1... | collective-permute-start | bytes 2359304 | tf_op jit(solution)/shard_map/ppermute | solution.py:29
  137.7 36.9 %collective-permute-start.19 = (bf16[768,512]{1,0:T(8,128)(2,1)}, bf16[768,512]{1,0:T(8,128)(2,1)}, u32[]{:S(2)}, u32[]{:S(2)}) collective-permute-start(bf16[768,512]{1,0:T(8,128)(2,1)} %get-tuple-element.56), channel_id=1, source_target_pairs={{0,11},{1,10},{2,3},{3,2},{4,15},{5,14},{6,7},{7,6},{8,9},{9,8},{1... | collective-permute-start | bytes 2359304 | tf_op jit(solution)/shard_map/ppermute | solution.py:29
  140.2 34.4 %copy-start.1 = (bf16[24,128,128]{2,1,0:T(8,128)(2,1)S(1)}, bf16[24,128,128]{2,1,0:T(8,128)(2,1)}, u32[]{:S(2)}) copy-start(bf16[24,128,128]{2,1,0:T(8,128)(2,1)} %sign_table.1.table_ref) | copy-start | bytes 2359300

commit v3 on v2

v3 whole, which is shorter than its diff:
```python
import functools

import jax
import jax.numpy as jnp
from jax import lax
from jax.experimental import pallas as pl
from jax.experimental.pallas import tpu as pltpu
from jax.sharding import Mesh
from jax.sharding import PartitionSpec as P

HB = 128
FP8_LIMIT = 448.0
LONG = 100_000_000_000
AXES = ("section", "chip", "core", "tensor")
VMEM = pl.BlockSpec(memory_space=pltpu.VMEM)
SMEM = pl.BlockSpec(memory_space=pltpu.SMEM)


def send(shard, place):
    sections, chips, cores, tensors = (lax.axis_size(axis) for axis in AXES)
    dps = chips * cores
    pairs = []
    for s in range(sections):
        for d in range(dps):
            for t in range(tensors):
                to_s, to_d, to_t = place(s, d, t)
                if 0 <= to_s < sections:
                    pairs.append(((s * dps + d) * tensors + t, (to_s * dps + to_d) * tensors + to_t % tensors))
    return lax.ppermute(shard, AXES, pairs)


def other_core(shard):
    return send(shard, lambda s, d, t: (s, d ^ 1, t))


def other_chip(shard):
    return send(shard, lambda s, d, t: (s, d ^ 2, t))


def signs_kernel(table_ref):
    order = table_ref.shape[0]
    both = lax.broadcasted_iota(jnp.int32, (order, order), 0) & lax.broadcasted_iota(jnp.int32, (order, order), 1)
    odd = jnp.zeros_like(both)
    for bit in range(order.bit_length() - 1):
        odd = odd ^ (both >> bit & 1)
    table_ref[...] = (1 - 2 * odd).astype(jnp.float32)


def hadamard_signs(order):
    return pl.pallas_call(
        signs_kernel,
        out_shape=jax.ShapeDtypeStruct((order, order), jnp.float32),
        out_specs=VMEM,
        cost_estimate=pl.CostEstimate(flops=LONG, bytes_accessed=0, transcendentals=0),
        name="hadamard_signs",
    )()


def after(value, *others):
    return lax.optimization_barrier((value, *others))[0]


def rotated_rows(pair, rest, table_ref, grads_refs, swapped, far):
    held_ref, a_ref, b_ref = grads_refs
    rows, tokens = pair.shape[0] // 2, held_ref.shape[0] // 2
    at = slice(far * tokens, (far + 1) * tokens)
    first, second = slice(0, rows), slice(rows, 2 * rows)
    total = None
    for weight, grads in (
        (rest[first, :], held_ref[at, :]),
        (pair[second if swapped else first, :], a_ref[at, :]),
        (pair[first if swapped else second, :], b_ref[0, at, :]),
        (rest[second, :], b_ref[1, at, :]),
    ):
        term = lax.dot_general(weight, grads, (((1,), (1,)), ((), ())), preferred_element_type=jnp.float32)
        total = term if total is None else total + term
    high = total.astype(jnp.bfloat16)
    low = (total - high.astype(jnp.float32)).astype(jnp.bfloat16)
    turned = []
    for b in range(rows // HB):
        both = jnp.concatenate([high[b * HB : (b + 1) * HB], low[b * HB : (b + 1) * HB]], axis=0)
        turned.append((jnp.dot(table_ref[b], both, preferred_element_type=jnp.float32) * HB**-0.5).astype(jnp.bfloat16))
    return jnp.concatenate(turned, axis=0)


def rotate_kernel(base_ref, table_ref, *refs):
    base = base_ref[0]
    given, outs, inside, made, come, gone = refs[:7], refs[7:11], refs[11:18], refs[18], refs[19], refs[20]
    fetches = [pltpu.make_async_copy(far, near, come.at[i]) for i, (far, near) in enumerate(zip(given, inside))]
    for fetch in fetches:
        fetch.start()
    grads, weights = inside[:3], inside[3:]

    def sends(k):
        for r, out_ref in enumerate(outs):
            yield jnp.bitwise_xor(base, k) == r, pltpu.make_async_copy(made.at[k], out_ref, gone.at[k])

    for step, k in enumerate((0, 2, 1, 3)):
        for fetch in {0: fetches[:5], 2: fetches[5:]}.get(step, ()):
            fetch.wait()
        done = rotated_rows(*weights[k % 2 * 2 : k % 2 * 2 + 2], table_ref.at[k % 2], grads, k % 2, k // 2)
        made[k] = done
        for here, copy in sends(k):
            pl.when(here)(copy.start)
    for k in range(4):
        for here, copy in sends(k):
            pl.when(here)(copy.wait)


def rotate(base, weights, table, grads):
    rows, tokens = weights[0].shape[0] // 2, grads[0].shape[0] // 2
    given = (*grads, *weights)
    return pl.pallas_call(
        rotate_kernel,
        out_shape=[jax.ShapeDtypeStruct((rows, tokens), jnp.bfloat16)] * 4,
        in_specs=[SMEM, VMEM] + [pl.BlockSpec(memory_space=pl.ANY)] * 7,
        out_specs=[pl.BlockSpec(memory_space=pl.ANY)] * 4,
        scratch_shapes=[pltpu.VMEM(array.shape, array.dtype) for array in given]
        + [pltpu.VMEM((4, rows, tokens), jnp.bfloat16)]
        + [pltpu.SemaphoreType.DMA((7,)), pltpu.SemaphoreType.DMA((4,))],
        compiler_params=pltpu.CompilerParams(vmem_limit_bytes=40 * 1024 * 1024),
        cost_estimate=pl.CostEstimate(flops=0, bytes_accessed=0, transcendentals=0),
        name="rotate",
    )(base, table, *given)


def back_kernel(rounds, here_ref, *refs):
    pieces, (limit_ref, table_ref), (out_ref, made, gone) = refs[: len(rounds)], refs[len(rounds) :][:2], refs[-3:]
    rows = made.shape[1]
    blocks = rows // HB
    copies = []
    for i, (r, piece) in enumerate(zip(rounds, pieces)):
        quarter = jnp.bitwise_xor(here_ref[0], r)
        for b in range(blocks):
            limit = limit_ref[quarter * blocks + b]
            at = slice(b * HB, (b + 1) * HB)
            values = jnp.clip(piece[at, :].astype(jnp.float32), -limit, limit).astype(jnp.bfloat16)
            turned = jnp.dot(table_ref[quarter * blocks + b], values, preferred_element_type=jnp.float32)
            made[i, at, :] = (turned * HB**-0.5).astype(jnp.bfloat16)
        place = pl.ds(pl.multiple_of(quarter * rows, rows), rows)
        copies.append(pltpu.make_async_copy(made.at[i], out_ref.at[place, :], gone.at[i]))
        copies[-1].start()
    for copy in copies:
        copy.wait()


def back(here, pieces, rounds, limit, table, *out):
    rows, tokens = pieces[0].shape
    anywhere = pl.BlockSpec(memory_space=pl.ANY)
    operands = (here, *pieces, limit, table, *out)
    return pl.pallas_call(
        functools.partial(back_kernel, rounds),
        out_shape=jax.ShapeDtypeStruct((4 * rows, tokens), jnp.bfloat16),
        in_specs=[SMEM] + [VMEM] * (len(pieces) + 2) + [anywhere] * len(out),
        out_specs=anywhere,
        scratch_shapes=[pltpu.VMEM((len(rounds), rows, tokens), jnp.bfloat16), pltpu.SemaphoreType.DMA((len(rounds),))],
        input_output_aliases={len(operands) - 1: 0} if out else {},
        compiler_params=pltpu.CompilerParams(vmem_limit_bytes=40 * 1024 * 1024),
        cost_estimate=pl.CostEstimate(flops=0, bytes_accessed=0, transcendentals=0),
        name="rotate_back",
    )(*operands)


def product_kernel(block_ref, inputs_ref, got_ref, grads_ref, other_ref, *rest):
    arrived, (out_ref, held, done) = rest[:-3], rest[-3:]
    tile = held.shape[2]
    tiles = got_ref.shape[1] // tile
    sum_rows = (((0,), (0,)), ((), ()))
    start = block_ref[0] * tiles

    def fetch(i):
        at = pl.ds(pl.multiple_of((start + i) * tile, tile), tile)
        return pltpu.make_async_copy(inputs_ref.at[:, at], held.at[i % 2], done.at[i % 2])

    fetch(0).start()
    for i in range(tiles):
        if i + 1 < tiles:
            fetch(i + 1).start()
        fetch(i).wait()
        at = slice(i * tile, (i + 1) * tile)
        total = lax.dot_general(held[i % 2], grads_ref[...], sum_rows, preferred_element_type=jnp.float32)
        total += lax.dot_general(got_ref[:, at], other_ref[...], sum_rows, preferred_element_type=jnp.float32)
        for piece in arrived:
            total += piece[at, :].astype(jnp.float32)
        out_ref[at, :] = total.astype(out_ref.dtype)


def product(inputs, block, got, grads, other, dtype, *arrived):
    tokens, columns = grads.shape
    rows = got.shape[1]
    return pl.pallas_call(
        product_kernel,
        out_shape=jax.ShapeDtypeStruct((rows, columns), dtype),
        in_specs=[SMEM, pl.BlockSpec(memory_space=pltpu.HBM)] + [VMEM] * (3 + len(arrived)),
        out_specs=VMEM,
        scratch_shapes=[pltpu.VMEM((2, tokens, rows // 4), inputs.dtype), pltpu.SemaphoreType.DMA((2,))],
        compiler_params=pltpu.CompilerParams(vmem_limit_bytes=40 * 1024 * 1024),
        cost_estimate=pl.CostEstimate(flops=0, bytes_accessed=0, transcendentals=0),
        name="weight_product",
    )(block, inputs, got, grads, other, *arrived)


def body(earlier_inputs, earlier_grads, current_grads, key_value_weight, exponents, sign_bits):
    chip, core, tensor = (lax.axis_index(axis) for axis in AXES[1:])
    dp = chip * lax.axis_size("core") + core
    parts = lax.axis_size("tensor")
    inputs_local, grads_before, weight_local = earlier_inputs[0], earlier_grads[0], key_value_weight[0]
    rows_here = weight_local.shape[0]
    quarter = rows_here // parts

    def scalar(value):
        return jnp.reshape(value, (1,)).astype(jnp.int32)

    def features(inputs, block):
        return lax.dynamic_slice_in_dim(inputs, block * rows_here, rows_here, 1)

    def down(shard, turn=0):
        return send(shard, lambda s, d, t: (s - 1, d ^ 2, t ^ turn))

    def over_z(shard, even, odd):
        return send(shard, lambda s, d, t: (s, d, t ^ (odd if d & 1 else even)))

    def quarter_for(weight, x):
        return lax.dynamic_slice_in_dim(weight, jnp.bitwise_xor(tensor, x) * quarter, quarter, 0)

    def signed(bits, shape):
        return plain * (2 * bits - 1).astype(jnp.float32).reshape(shape)

    tokens, columns = current_grads.shape[1:]
    plain = hadamard_signs(HB)
    ahead, behind = quarter_for(weight_local, 1 + 2 * core), quarter_for(weight_local, 3 - 2 * core)
    sliced = ahead
    pair = [over_z(ahead, 1, 3), over_z(behind, 3, 1)]
    limit = (FP8_LIMIT * jnp.exp2(exponents[0].astype(jnp.float32))).astype(jnp.bfloat16)
    blocks = limit.shape[0]
    limit = jnp.pad(limit, ((0, -blocks % 16), (0, 0)))
    grads_far = down(jnp.concatenate([current_grads[0], limit], axis=0))

    inputs_then = after(inputs_local, sliced)
    grads_other = other_core(grads_before)
    got_far = other_core(features(inputs_then, jnp.bitwise_xor(dp, 3)))
    weight_then = after(weight_local, got_far)
    here, opposite = quarter_for(weight_then, 0), quarter_for(weight_then, 2)
    partial = product(
        inputs_local, scalar(jnp.bitwise_xor(dp, 2)), got_far, grads_before, grads_other, jnp.bfloat16
    )
    grads_far, partial, here, opposite, *pair = lax.optimization_barrier(
        (grads_far, partial, here, opposite, *pair)
    )

    grads_near = other_chip(grads_far)
    pair = down(jnp.concatenate(pair, axis=0))
    opposite = over_z(opposite, 2, 2)
    arrived = other_chip(after(partial, grads_near))
    bits = lax.dynamic_slice_in_dim(sign_bits, dp * quarter, quarter, 0)
    bits = send(bits, lambda s, d, t: (s, t ^ 2, d))
    rest = down(after(jnp.concatenate([here, opposite], axis=0), grads_near))
    got_near = features(after(inputs_local, grads_far), jnp.bitwise_xor(dp, 1))
    grads_near, plain, bits, got_near = lax.optimization_barrier((grads_near, plain, bits, got_near))

    limit = grads_near[tokens : tokens + blocks]
    held = jnp.concatenate([grads_near[:tokens], grads_far[:tokens]], axis=0)
    got_near = other_core(got_near)
    step_a = over_z(held, 1, 3)
    step_a, pair, bits_other = lax.optimization_barrier((step_a, pair, other_core(bits)))
    step_b = over_z(jnp.stack([held, step_a]), 3, 1)
    weights = (pair, rest, other_core(pair), other_core(rest))
    step_b, got_near, *weights = lax.optimization_barrier((step_b, got_near, *weights))

    signs_there = jnp.concatenate([bits, bits_other]).reshape(2, -1, 1, HB)
    table = signed(signs_there, signs_there.shape).astype(jnp.bfloat16)
    table = jnp.concatenate([table, table], axis=3)
    turned = rotate(scalar(jnp.bitwise_xor(dp, tensor)), weights, table, (held, step_a, step_b))
    arrived, *later = lax.optimization_barrier((arrived, *turned[2:]))
    turned = [*turned[:2], *later]

    pieces = [
        send(turned[r], lambda s, d, t, r=r: (s, (t ^ r) & 2 | d & 1, (d & 2 ^ 2) | (t ^ r) & 1)) for r in range(parts)
    ]
    limit = limit.astype(jnp.float32)[:, None, :]
    weight_grad = product(
        inputs_local, scalar(dp), got_near, grads_before, grads_other, jnp.float32, arrived
    )
    place = scalar(chip * 2 + jnp.bitwise_and(tensor, 1))
    table = signed(sign_bits, (-1, HB, 1)).astype(jnp.bfloat16)
    upstream_grad = back(place, pieces[:2], (0, 1), limit, table)
    upstream_grad = back(place, pieces[2:], (2, 3), limit, table, upstream_grad)
    return (upstream_grad[None], weight_grad[None])


def solution(mesh):
    sections, dps, tensors = (mesh.shape[axis] for axis in ("section", "dp", "tensor"))
    split = Mesh(mesh.devices.reshape(sections, dps // 2, 2, tensors), AXES)
    dp = ("chip", "core")
    placed = (
        P("section", dp, None),
        P("section", dp, "tensor"),
        P("section", dp, "tensor"),
        P("section", dp, "tensor"),
        P("section", "tensor", dp),
        P("tensor"),
    )
    return jax.shard_map(
        body,
        mesh=split,
        in_specs=placed,
        out_specs=(P("section", "tensor", dp), P("section", dp, "tensor")),
        check_vma=False,
    )
```

time: 179 us -> 171 us (0.955)
  Pallas kernels: 43.5 us -> 34.7 us
  waiting for transfers between devices: 86.9 us -> 80 us
  starting transfers between devices: 29.7 us -> 34.2 us
  other arithmetic: 4.94 us -> 7.27 us
    ppermute x20 -> x21, waiting for transfers between devices: 86.9 us -> 80 us  [send(): return lax.ppermute(shard, AXES, pairs)]
    pallas_call x4, Pallas kernels: 28.8 us -> 22.5 us  [the longest x2 19.3 us: product(): pl.pallas_call(product_kernel, out_shape=jax.ShapeDtypeStruct((rows, colu...]
    ppermute x20 -> x21, starting transfers between devices: 29.7 us -> 34.2 us  [send(): return lax.ppermute(shard, AXES, pairs)]
    pallas_call x1, Pallas kernels: 14 us -> 11.5 us  [rotate(): pl.pallas_call(rotate_kernel, out_shape=[jax.ShapeDtypeStruct((rows, toke...]
    concatenate x1, other arithmetic: 0.04 us -> 1.89 us  [body(): grads_far = down(jnp.concatenate([current_grads[0], limit], axis=0))]
  transfers between devices with their start and end apart: 20 -> 21, of which waited for: 9 -> 10; matrix products, arithmetic and copies ran while one was open for 5% -> 9% of each run, Pallas kernels for 22% -> 20%
where the time goes in v3:
time: 171 us; the launch traced here: 169 us
  waiting for transfers between devices  80 us (47%)
  Pallas kernels  34.7 us (20%)
  starting transfers between devices  34.2 us (20%)
  local copies, waits for them, and re-layouts  12.1 us (7%)
  other arithmetic  7.27 us (4%)
    ppermute x21, waiting for transfers between devices, send(): return lax.ppermute(shard, AXES, pairs)  80 us
    ppermute x21, starting transfers between devices, send(): return lax.ppermute(shard, AXES, pairs)  34.2 us
    pallas_call x2, Pallas kernels, product(): pl.pallas_call(product_kernel, out_shape=jax.ShapeDtypeStruct((rows, colu...  19.3 us
    pallas_call x1, Pallas kernels, rotate(): pl.pallas_call(rotate_kernel, out_shape=[jax.ShapeDtypeStruct((rows, toke...  11.5 us
    dynamic_slice x2, local copies, waits for them, and re-layouts, features(): return lax.dynamic_slice_in_dim(inputs, block * rows_here, rows_here, 1)  7.52 us
  transfers between devices with their start and end apart: 21, of which 10 were waited for; matrix products, arithmetic and copies ran while one was open for 9% of the time, Pallas kernels for 20%

profile of v3, /device:TPU:20, one launch (start us, length us, event | category | flops | bytes accessed | tf_op | source)
XLA Modules:
  0.0 169.2 jit_solution(1990283166486441361)
XLA Ops:
  0.6 0.8 fusion.2
  1.4 1.9 %fusion.1 = bf16[544,512]{1,0:T(8,128)(2,1)} fusion(bf16[24,512]{1,0:T(8,128)(2,1)S(1)} %fusion.2, bf16[512,512]{1,0:T(8,128)(2,1)} %bitcast.31), kind=kLoop, calls=%fused_computation.11 | loop fusion | flops 1671168 | bytes 1105920 | tf_op jit(solution)/shard_map/concatenate | solution.py:237
  3.3 2.4 %collective-permute-start = (bf16[544,512]{1,0:T(8,128)(2,1)}, bf16[544,512]{1,0:T(8,128)(2,1)}, u32[]{:S(2)}, u32[]{:S(2)}) collective-permute-start(bf16[544,512]{1,0:T(8,128)(2,1)} %fusion.1), channel_id=1, source_target_pairs={{16,8},{17,9},{18,10},{19,11},{20,12},{21,13},{22,14},{23,15},{24,... | collective-permute-start | bytes 1671176 | tf_op jit(solution)/shard_map/ppermute | solution.py:29
  5.8 2.6 %dynamic-slice_bitcast_fusion = (bf16[768,512]{1,0:T(8,128)(2,1)}, bf16[768,512]{1,0:T(8,128)(2,1)}) fusion(bf16[1,3072,512]{2,1,0:T(8,128)(2,1)} %param.9, s32[]{:T(128)S(6)} %select_n.25, s32[]{:T(128)S(6)} %select_n.21), kind=kLoop, calls=%fused_computation.9 | loop fusion | bytes 3145736 | tf_op jit(solution)/shard_map/dynamic_slice | solution.py:224
  8.4 1.9 %collective-permute-start.3 = (bf16[768,512]{1,0:T(8,128)(2,1)}, bf16[768,512]{1,0:T(8,128)(2,1)}, u32[]{:S(2)}, u32[]{:S(2)}) collective-permute-start(bf16[768,512]{1,0:T(8,128)(2,1)} %get-tuple-element.65), channel_id=1, source_target_pairs={{0,1},{1,0},{2,3},{3,2},{4,7},{5,6},{6,5},{7,4},{8,9},{9,8},{10,11... | collective-permute-start | bytes 2359304 | tf_op jit(solution)/shard_map/ppermute | solution.py:29
  10.3 3.8 %constant_dynamic-slice_fusion.3 = bf16[512,3072]{1,0:T(8,128)(2,1)} fusion(bf16[512,12288]{1,0:T(8,128)(2,1)} %bitcast.24, s32[]{:T(128)S(6)} %select_n.22), kind=kLoop, calls=%fused_computation.22 | loop fusion | bytes 6291460 | tf_op jit(solution)/shard_map/dynamic_slice | solution.py:215
  14.1 1.4 collective-permute-start.1
  15.5 1.6 collective-permute-start.4
  17.1 0.7 hadamard_signs.1
  17.8 0.1 dynamic_slice.32
  17.9 3.9 %collective-permute-done.1.got_ref = bf16[512,3072]{1,0:T(8,128)(2,1)S(1)} collective-permute-done((bf16[512,3072]{1,0:T(8,128)(2,1)}, bf16[512,3072]{1,0:T(8,128)(2,1)S(1)}, u32[]{:S(2)}, u32[]{:S(2)}) %collective-permute-start.1) | collective-permute-done | bytes 3145760 | tf_op jit(solution)/shard_map/ppermute | solution.py:29
  21.7 1.1 collective-permute-start.7
  22.9 8.2 %weight_product.2 = bf16[3072,512]{1,0:T(8,128)(2,1)} custom-call(s32[1]{0:T(128)} %bitcast.3.block_ref, bf16[512,12288]{1,0:T(8,128)(2,1)} %bitcast.25, bf16[512,3072]{1,0:T(8,128)(2,1)S(1)} %collective-permute-done.1.got_ref, bf16[512,512]{1,0:T(8,128)(2,1)} %bitcast.6.grads_ref, bf16[512,512]{1,0:T(8,128)(2,1)} %collective-permute-done.2.other_ref), custom_call_target="tpu_custom_call" | custom-call | tf_op jit(solution)/shard_map/weight_product/pallas_call | solution.py:191
  31.1 0.1 constant_dynamic-slice_fusion.1
  31.3 2.6 %collective-permute-start.5 = (bf16[544,512]{1,0:T(8,128)(2,1)}, bf16[544,512]{1,0:T(8,128)(2,1)S(1)}, u32[]{:S(2)}, u32[]{:S(2)}) collective-permute-start(bf16[544,512]{1,0:T(8,128)(2,1)} %collective-permute-done), channel_id=1, source_target_pairs={{0,8},{1,9},{2,10},{3,11},{4,12},{5,13},{6,14},{7,15},{8,0},{9,1},... | collective-permute-start | bytes 1671176 | tf_op jit(solution)/shard_map/ppermute | solution.py:29
  33.9 0.9 collective-permute-start.13
  34.8 1.5 pad_maximum_fusion.1
  36.3 4.0 %collective-permute-start.9 = (bf16[1536,512]{1,0:T(8,128)(2,1)S(1)}, bf16[1536,512]{1,0:T(8,128)(2,1)}, u32[]{:S(2)}, u32[]{:S(2)}) collective-permute-start(bf16[1536,512]{1,0:T(8,128)(2,1)S(1)} %pad_maximum_fusion.1), channel_id=1, source_target_pairs={{16,8},{17,9},{18,10},{19,11},{20,12},{21,13},{22,14},{23,15},{24,... | collective-permute-start | bytes 4718600 | tf_op jit(solution)/shard_map/ppermute | solution.py:29
  40.3 3.8 %constant_dynamic-slice_fusion = bf16[512,3072]{1,0:T(8,128)(2,1)} fusion(bf16[512,12288]{1,0:T(8,128)(2,1)} %bitcast.26, s32[]{:T(128)S(6)} %select_n.27), kind=kLoop, calls=%fused_computation.19 | loop fusion | bytes 6291460 | tf_op jit(solution)/shard_map/dynamic_slice | solution.py:215
  44.1 1.1 slice.10
  45.2 0.8 collective-permute-done.5
  46.0 0.1 fusion.5
  46.2 0.6 copy-done.1
  46.8 0.6 collective-permute-start.8
  47.4 0.5 collective-permute-start.12
  47.9 5.8 %collective-permute-done.13 = bf16[768,512]{1,0:T(8,128)(2,1)S(1)} collective-permute-done((bf16[768,512]{1,0:T(8,128)(2,1)S(1)}, bf16[768,512]{1,0:T(8,128)(2,1)S(1)}, u32[]{:S(2)}, u32[]{:S(2)}) %collective-permute-start.13) | collective-permute-done | bytes 786464 | tf_op jit(solution)/shard_map/ppermute | solution.py:29
  53.7 0.1 pad_maximum_fusion.2
  53.9 2.7 %collective-permute-start.14 = (bf16[1536,512]{1,0:T(8,128)(2,1)S(1)}, bf16[1536,512]{1,0:T(8,128)(2,1)}, u32[]{:S(2)}, u32[]{:S(2)}) collective-permute-start(bf16[1536,512]{1,0:T(8,128)(2,1)S(1)} %pad_maximum_fusion.2), channel_id=1, source_target_pairs={{16,8},{17,9},{18,10},{19,11},{20,12},{21,13},{22,14},{23,15},{24,... | collective-permute-start | bytes 4718600 | tf_op jit(solution)/shard_map/ppermute | solution.py:29
  56.6 2.1 %collective-permute-start.6 = (bf16[3072,512]{1,0:T(8,128)(2,1)}, bf16[3072,512]{1,0:T(8,128)(2,1)}, u32[]{:S(2)}, u32[]{:S(2)}) collective-permute-start(bf16[3072,512]{1,0:T(8,128)(2,1)} %weight_product.2), channel_id=1, source_target_pairs={{0,8},{1,9},{2,10},{3,11},{4,12},{5,13},{6,14},{7,15},{8,0},{9,1},... | collective-permute-start | bytes 9437192 | tf_op jit(solution)/shard_map/ppermute | solution.py:29
  58.7 18.0 %collective-permute-done.9.refs_3_ = bf16[1536,512]{1,0:T(8,128)(2,1)} collective-permute-done((bf16[1536,512]{1,0:T(8,128)(2,1)S(1)}, bf16[1536,512]{1,0:T(8,128)(2,1)}, u32[]{:S(2)}, u32[]{:S(2)}) %collective-permute-start.9) | collective-permute-done | bytes 1572896 | tf_op jit(solution)/shard_map/ppermute | solution.py:29
  76.8 1.5 pad_maximum_fusion
  78.2 1.3 collective-permute-start.11
  79.5 29.1 %collective-permute-done.14.refs_4_ = bf16[1536,512]{1,0:T(8,128)(2,1)} collective-permute-done((bf16[1536,512]{1,0:T(8,128)(2,1)S(1)}, bf16[1536,512]{1,0:T(8,128)(2,1)}, u32[]{:S(2)}, u32[]{:S(2)}) %collective-permute-start.14) | collective-permute-done | bytes 1572896 | tf_op jit(solution)/shard_map/ppermute | solution.py:29
  108.6 0.1 multiply_convert_fusion.1
  108.8 3.6 %collective-permute-done.16.refs_6_ = bf16[1536,512]{1,0:T(8,128)(2,1)} collective-permute-done((bf16[1536,512]{1,0:T(8,128)(2,1)}, bf16[1536,512]{1,0:T(8,128)(2,1)}, u32[]{:S(2)}, u32[]{:S(2)}) %collective-permute-start.16) | collective-permute-done | bytes 1572896 | tf_op jit(solution)/shard_map/ppermute | solution.py:29
  112.3 11.5 %rotate.1 = (bf16[768,512]{1,0:T(8,128)(2,1)}, bf16[768,512]{1,0:T(8,128)(2,1)}, bf16[768,512]{1,0:T(8,128)(2,1)}, bf16[768,512]{1,0:T(8,128)(2,1)}) custom-call(s32[1]{0:T(128)} %bitcast.9.base_ref, bf16[2,6,128,256]{3,2,1,0:T(8,128)(2,1)S(1)} %pad_maximum_fusion.4.table_ref, bf16[1024,512]{1,0:T(8,128)(2,1)S(1)} %get-tuple-element.69.refs_0_, ...), custom_call_target="tpu_custom_call" | custom-call | tf_op jit(solution)/shard_map/rotate/pallas_call | solution.py:113
  123.8 1.2 collective-permute-done.6.rest_0_
  125.0 3.6 %collective-permute-start.19 = (bf16[768,512]{1,0:T(8,128)(2,1)}, bf16[768,512]{1,0:T(8,128)(2,1)S(1)}, u32[]{:S(2)}, u32[]{:S(2)}) collective-permute-start(bf16[768,512]{1,0:T(8,128)(2,1)} %get-tuple-element.60), channel_id=1, source_target_pairs={{0,2},{1,3},{2,10},{3,11},{4,6},{5,7},{6,14},{7,15},{8,0},{9,1},{1... | collective-permute-start | bytes 2359304 | tf_op jit(solution)/shard_map/ppermute | solution.py:29
  128.6 3.3 %collective-permute-start.17 = (bf16[768,512]{1,0:T(8,128)(2,1)}, bf16[768,512]{1,0:T(8,128)(2,1)S(1)}, u32[]{:S(2)}, u32[]{:S(2)}) collective-permute-start(bf16[768,512]{1,0:T(8,128)(2,1)} %get-tuple-element.58), channel_id=1, source_target_pairs={{0,10},{1,11},{2,2},{3,3},{4,14},{5,15},{6,6},{7,7},{8,8},{9,9},{1... | collective-permute-start | bytes 2359304 | tf_op jit(solution)/shard_map/ppermute | solution.py:29
  131.9 3.9 %collective-permute-start.18 = (bf16[768,512]{1,0:T(8,128)(2,1)}, bf16[768,512]{1,0:T(8,128)(2,1)S(1)}, u32[]{:S(2)}, u32[]{:S(2)}) collective-permute-start(bf16[768,512]{1,0:T(8,128)(2,1)} %get-tuple-element.59), channel_id=1, source_target_pairs={{0,11},{1,10},{2,3},{3,2},{4,15},{5,14},{6,7},{7,6},{8,9},{9,8},{1... | collective-permute-start | bytes 2359304 | tf_op jit(solution)/shard_map/ppermute | solution.py:29
  135.8 0.7 slice_convert_fusion
  136.6 0.5 multiply_convert_fusion.refs_3_
  137.1 11.1 %weight_product.3 = f32[3072,512]{1,0:T(8,128)} custom-call(s32[1]{0:T(128)} %bitcast.16.block_ref, bf16[512,12288]{1,0:T(8,128)(2,1)} %bitcast.27, bf16[512,3072]{1,0:T(8,128)(2,1)} %collective-permute-done.12.got_ref, bf16[512,512]{1,0:T(8,128)(2,1)} %bitcast.6.grads_ref, bf16[512,512]{1,0:T(8,128)(2,1)} %collective-permute-done.2.other_ref, ...), custom_call_target="tpu_custom_call" | custom-call | tf_op jit(solution)/shard_map/weight_product/pallas_call | solution.py:191
  148.2 12.5 %collective-permute-done.19.refs_0_ = bf16[768,512]{1,0:T(8,128)(2,1)S(1)} collective-permute-done((bf16[768,512]{1,0:T(8,128)(2,1)}, bf16[768,512]{1,0:T(8,128)(2,1)S(1)}, u32[]{:S(2)}, u32[]{:S(2)}) %collective-permute-start.19) | collective-permute-done | bytes 786464 | tf_op jit(solution)/shard_map/ppermute | solution.py:29
  160.7 0.2 collective-permute-done.20.refs_1_
  160.8 1.6 rotate_back.2.refs_4_
  162.5 5.0 %collective-permute-done.18.refs_1_ = bf16[768,512]{1,0:T(8,128)(2,1)S(1)} collective-permute-done((bf16[768,512]{1,0:T(8,128)(2,1)}, bf16[768,512]{1,0:T(8,128)(2,1)S(1)}, u32[]{:S(2)}, u32[]{:S(2)}) %collective-permute-start.18) | collective-permute-done | bytes 786464 | tf_op jit(solution)/shard_map/ppermute | solution.py:29
  167.5 1.6 rotate_back.3
  (28 shorter events, 0.2 us)
Async XLA Ops:
  3.3 27.9 %collective-permute-start = (bf16[544,512]{1,0:T(8,128)(2,1)}, bf16[544,512]{1,0:T(8,128)(2,1)}, u32[]{:S(2)}, u32[]{:S(2)}) collective-permute-start(bf16[544,512]{1,0:T(8,128)(2,1)} %fusion.1), channel_id=1, source_target_pairs={{16,8},{17,9},{18,10},{19,11},{20,12},{21,13},{22,14},{23,15},{24,... | collective-permute-start | bytes 1671176 | tf_op jit(solution)/shard_map/ppermute | solution.py:29
  8.4 22.8 %collective-permute-start.3 = (bf16[768,512]{1,0:T(8,128)(2,1)}, bf16[768,512]{1,0:T(8,128)(2,1)}, u32[]{:S(2)}, u32[]{:S(2)}) collective-permute-start(bf16[768,512]{1,0:T(8,128)(2,1)} %get-tuple-element.65), channel_id=1, source_target_pairs={{0,1},{1,0},{2,3},{3,2},{4,7},{5,6},{6,5},{7,4},{8,9},{9,8},{10,11... | collective-permute-start | bytes 2359304 | tf_op jit(solution)/shard_map/ppermute | solution.py:29
  14.1 7.6 %collective-permute-start.1 = (bf16[512,3072]{1,0:T(8,128)(2,1)}, bf16[512,3072]{1,0:T(8,128)(2,1)S(1)}, u32[]{:S(2)}, u32[]{:S(2)}) collective-permute-start(bf16[512,3072]{1,0:T(8,128)(2,1)} %constant_dynamic-slice_fusion.3), channel_id=1, source_target_pairs={{0,4},{1,5},{2,6},{3,7},{4,0},{5,1},{6,2},{7,3},{8,12},{9,13},{10,... | collective-permute-start | bytes 9437192 | tf_op jit(solution)/shard_map/ppermute | solution.py:29
  15.5 7.4 %collective-permute-start.2 = (bf16[512,512]{1,0:T(8,128)(2,1)}, bf16[512,512]{1,0:T(8,128)(2,1)}, u32[]{:S(2)}, u32[]{:S(2)}) collective-permute-start(bf16[512,512]{1,0:T(8,128)(2,1)} %bitcast.6.grads_ref), channel_id=1, source_target_pairs={{0,4},{1,5},{2,6},{3,7},{4,0},{5,1},{6,2},{7,3},{8,12},{9,13},{10,... | collective-permute-start | bytes 1572872 | tf_op jit(solution)/shard_map/ppermute | solution.py:29
  15.5 2.3 %copy-start.3 = (s32[3072]{0:T(1024)S(1)}, s32[3072]{0:T(1024)}, u32[]{:S(2)}) copy-start(s32[3072]{0:T(1024)} %param.11) | copy-start | bytes 36868
  15.5 15.8 %collective-permute-start.4 = (bf16[768,512]{1,0:T(8,128)(2,1)}, bf16[768,512]{1,0:T(8,128)(2,1)}, u32[]{:S(2)}, u32[]{:S(2)}) collective-permute-start(bf16[768,512]{1,0:T(8,128)(2,1)} %get-tuple-element.64), channel_id=1, source_target_pairs={{0,3},{1,2},{2,1},{3,0},{4,5},{5,4},{6,7},{7,6},{8,11},{9,10},{10,... | collective-permute-start | bytes 2359304 | tf_op jit(solution)/shard_map/ppermute | solution.py:29
  21.7 23.4 %collective-permute-start.7 = (s32[768]{0:T(1024)S(1)}, s32[768]{0:T(1024)S(1)}, u32[]{:S(2)}, u32[]{:S(2)}) collective-permute-start(s32[768]{0:T(1024)S(1)} %dynamic_slice.32), channel_id=1, source_target_pairs={{0,8},{1,12},{2,0},{3,4},{4,9},{5,13},{6,1},{7,5},{8,10},{9,14},{1... | collective-permute-start | bytes 9224 | tf_op jit(solution)/shard_map/ppermute | solution.py:29
  22.9 8.2 %copy-start = (bf16[1,3072,512]{2,1,0:T(8,128)(2,1)S(1)}, bf16[1,3072,512]{2,1,0:T(8,128)(2,1)}, u32[]{:S(2)}) copy-start(bf16[1,3072,512]{2,1,0:T(8,128)(2,1)} %param.9) | copy-start | bytes 9437188
  31.3 14.7 %collective-permute-start.5 = (bf16[544,512]{1,0:T(8,128)(2,1)}, bf16[544,512]{1,0:T(8,128)(2,1)S(1)}, u32[]{:S(2)}, u32[]{:S(2)}) collective-permute-start(bf16[544,512]{1,0:T(8,128)(2,1)} %collective-permute-done), channel_id=1, source_target_pairs={{0,8},{1,9},{2,10},{3,11},{4,12},{5,13},{6,14},{7,15},{8,0},{9,1},... | collective-permute-start | bytes 1671176 | tf_op jit(solution)/shard_map/ppermute | solution.py:29
  33.9 19.8 %collective-permute-start.13 = (bf16[768,512]{1,0:T(8,128)(2,1)S(1)}, bf16[768,512]{1,0:T(8,128)(2,1)S(1)}, u32[]{:S(2)}, u32[]{:S(2)}) collective-permute-start(bf16[768,512]{1,0:T(8,128)(2,1)S(1)} %get-tuple-element.49), channel_id=1, source_target_pairs={{0,2},{1,3},{2,0},{3,1},{4,6},{5,7},{6,4},{7,5},{8,10},{9,11},{10,... | collective-permute-start | bytes 2359304 | tf_op jit(solution)/shard_map/ppermute | solution.py:29
  36.3 40.5 %collective-permute-start.9 = (bf16[1536,512]{1,0:T(8,128)(2,1)S(1)}, bf16[1536,512]{1,0:T(8,128)(2,1)}, u32[]{:S(2)}, u32[]{:S(2)}) collective-permute-start(bf16[1536,512]{1,0:T(8,128)(2,1)S(1)} %pad_maximum_fusion.1), channel_id=1, source_target_pairs={{16,8},{17,9},{18,10},{19,11},{20,12},{21,13},{22,14},{23,15},{24,... | collective-permute-start | bytes 4718600 | tf_op jit(solution)/shard_map/ppermute | solution.py:29
  46.0 0.8 copy-start.1
  46.8 30.0 %collective-permute-start.8 = (bf16[1024,512]{1,0:T(8,128)(2,1)S(1)}, bf16[1024,512]{1,0:T(8,128)(2,1)S(1)}, u32[]{:S(2)}, u32[]{:S(2)}) collective-permute-start(bf16[1024,512]{1,0:T(8,128)(2,1)S(1)} %get-tuple-element.69.refs_0_), channel_id=1, source_target_pairs={{0,1},{1,0},{2,3},{3,2},{4,7},{5,6},{6,5},{7,4},{8,9},{9,8},{10,11... | collective-permute-start | bytes 3145736 | tf_op jit(solution)/shard_map/ppermute | solution.py:29
  47.4 9.2 %collective-permute-start.10 = (s32[768]{0:T(1024)S(1)}, s32[768]{0:T(1024)S(1)}, u32[]{:S(2)}, u32[]{:S(2)}) collective-permute-start(s32[768]{0:T(1024)S(1)} %collective-permute-done.7), channel_id=1, source_target_pairs={{0,4},{1,5},{2,6},{3,7},{4,0},{5,1},{6,2},{7,3},{8,12},{9,13},{10,... | collective-permute-start | bytes 9224 | tf_op jit(solution)/shard_map/ppermute | solution.py:29
  47.4 61.4 %collective-permute-start.12 = (bf16[512,3072]{1,0:T(8,128)(2,1)}, bf16[512,3072]{1,0:T(8,128)(2,1)}, u32[]{:S(2)}, u32[]{:S(2)}) collective-permute-start(bf16[512,3072]{1,0:T(8,128)(2,1)} %constant_dynamic-slice_fusion), channel_id=1, source_target_pairs={{0,4},{1,5},{2,6},{3,7},{4,0},{5,1},{6,2},{7,3},{8,12},{9,13},{10,... | collective-permute-start | bytes 9437192 | tf_op jit(solution)/shard_map/ppermute | solution.py:29
  53.9 54.7 %collective-permute-start.14 = (bf16[1536,512]{1,0:T(8,128)(2,1)S(1)}, bf16[1536,512]{1,0:T(8,128)(2,1)}, u32[]{:S(2)}, u32[]{:S(2)}) collective-permute-start(bf16[1536,512]{1,0:T(8,128)(2,1)S(1)} %pad_maximum_fusion.2), channel_id=1, source_target_pairs={{16,8},{17,9},{18,10},{19,11},{20,12},{21,13},{22,14},{23,15},{24,... | collective-permute-start | bytes 4718600 | tf_op jit(solution)/shard_map/ppermute | solution.py:29
  56.6 68.4 %collective-permute-start.6 = (bf16[3072,512]{1,0:T(8,128)(2,1)}, bf16[3072,512]{1,0:T(8,128)(2,1)}, u32[]{:S(2)}, u32[]{:S(2)}) collective-permute-start(bf16[3072,512]{1,0:T(8,128)(2,1)} %weight_product.2), channel_id=1, source_target_pairs={{0,8},{1,9},{2,10},{3,11},{4,12},{5,13},{6,14},{7,15},{8,0},{9,1},... | collective-permute-start | bytes 9437192 | tf_op jit(solution)/shard_map/ppermute | solution.py:29
  76.7 31.9 %copy-start.2 = (f32[128,128]{1,0:T(8,128)S(1)}, f32[128,128]{1,0:T(8,128)}, u32[]{:S(2)}) copy-start(f32[128,128]{1,0:T(8,128)} %hadamard_signs.1) | copy-start | bytes 196612
  78.2 30.5 %collective-permute-start.11 = (bf16[2,1024,512]{2,1,0:T(8,128)(2,1)}, bf16[2,1024,512]{2,1,0:T(8,128)(2,1)}, u32[]{:S(2)}, u32[]{:S(2)}) collective-permute-start(bf16[2,1024,512]{2,1,0:T(8,128)(2,1)} %pad_maximum_fusion), channel_id=1, source_target_pairs={{0,3},{1,2},{2,1},{3,0},{4,5},{5,4},{6,7},{7,6},{8,11},{9,10},{10,... | collective-permute-start | bytes 6291464 | tf_op jit(solution)/shard_map/ppermute | solution.py:29
  79.5 29.2 %collective-permute-start.15 = (bf16[1536,512]{1,0:T(8,128)(2,1)}, bf16[1536,512]{1,0:T(8,128)(2,1)}, u32[]{:S(2)}, u32[]{:S(2)}) collective-permute-start(bf16[1536,512]{1,0:T(8,128)(2,1)} %collective-permute-done.9.refs_3_), channel_id=1, source_target_pairs={{0,4},{1,5},{2,6},{3,7},{4,0},{5,1},{6,2},{7,3},{8,12},{9,13},{10,... | collective-permute-start | bytes 4718600 | tf_op jit(solution)/shard_map/ppermute | solution.py:29
  108.6 3.8 %collective-permute-start.16 = (bf16[1536,512]{1,0:T(8,128)(2,1)}, bf16[1536,512]{1,0:T(8,128)(2,1)}, u32[]{:S(2)}, u32[]{:S(2)}) collective-permute-start(bf16[1536,512]{1,0:T(8,128)(2,1)} %collective-permute-done.14.refs_4_), channel_id=1, source_target_pairs={{0,4},{1,5},{2,6},{3,7},{4,0},{5,1},{6,2},{7,3},{8,12},{9,13},{10,... | collective-permute-start | bytes 4718600 | tf_op jit(solution)/shard_map/ppermute | solution.py:29
  125.0 35.7 %collective-permute-start.19 = (bf16[768,512]{1,0:T(8,128)(2,1)}, bf16[768,512]{1,0:T(8,128)(2,1)S(1)}, u32[]{:S(2)}, u32[]{:S(2)}) collective-permute-start(bf16[768,512]{1,0:T(8,128)(2,1)} %get-tuple-element.60), channel_id=1, source_target_pairs={{0,2},{1,3},{2,10},{3,11},{4,6},{5,7},{6,14},{7,15},{8,0},{9,1},{1... | collective-permute-start | bytes 2359304 | tf_op jit(solution)/shard_map/ppermute | solution.py:29
  128.6 32.3 %collective-permute-start.20 = (bf16[768,512]{1,0:T(8,128)(2,1)}, bf16[768,512]{1,0:T(8,128)(2,1)S(1)}, u32[]{:S(2)}, u32[]{:S(2)}) collective-permute-start(bf16[768,512]{1,0:T(8,128)(2,1)} %get-tuple-element.61), channel_id=1, source_target_pairs={{0,3},{1,2},{2,11},{3,10},{4,7},{5,6},{6,15},{7,14},{8,1},{9,0},{1... | collective-permute-start | bytes 2359304 | tf_op jit(solution)/shard_map/ppermute | solution.py:29
  128.6 33.9 %collective-permute-start.17 = (bf16[768,512]{1,0:T(8,128)(2,1)}, bf16[768,512]{1,0:T(8,128)(2,1)S(1)}, u32[]{:S(2)}, u32[]{:S(2)}) collective-permute-start(bf16[768,512]{1,0:T(8,128)(2,1)} %get-tuple-element.58), channel_id=1, source_target_pairs={{0,10},{1,11},{2,2},{3,3},{4,14},{5,15},{6,6},{7,7},{8,8},{9,9},{1... | collective-permute-start | bytes 2359304 | tf_op jit(solution)/shard_map/ppermute | solution.py:29
  131.9 35.5 %collective-permute-start.18 = (bf16[768,512]{1,0:T(8,128)(2,1)}, bf16[768,512]{1,0:T(8,128)(2,1)S(1)}, u32[]{:S(2)}, u32[]{:S(2)}) collective-permute-start(bf16[768,512]{1,0:T(8,128)(2,1)} %get-tuple-element.59), channel_id=1, source_target_pairs={{0,11},{1,10},{2,3},{3,2},{4,15},{5,14},{6,7},{7,6},{8,9},{9,8},{1... | collective-permute-start | bytes 2359304 | tf_op jit(solution)/shard_map/ppermute | solution.py:29

commit v4 on v3

--- a/solution.py
+++ b/solution.py
@@ -86,7 +86,12 @@
 def rotate_kernel(base_ref, table_ref, *refs):
     base = base_ref[0]
     given, outs, inside, made, come, gone = refs[:7], refs[7:11], refs[11:18], refs[18], refs[19], refs[20]
-    fetches = [pltpu.make_async_copy(far, near, come.at[i]) for i, (far, near) in enumerate(zip(given, inside))]
+    extra = given[3].shape[0] - inside[3].shape[0]
+    moves = list(zip(given[:3], inside[:3]))
+    for pair, rest, pair_in, rest_in in ((*given[3:5], *inside[3:5]), (*given[5:], *inside[5:])):
+        held = pair_in.shape[0]
+        moves += [(pair.at[:held, :], pair_in), (pair.at[held:, :], rest_in.at[:extra, :]), (rest, rest_in.at[extra:, :])]
+    fetches = [pltpu.make_async_copy(far, near, come.at[i]) for i, (far, near) in enumerate(moves)]
     for fetch in fetches:
         fetch.start()
     grads, weights = inside[:3], inside[3:]
@@ -96,7 +101,7 @@
             yield jnp.bitwise_xor(base, k) == r, pltpu.make_async_copy(made.at[k], out_ref, gone.at[k])
 
     for step, k in enumerate((0, 2, 1, 3)):
-        for fetch in {0: fetches[:5], 2: fetches[5:]}.get(step, ()):
+        for fetch in {0: fetches[:6], 2: fetches[6:]}.get(step, ()):
             fetch.wait()
         done = rotated_rows(*weights[k % 2 * 2 : k % 2 * 2 + 2], table_ref.at[k % 2], grads, k % 2, k // 2)
         made[k] = done
@@ -108,16 +113,17 @@
 
 
 def rotate(base, weights, table, grads):
-    rows, tokens = weights[0].shape[0] // 2, grads[0].shape[0] // 2
+    rows, tokens = (weights[0].shape[0] + weights[1].shape[0]) // 4, grads[0].shape[0] // 2
     given = (*grads, *weights)
+    inside = [array.shape for array in grads] + [(2 * rows, weights[0].shape[1])] * 4
     return pl.pallas_call(
         rotate_kernel,
         out_shape=[jax.ShapeDtypeStruct((rows, tokens), jnp.bfloat16)] * 4,
         in_specs=[SMEM, VMEM] + [pl.BlockSpec(memory_space=pl.ANY)] * 7,
         out_specs=[pl.BlockSpec(memory_space=pl.ANY)] * 4,
-        scratch_shapes=[pltpu.VMEM(array.shape, array.dtype) for array in given]
+        scratch_shapes=[pltpu.VMEM(shape, jnp.bfloat16) for shape in inside]
         + [pltpu.VMEM((4, rows, tokens), jnp.bfloat16)]
-        + [pltpu.SemaphoreType.DMA((7,)), pltpu.SemaphoreType.DMA((4,))],
+        + [pltpu.SemaphoreType.DMA((9,)), pltpu.SemaphoreType.DMA((4,))],
         compiler_params=pltpu.CompilerParams(vmem_limit_bytes=40 * 1024 * 1024),
         cost_estimate=pl.CostEstimate(flops=0, bytes_accessed=0, transcendentals=0),
         name="rotate",
@@ -249,12 +255,12 @@
     )
 
     grads_near = other_chip(grads_far)
-    pair = down(jnp.concatenate(pair, axis=0))
+    pair = down(jnp.concatenate([*pair, here[:HB]], axis=0))
     opposite = over_z(opposite, 2, 2)
     arrived = other_chip(after(partial, grads_near))
     bits = lax.dynamic_slice_in_dim(sign_bits, dp * quarter, quarter, 0)
     bits = send(bits, lambda s, d, t: (s, t ^ 2, d))
-    rest = down(after(jnp.concatenate([here, opposite], axis=0), grads_near))
+    rest = down(after(jnp.concatenate([here[HB:], opposite], axis=0), grads_near))
     got_near = features(after(inputs_local, grads_far), jnp.bitwise_xor(dp, 1))
     grads_near, plain, bits, got_near = lax.optimization_barrier((grads_near, plain, bits, got_near))
 

time: 171 us -> 168 us (0.982)
  waiting for transfers between devices: 80 us -> 74.7 us
  other arithmetic: 7.27 us -> 10.2 us
    ppermute x21, waiting for transfers between devices: 80 us -> 74.7 us  [send(): return lax.ppermute(shard, AXES, pairs)]
    concatenate x2, other arithmetic: 1.57 us -> 3.92 us  [the longest x1 2.69 us: body(): pair = down(jnp.concatenate([*pair, here[:HB]], axis=0))]
  transfers between devices with their start and end apart: 21 -> 21, of which waited for: 10 -> 9; matrix products, arithmetic and copies ran while one was open for 9% -> 10% of each run, Pallas kernels for 20% -> 20%
where the time goes in v4:
time: 168 us; the launch traced here: 167 us
  waiting for transfers between devices  74.7 us (44%)
  Pallas kernels  34.3 us (20%)
  starting transfers between devices  33.8 us (20%)
  local copies, waits for them, and re-layouts  13.4 us (8%)
  other arithmetic  10.2 us (6%)
    ppermute x21, waiting for transfers between devices, send(): return lax.ppermute(shard, AXES, pairs)  74.7 us
    ppermute x21, starting transfers between devices, send(): return lax.ppermute(shard, AXES, pairs)  33.8 us
    pallas_call x2, Pallas kernels, product(): pl.pallas_call(product_kernel, out_shape=jax.ShapeDtypeStruct((rows, colu...  19.3 us
    pallas_call x1, Pallas kernels, rotate(): pl.pallas_call(rotate_kernel, out_shape=[jax.ShapeDtypeStruct((rows, toke...  11.1 us
    dynamic_slice x2, local copies, waits for them, and re-layouts, features(): return lax.dynamic_slice_in_dim(inputs, block * rows_here, rows_here, 1)  7.57 us
    dynamic_slice x2, local copies, waits for them, and re-layouts, quarter_for(): lax.dynamic_slice_in_dim(weight, jnp.bitwise_xor(tensor, x) * quarter, qu...  3.69 us
  transfers between devices with their start and end apart: 21, of which 9 were waited for; matrix products, arithmetic and copies ran while one was open for 10% of the time, Pallas kernels for 20%

profile of v4, /device:TPU:20, one launch (start us, length us, event | category | flops | bytes accessed | tf_op | source)
XLA Modules:
  0.0 167.4 jit_solution(13460363987893657771)
XLA Ops:
  0.7 2.6 %dynamic-slice_bitcast_fusion = (bf16[768,512]{1,0:T(8,128)(2,1)}, bf16[768,512]{1,0:T(8,128)(2,1)}) fusion(bf16[1,3072,512]{2,1,0:T(8,128)(2,1)} %param.9, s32[]{:T(128)S(6)} %select_n.25, s32[]{:T(128)S(6)} %select_n.21), kind=kLoop, calls=%fused_computation.9 | loop fusion | bytes 3145736 | tf_op jit(solution)/shard_map/dynamic_slice | solution.py:230
  3.3 3.8 %constant_dynamic-slice_fusion.3 = bf16[512,3072]{1,0:T(8,128)(2,1)} fusion(bf16[512,12288]{1,0:T(8,128)(2,1)} %bitcast.24, s32[]{:T(128)S(6)} %select_n.22), kind=kLoop, calls=%fused_computation.22 | loop fusion | bytes 6291460 | tf_op jit(solution)/shard_map/dynamic_slice | solution.py:221
  7.1 1.9 %collective-permute-start.3 = (bf16[768,512]{1,0:T(8,128)(2,1)}, bf16[768,512]{1,0:T(8,128)(2,1)}, u32[]{:S(2)}, u32[]{:S(2)}) collective-permute-start(bf16[768,512]{1,0:T(8,128)(2,1)} %get-tuple-element.65), channel_id=1, source_target_pairs={{0,1},{1,0},{2,3},{3,2},{4,7},{5,6},{6,5},{7,4},{8,9},{9,8},{10,11... | collective-permute-start | bytes 2359304 | tf_op jit(solution)/shard_map/ppermute | solution.py:29
  9.0 2.3 %collective-permute-start.2 = (bf16[512,512]{1,0:T(8,128)(2,1)}, bf16[512,512]{1,0:T(8,128)(2,1)}, u32[]{:S(2)}, u32[]{:S(2)}) collective-permute-start(bf16[512,512]{1,0:T(8,128)(2,1)} %bitcast.6.grads_ref), channel_id=1, source_target_pairs={{0,4},{1,5},{2,6},{3,7},{4,0},{5,1},{6,2},{7,3},{8,12},{9,13},{10,... | collective-permute-start | bytes 1572872 | tf_op jit(solution)/shard_map/ppermute | solution.py:29
  11.4 0.3 collective-permute-start.4
  11.7 0.9 fusion.1
  12.6 2.4 %collective-permute-start = (bf16[544,512]{1,0:T(8,128)(2,1)}, bf16[544,512]{1,0:T(8,128)(2,1)}, u32[]{:S(2)}, u32[]{:S(2)}) collective-permute-start(bf16[544,512]{1,0:T(8,128)(2,1)} %fusion.1), channel_id=1, source_target_pairs={{16,8},{17,9},{18,10},{19,11},{20,12},{21,13},{22,14},{23,15},{24,... | collective-permute-start | bytes 1671176 | tf_op jit(solution)/shard_map/ppermute | solution.py:29
  15.0 0.1 dynamic_slice.32
  15.1 1.2 collective-permute-start.7
  16.3 8.2 %weight_product.2 = bf16[3072,512]{1,0:T(8,128)(2,1)} custom-call(s32[1]{0:T(128)} %bitcast.3.block_ref, bf16[512,12288]{1,0:T(8,128)(2,1)} %bitcast.25, bf16[512,3072]{1,0:T(8,128)(2,1)S(1)} %collective-permute-done.1.got_ref, bf16[512,512]{1,0:T(8,128)(2,1)} %bitcast.6.grads_ref, bf16[512,512]{1,0:T(8,128)(2,1)} %collective-permute-done.2.other_ref), custom_call_target="tpu_custom_call" | custom-call | tf_op jit(solution)/shard_map/weight_product/pallas_call | solution.py:197
  24.5 1.1 constant_dynamic-slice_fusion.1
  25.6 4.3 %collective-permute-done = bf16[544,512]{1,0:T(8,128)(2,1)} collective-permute-done((bf16[544,512]{1,0:T(8,128)(2,1)}, bf16[544,512]{1,0:T(8,128)(2,1)}, u32[]{:S(2)}, u32[]{:S(2)}) %collective-permute-start) | collective-permute-done | bytes 557088 | tf_op jit(solution)/shard_map/ppermute | solution.py:29
  29.9 2.4 %collective-permute-start.5 = (bf16[544,512]{1,0:T(8,128)(2,1)}, bf16[544,512]{1,0:T(8,128)(2,1)S(1)}, u32[]{:S(2)}, u32[]{:S(2)}) collective-permute-start(bf16[544,512]{1,0:T(8,128)(2,1)} %collective-permute-done), channel_id=1, source_target_pairs={{0,8},{1,9},{2,10},{3,11},{4,12},{5,13},{6,14},{7,15},{8,0},{9,1},... | collective-permute-start | bytes 1671176 | tf_op jit(solution)/shard_map/ppermute | solution.py:29
  32.3 2.7 %pad_maximum_fusion.1 = bf16[1664,512]{1,0:T(8,128)(2,1)} fusion(bf16[128,512]{1,0:T(8,128)(2,1)S(1)} %slice.17, bf16[768,512]{1,0:T(8,128)(2,1)} %collective-permute-done.4, bf16[768,512]{1,0:T(8,128)(2,1)} %collective-permute-done.3), kind=kLoop, calls=%fused_computation.1 | loop fusion | flops 5111808 | bytes 3407872 | tf_op jit(solution)/shard_map/concatenate | solution.py:258
  35.0 1.9 %collective-permute-start.9 = (bf16[1664,512]{1,0:T(8,128)(2,1)}, bf16[1664,512]{1,0:T(8,128)(2,1)}, u32[]{:S(2)}, u32[]{:S(2)}) collective-permute-start(bf16[1664,512]{1,0:T(8,128)(2,1)} %pad_maximum_fusion.1), channel_id=1, source_target_pairs={{16,8},{17,9},{18,10},{19,11},{20,12},{21,13},{22,14},{23,15},{24,... | collective-permute-start | bytes 5111816 | tf_op jit(solution)/shard_map/ppermute | solution.py:29
  37.0 1.9 %collective-permute-start.13 = (bf16[768,512]{1,0:T(8,128)(2,1)}, bf16[768,512]{1,0:T(8,128)(2,1)}, u32[]{:S(2)}, u32[]{:S(2)}) collective-permute-start(bf16[768,512]{1,0:T(8,128)(2,1)} %get-tuple-element.49), channel_id=1, source_target_pairs={{0,2},{1,3},{2,0},{3,1},{4,6},{5,7},{6,4},{7,5},{8,10},{9,11},{10,... | collective-permute-start | bytes 2359304 | tf_op jit(solution)/shard_map/ppermute | solution.py:29
  38.9 0.7 hadamard_signs.1
  39.6 3.8 %constant_dynamic-slice_fusion = bf16[512,3072]{1,0:T(8,128)(2,1)} fusion(bf16[512,12288]{1,0:T(8,128)(2,1)} %bitcast.26, s32[]{:T(128)S(6)} %select_n.27), kind=kLoop, calls=%fused_computation.19 | loop fusion | bytes 6291460 | tf_op jit(solution)/shard_map/dynamic_slice | solution.py:221
  43.3 1.1 slice.16
  44.4 0.8 copy-done.1
  45.3 0.1 fusion.5
  45.4 2.5 %collective-permute-start.8 = (bf16[1024,512]{1,0:T(8,128)(2,1)S(1)}, bf16[1024,512]{1,0:T(8,128)(2,1)S(1)}, u32[]{:S(2)}, u32[]{:S(2)}) collective-permute-start(bf16[1024,512]{1,0:T(8,128)(2,1)S(1)} %get-tuple-element.69.refs_0_), channel_id=1, source_target_pairs={{0,1},{1,0},{2,3},{3,2},{4,7},{5,6},{6,5},{7,4},{8,9},{9,8},{10,11... | collective-permute-start | bytes 3145736 | tf_op jit(solution)/shard_map/ppermute | solution.py:29
  48.0 1.8 %collective-permute-start.6 = (bf16[3072,512]{1,0:T(8,128)(2,1)}, bf16[3072,512]{1,0:T(8,128)(2,1)}, u32[]{:S(2)}, u32[]{:S(2)}) collective-permute-start(bf16[3072,512]{1,0:T(8,128)(2,1)} %weight_product.2), channel_id=1, source_target_pairs={{0,8},{1,9},{2,10},{3,11},{4,12},{5,13},{6,14},{7,15},{8,0},{9,1},... | collective-permute-start | bytes 9437192 | tf_op jit(solution)/shard_map/ppermute | solution.py:29
  49.8 7.2 %collective-permute-done.13 = bf16[768,512]{1,0:T(8,128)(2,1)} collective-permute-done((bf16[768,512]{1,0:T(8,128)(2,1)}, bf16[768,512]{1,0:T(8,128)(2,1)}, u32[]{:S(2)}, u32[]{:S(2)}) %collective-permute-start.13) | collective-permute-done | bytes 786464 | tf_op jit(solution)/shard_map/ppermute | solution.py:29
  57.0 1.2 pad_maximum_fusion.2
  58.2 3.5 %collective-permute-start.14 = (bf16[1408,512]{1,0:T(8,128)(2,1)S(1)}, bf16[1408,512]{1,0:T(8,128)(2,1)S(1)}, u32[]{:S(2)}, u32[]{:S(2)}) collective-permute-start(bf16[1408,512]{1,0:T(8,128)(2,1)S(1)} %pad_maximum_fusion.2), channel_id=1, source_target_pairs={{16,8},{17,9},{18,10},{19,11},{20,12},{21,13},{22,14},{23,15},{24,... | collective-permute-start | bytes 4325384 | tf_op jit(solution)/shard_map/ppermute | solution.py:29
  61.8 5.7 %collective-permute-done.8.refs_1_ = bf16[1024,512]{1,0:T(8,128)(2,1)S(1)} collective-permute-done((bf16[1024,512]{1,0:T(8,128)(2,1)S(1)}, bf16[1024,512]{1,0:T(8,128)(2,1)S(1)}, u32[]{:S(2)}, u32[]{:S(2)}) %collective-permute-start.8) | collective-permute-done | bytes 1048608 | tf_op jit(solution)/shard_map/ppermute | solution.py:29
  67.5 10.8 %collective-permute-done.9.refs_3_ = bf16[1664,512]{1,0:T(8,128)(2,1)} collective-permute-done((bf16[1664,512]{1,0:T(8,128)(2,1)}, bf16[1664,512]{1,0:T(8,128)(2,1)}, u32[]{:S(2)}, u32[]{:S(2)}) %collective-permute-start.9) | collective-permute-done | bytes 1703968 | tf_op jit(solution)/shard_map/ppermute | solution.py:29
  78.3 1.6 pad_maximum_fusion
  79.8 2.0 %collective-permute-start.11 = (bf16[2,1024,512]{2,1,0:T(8,128)(2,1)}, bf16[2,1024,512]{2,1,0:T(8,128)(2,1)}, u32[]{:S(2)}, u32[]{:S(2)}) collective-permute-start(bf16[2,1024,512]{2,1,0:T(8,128)(2,1)} %pad_maximum_fusion), channel_id=1, source_target_pairs={{0,3},{1,2},{2,1},{3,0},{4,5},{5,4},{6,7},{7,6},{8,11},{9,10},{10,... | collective-permute-start | bytes 6291464 | tf_op jit(solution)/shard_map/ppermute | solution.py:29
  81.8 24.7 %collective-permute-done.14.refs_4_ = bf16[1408,512]{1,0:T(8,128)(2,1)S(1)} collective-permute-done((bf16[1408,512]{1,0:T(8,128)(2,1)S(1)}, bf16[1408,512]{1,0:T(8,128)(2,1)S(1)}, u32[]{:S(2)}, u32[]{:S(2)}) %collective-permute-start.14) | collective-permute-done | bytes 1441824 | tf_op jit(solution)/shard_map/ppermute | solution.py:29
  106.6 0.7 fusion.4
  107.3 0.9 multiply_convert_fusion.1
  108.2 0.1 pad_maximum_fusion.4.table_ref
  108.3 1.7 collective-permute-done.16.refs_6_
  110.0 11.1 %rotate.1 = (bf16[768,512]{1,0:T(8,128)(2,1)}, bf16[768,512]{1,0:T(8,128)(2,1)}, bf16[768,512]{1,0:T(8,128)(2,1)}, bf16[768,512]{1,0:T(8,128)(2,1)}) custom-call(s32[1]{0:T(128)} %bitcast.9.base_ref, bf16[2,6,128,256]{3,2,1,0:T(8,128)(2,1)S(1)} %pad_maximum_fusion.4.table_ref, bf16[1024,512]{1,0:T(8,128)(2,1)S(1)} %get-tuple-element.69.refs_0_, ...), custom_call_target="tpu_custom_call" | custom-call | tf_op jit(solution)/shard_map/rotate/pallas_call | solution.py:119
  121.1 2.3 %collective-permute-start.19 = (bf16[768,512]{1,0:T(8,128)(2,1)}, bf16[768,512]{1,0:T(8,128)(2,1)S(1)}, u32[]{:S(2)}, u32[]{:S(2)}) collective-permute-start(bf16[768,512]{1,0:T(8,128)(2,1)} %get-tuple-element.60), channel_id=1, source_target_pairs={{0,2},{1,3},{2,10},{3,11},{4,6},{5,7},{6,14},{7,15},{8,0},{9,1},{1... | collective-permute-start | bytes 2359304 | tf_op jit(solution)/shard_map/ppermute | solution.py:29
  123.4 1.8 %collective-permute-start.20 = (bf16[768,512]{1,0:T(8,128)(2,1)}, bf16[768,512]{1,0:T(8,128)(2,1)S(1)}, u32[]{:S(2)}, u32[]{:S(2)}) collective-permute-start(bf16[768,512]{1,0:T(8,128)(2,1)} %get-tuple-element.61), channel_id=1, source_target_pairs={{0,3},{1,2},{2,11},{3,10},{4,7},{5,6},{6,15},{7,14},{8,1},{9,0},{1... | collective-permute-start | bytes 2359304 | tf_op jit(solution)/shard_map/ppermute | solution.py:29
  125.1 4.1 %collective-permute-start.17 = (bf16[768,512]{1,0:T(8,128)(2,1)}, bf16[768,512]{1,0:T(8,128)(2,1)S(1)}, u32[]{:S(2)}, u32[]{:S(2)}) collective-permute-start(bf16[768,512]{1,0:T(8,128)(2,1)} %get-tuple-element.58), channel_id=1, source_target_pairs={{0,10},{1,11},{2,2},{3,3},{4,14},{5,15},{6,6},{7,7},{8,8},{9,9},{1... | collective-permute-start | bytes 2359304 | tf_op jit(solution)/shard_map/ppermute | solution.py:29
  129.2 1.3 collective-permute-start.18
  130.6 0.7 slice_convert_fusion
  131.4 1.3 multiply_convert_fusion.refs_3_
  132.7 11.1 %weight_product.3 = f32[3072,512]{1,0:T(8,128)} custom-call(s32[1]{0:T(128)} %bitcast.16.block_ref, bf16[512,12288]{1,0:T(8,128)(2,1)} %bitcast.27, bf16[512,3072]{1,0:T(8,128)(2,1)} %collective-permute-done.12.got_ref, bf16[512,512]{1,0:T(8,128)(2,1)} %bitcast.6.grads_ref, bf16[512,512]{1,0:T(8,128)(2,1)} %collective-permute-done.2.other_ref, ...), custom_call_target="tpu_custom_call" | custom-call | tf_op jit(solution)/shard_map/weight_product/pallas_call | solution.py:197
  143.8 13.8 %collective-permute-done.19.refs_0_ = bf16[768,512]{1,0:T(8,128)(2,1)S(1)} collective-permute-done((bf16[768,512]{1,0:T(8,128)(2,1)}, bf16[768,512]{1,0:T(8,128)(2,1)S(1)}, u32[]{:S(2)}, u32[]{:S(2)}) %collective-permute-start.19) | collective-permute-done | bytes 786464 | tf_op jit(solution)/shard_map/ppermute | solution.py:29
  157.6 2.3 %collective-permute-done.20.refs_1_ = bf16[768,512]{1,0:T(8,128)(2,1)S(1)} collective-permute-done((bf16[768,512]{1,0:T(8,128)(2,1)}, bf16[768,512]{1,0:T(8,128)(2,1)S(1)}, u32[]{:S(2)}, u32[]{:S(2)}) %collective-permute-start.20) | collective-permute-done | bytes 786464 | tf_op jit(solution)/shard_map/ppermute | solution.py:29
  159.9 1.6 rotate_back.2.refs_4_
  161.5 4.1 %collective-permute-done.18.refs_1_ = bf16[768,512]{1,0:T(8,128)(2,1)S(1)} collective-permute-done((bf16[768,512]{1,0:T(8,128)(2,1)}, bf16[768,512]{1,0:T(8,128)(2,1)S(1)}, u32[]{:S(2)}, u32[]{:S(2)}) %collective-permute-start.18) | collective-permute-done | bytes 786464 | tf_op jit(solution)/shard_map/ppermute | solution.py:29
  165.6 1.6 rotate_back.3
  (34 shorter events, 0.2 us)
Async XLA Ops:
  3.3 8.4 %copy-start.3 = (s32[1,24,512]{2,1,0:T(8,128)S(1)}, s32[1,24,512]{2,1,0:T(8,128)}, u32[]{:S(2)}) copy-start(s32[1,24,512]{2,1,0:T(8,128)} %param.10) | copy-start | bytes 147460
  3.3 8.4 %copy-start.2 = (bf16[1,512,512]{2,1,0:T(8,128)(2,1)S(1)}, bf16[1,512,512]{2,1,0:T(8,128)(2,1)}, u32[]{:S(2)}) copy-start(bf16[1,512,512]{2,1,0:T(8,128)(2,1)} %param.8) | copy-start | bytes 1572868
  3.3 11.7 %copy-start.4 = (s32[3072]{0:T(1024)S(1)}, s32[3072]{0:T(1024)}, u32[]{:S(2)}) copy-start(s32[3072]{0:T(1024)} %param.11) | copy-start | bytes 36868
  7.1 8.0 %collective-permute-start.1 = (bf16[512,3072]{1,0:T(8,128)(2,1)}, bf16[512,3072]{1,0:T(8,128)(2,1)S(1)}, u32[]{:S(2)}, u32[]{:S(2)}) collective-permute-start(bf16[512,3072]{1,0:T(8,128)(2,1)} %constant_dynamic-slice_fusion.3), channel_id=1, source_target_pairs={{0,4},{1,5},{2,6},{3,7},{4,0},{5,1},{6,2},{7,3},{8,12},{9,13},{10,... | collective-permute-start | bytes 9437192 | tf_op jit(solution)/shard_map/ppermute | solution.py:29
  7.1 22.8 %collective-permute-start.3 = (bf16[768,512]{1,0:T(8,128)(2,1)}, bf16[768,512]{1,0:T(8,128)(2,1)}, u32[]{:S(2)}, u32[]{:S(2)}) collective-permute-start(bf16[768,512]{1,0:T(8,128)(2,1)} %get-tuple-element.65), channel_id=1, source_target_pairs={{0,1},{1,0},{2,3},{3,2},{4,7},{5,6},{6,5},{7,4},{8,9},{9,8},{10,11... | collective-permute-start | bytes 2359304 | tf_op jit(solution)/shard_map/ppermute | solution.py:29
  9.0 7.2 %collective-permute-start.2 = (bf16[512,512]{1,0:T(8,128)(2,1)}, bf16[512,512]{1,0:T(8,128)(2,1)}, u32[]{:S(2)}, u32[]{:S(2)}) collective-permute-start(bf16[512,512]{1,0:T(8,128)(2,1)} %bitcast.6.grads_ref), channel_id=1, source_target_pairs={{0,4},{1,5},{2,6},{3,7},{4,0},{5,1},{6,2},{7,3},{8,12},{9,13},{10,... | collective-permute-start | bytes 1572872 | tf_op jit(solution)/shard_map/ppermute | solution.py:29
  11.4 18.5 %collective-permute-start.4 = (bf16[768,512]{1,0:T(8,128)(2,1)}, bf16[768,512]{1,0:T(8,128)(2,1)}, u32[]{:S(2)}, u32[]{:S(2)}) collective-permute-start(bf16[768,512]{1,0:T(8,128)(2,1)} %get-tuple-element.64), channel_id=1, source_target_pairs={{0,3},{1,2},{2,1},{3,0},{4,5},{5,4},{6,7},{7,6},{8,11},{9,10},{10,... | collective-permute-start | bytes 2359304 | tf_op jit(solution)/shard_map/ppermute | solution.py:29
  12.6 17.4 %collective-permute-start = (bf16[544,512]{1,0:T(8,128)(2,1)}, bf16[544,512]{1,0:T(8,128)(2,1)}, u32[]{:S(2)}, u32[]{:S(2)}) collective-permute-start(bf16[544,512]{1,0:T(8,128)(2,1)} %fusion.1), channel_id=1, source_target_pairs={{16,8},{17,9},{18,10},{19,11},{20,12},{21,13},{22,14},{23,15},{24,... | collective-permute-start | bytes 1671176 | tf_op jit(solution)/shard_map/ppermute | solution.py:29
  15.1 29.3 %collective-permute-start.7 = (s32[768]{0:T(1024)S(1)}, s32[768]{0:T(1024)S(1)}, u32[]{:S(2)}, u32[]{:S(2)}) collective-permute-start(s32[768]{0:T(1024)S(1)} %dynamic_slice.32), channel_id=1, source_target_pairs={{0,8},{1,12},{2,0},{3,4},{4,9},{5,13},{6,1},{7,5},{8,10},{9,14},{1... | collective-permute-start | bytes 9224 | tf_op jit(solution)/shard_map/ppermute | solution.py:29
  16.3 8.2 %copy-start = (bf16[1,3072,512]{2,1,0:T(8,128)(2,1)S(1)}, bf16[1,3072,512]{2,1,0:T(8,128)(2,1)}, u32[]{:S(2)}) copy-start(bf16[1,3072,512]{2,1,0:T(8,128)(2,1)} %param.9) | copy-start | bytes 9437188
  29.9 14.5 %collective-permute-start.5 = (bf16[544,512]{1,0:T(8,128)(2,1)}, bf16[544,512]{1,0:T(8,128)(2,1)S(1)}, u32[]{:S(2)}, u32[]{:S(2)}) collective-permute-start(bf16[544,512]{1,0:T(8,128)(2,1)} %collective-permute-done), channel_id=1, source_target_pairs={{0,8},{1,9},{2,10},{3,11},{4,12},{5,13},{6,14},{7,15},{8,0},{9,1},... | collective-permute-start | bytes 1671176 | tf_op jit(solution)/shard_map/ppermute | solution.py:29
  35.0 43.2 %collective-permute-start.9 = (bf16[1664,512]{1,0:T(8,128)(2,1)}, bf16[1664,512]{1,0:T(8,128)(2,1)}, u32[]{:S(2)}, u32[]{:S(2)}) collective-permute-start(bf16[1664,512]{1,0:T(8,128)(2,1)} %pad_maximum_fusion.1), channel_id=1, source_target_pairs={{16,8},{17,9},{18,10},{19,11},{20,12},{21,13},{22,14},{23,15},{24,... | collective-permute-start | bytes 5111816 | tf_op jit(solution)/shard_map/ppermute | solution.py:29
  37.0 20.0 %collective-permute-start.13 = (bf16[768,512]{1,0:T(8,128)(2,1)}, bf16[768,512]{1,0:T(8,128)(2,1)}, u32[]{:S(2)}, u32[]{:S(2)}) collective-permute-start(bf16[768,512]{1,0:T(8,128)(2,1)} %get-tuple-element.49), channel_id=1, source_target_pairs={{0,2},{1,3},{2,0},{3,1},{4,6},{5,7},{6,4},{7,5},{8,10},{9,11},{10,... | collective-permute-start | bytes 2359304 | tf_op jit(solution)/shard_map/ppermute | solution.py:29
  44.4 0.8 copy-start.1
  45.4 22.0 %collective-permute-start.8 = (bf16[1024,512]{1,0:T(8,128)(2,1)S(1)}, bf16[1024,512]{1,0:T(8,128)(2,1)S(1)}, u32[]{:S(2)}, u32[]{:S(2)}) collective-permute-start(bf16[1024,512]{1,0:T(8,128)(2,1)S(1)} %get-tuple-element.69.refs_0_), channel_id=1, source_target_pairs={{0,1},{1,0},{2,3},{3,2},{4,7},{5,6},{6,5},{7,4},{8,9},{9,8},{10,11... | collective-permute-start | bytes 3145736 | tf_op jit(solution)/shard_map/ppermute | solution.py:29
  48.0 73.1 %collective-permute-start.6 = (bf16[3072,512]{1,0:T(8,128)(2,1)}, bf16[3072,512]{1,0:T(8,128)(2,1)}, u32[]{:S(2)}, u32[]{:S(2)}) collective-permute-start(bf16[3072,512]{1,0:T(8,128)(2,1)} %weight_product.2), channel_id=1, source_target_pairs={{0,8},{1,9},{2,10},{3,11},{4,12},{5,13},{6,14},{7,15},{8,0},{9,1},... | collective-permute-start | bytes 9437192 | tf_op jit(solution)/shard_map/ppermute | solution.py:29
  49.8 8.4 %collective-permute-start.10 = (s32[768]{0:T(1024)S(1)}, s32[768]{0:T(1024)S(1)}, u32[]{:S(2)}, u32[]{:S(2)}) collective-permute-start(s32[768]{0:T(1024)S(1)} %collective-permute-done.7), channel_id=1, source_target_pairs={{0,4},{1,5},{2,6},{3,7},{4,0},{5,1},{6,2},{7,3},{8,12},{9,13},{10,... | collective-permute-start | bytes 9224 | tf_op jit(solution)/shard_map/ppermute | solution.py:29
  57.0 53.0 %collective-permute-start.12 = (bf16[512,3072]{1,0:T(8,128)(2,1)}, bf16[512,3072]{1,0:T(8,128)(2,1)}, u32[]{:S(2)}, u32[]{:S(2)}) collective-permute-start(bf16[512,3072]{1,0:T(8,128)(2,1)} %constant_dynamic-slice_fusion), channel_id=1, source_target_pairs={{0,4},{1,5},{2,6},{3,7},{4,0},{5,1},{6,2},{7,3},{8,12},{9,13},{10,... | collective-permute-start | bytes 9437192 | tf_op jit(solution)/shard_map/ppermute | solution.py:29
  58.2 9.3 %copy-start.5 = (s32[768]{0:T(1024)}, s32[768]{0:T(1024)S(1)}, u32[]{:S(2)}) copy-start(s32[768]{0:T(1024)S(1)} %collective-permute-done.10) | copy-start | bytes 9220
  58.2 48.4 %collective-permute-start.14 = (bf16[1408,512]{1,0:T(8,128)(2,1)S(1)}, bf16[1408,512]{1,0:T(8,128)(2,1)S(1)}, u32[]{:S(2)}, u32[]{:S(2)}) collective-permute-start(bf16[1408,512]{1,0:T(8,128)(2,1)S(1)} %pad_maximum_fusion.2), channel_id=1, source_target_pairs={{16,8},{17,9},{18,10},{19,11},{20,12},{21,13},{22,14},{23,15},{24,... | collective-permute-start | bytes 4325384 | tf_op jit(solution)/shard_map/ppermute | solution.py:29
  79.8 30.1 %collective-permute-start.11 = (bf16[2,1024,512]{2,1,0:T(8,128)(2,1)}, bf16[2,1024,512]{2,1,0:T(8,128)(2,1)}, u32[]{:S(2)}, u32[]{:S(2)}) collective-permute-start(bf16[2,1024,512]{2,1,0:T(8,128)(2,1)} %pad_maximum_fusion), channel_id=1, source_target_pairs={{0,3},{1,2},{2,1},{3,0},{4,5},{5,4},{6,7},{7,6},{8,11},{9,10},{10,... | collective-permute-start | bytes 6291464 | tf_op jit(solution)/shard_map/ppermute | solution.py:29
  81.8 26.4 %collective-permute-start.15 = (bf16[1664,512]{1,0:T(8,128)(2,1)}, bf16[1664,512]{1,0:T(8,128)(2,1)}, u32[]{:S(2)}, u32[]{:S(2)}) collective-permute-start(bf16[1664,512]{1,0:T(8,128)(2,1)} %collective-permute-done.9.refs_3_), channel_id=1, source_target_pairs={{0,4},{1,5},{2,6},{3,7},{4,0},{5,1},{6,2},{7,3},{8,12},{9,13},{10,... | collective-permute-start | bytes 5111816 | tf_op jit(solution)/shard_map/ppermute | solution.py:29
  106.6 3.4 %collective-permute-start.16 = (bf16[1408,512]{1,0:T(8,128)(2,1)S(1)}, bf16[1408,512]{1,0:T(8,128)(2,1)}, u32[]{:S(2)}, u32[]{:S(2)}) collective-permute-start(bf16[1408,512]{1,0:T(8,128)(2,1)S(1)} %collective-permute-done.14.refs_4_), channel_id=1, source_target_pairs={{0,4},{1,5},{2,6},{3,7},{4,0},{5,1},{6,2},{7,3},{8,12},{9,13},{10,... | collective-permute-start | bytes 4325384 | tf_op jit(solution)/shard_map/ppermute | solution.py:29
  121.1 36.5 %collective-permute-start.19 = (bf16[768,512]{1,0:T(8,128)(2,1)}, bf16[768,512]{1,0:T(8,128)(2,1)S(1)}, u32[]{:S(2)}, u32[]{:S(2)}) collective-permute-start(bf16[768,512]{1,0:T(8,128)(2,1)} %get-tuple-element.60), channel_id=1, source_target_pairs={{0,2},{1,3},{2,10},{3,11},{4,6},{5,7},{6,14},{7,15},{8,0},{9,1},{1... | collective-permute-start | bytes 2359304 | tf_op jit(solution)/shard_map/ppermute | solution.py:29
  123.4 36.5 %collective-permute-start.20 = (bf16[768,512]{1,0:T(8,128)(2,1)}, bf16[768,512]{1,0:T(8,128)(2,1)S(1)}, u32[]{:S(2)}, u32[]{:S(2)}) collective-permute-start(bf16[768,512]{1,0:T(8,128)(2,1)} %get-tuple-element.61), channel_id=1, source_target_pairs={{0,3},{1,2},{2,11},{3,10},{4,7},{5,6},{6,15},{7,14},{8,1},{9,0},{1... | collective-permute-start | bytes 2359304 | tf_op jit(solution)/shard_map/ppermute | solution.py:29
  125.1 36.4 %collective-permute-start.17 = (bf16[768,512]{1,0:T(8,128)(2,1)}, bf16[768,512]{1,0:T(8,128)(2,1)S(1)}, u32[]{:S(2)}, u32[]{:S(2)}) collective-permute-start(bf16[768,512]{1,0:T(8,128)(2,1)} %get-tuple-element.58), channel_id=1, source_target_pairs={{0,10},{1,11},{2,2},{3,3},{4,14},{5,15},{6,6},{7,7},{8,8},{9,9},{1... | collective-permute-start | bytes 2359304 | tf_op jit(solution)/shard_map/ppermute | solution.py:29
  129.2 36.4 %collective-permute-start.18 = (bf16[768,512]{1,0:T(8,128)(2,1)}, bf16[768,512]{1,0:T(8,128)(2,1)S(1)}, u32[]{:S(2)}, u32[]{:S(2)}) collective-permute-start(bf16[768,512]{1,0:T(8,128)(2,1)} %get-tuple-element.59), channel_id=1, source_target_pairs={{0,11},{1,10},{2,3},{3,2},{4,15},{5,14},{6,7},{7,6},{8,9},{9,8},{1... | collective-permute-start | bytes 2359304 | tf_op jit(solution)/shard_map/ppermute | solution.py:29

commit v5 on v4

--- a/solution.py
+++ b/solution.py
@@ -242,22 +242,23 @@
     limit = jnp.pad(limit, ((0, -blocks % 16), (0, 0)))
     grads_far = down(jnp.concatenate([current_grads[0], limit], axis=0))
 
-    inputs_then = after(inputs_local, sliced)
     grads_other = other_core(grads_before)
-    got_far = other_core(features(inputs_then, jnp.bitwise_xor(dp, 3)))
-    weight_then = after(weight_local, got_far)
+    for_far = features(after(inputs_local, sliced), jnp.bitwise_xor(dp, 3))
+    weight_then = after(weight_local, sliced)
     here, opposite = quarter_for(weight_then, 0), quarter_for(weight_then, 2)
-    partial = product(
-        inputs_local, scalar(jnp.bitwise_xor(dp, 2)), got_far, grads_before, grads_other, jnp.bfloat16
-    )
-    grads_far, partial, here, opposite, *pair = lax.optimization_barrier(
-        (grads_far, partial, here, opposite, *pair)
+    grads_far, grads_other, for_far, here, opposite, *pair = lax.optimization_barrier(
+        (grads_far, grads_other, for_far, here, opposite, *pair)
     )
 
     grads_near = other_chip(grads_far)
     pair = down(jnp.concatenate([*pair, here[:HB]], axis=0))
     opposite = over_z(opposite, 2, 2)
-    arrived = other_chip(after(partial, grads_near))
+    got_far = other_core(for_far)
+    partial = product(
+        inputs_local, scalar(jnp.bitwise_xor(dp, 2)), got_far, grads_before, grads_other, jnp.bfloat16
+    )
+    grads_near, partial = lax.optimization_barrier((grads_near, partial))
+    arrived = other_chip(partial)
     bits = lax.dynamic_slice_in_dim(sign_bits, dp * quarter, quarter, 0)
     bits = send(bits, lambda s, d, t: (s, t ^ 2, d))
     rest = down(after(jnp.concatenate([here[HB:], opposite], axis=0), grads_near))
@@ -289,6 +290,7 @@
     )
     place = scalar(chip * 2 + jnp.bitwise_and(tensor, 1))
     table = signed(sign_bits, (-1, HB, 1)).astype(jnp.bfloat16)
+    limit, weight_grad = lax.optimization_barrier((limit, weight_grad))
     upstream_grad = back(place, pieces[:2], (0, 1), limit, table)
     upstream_grad = back(place, pieces[2:], (2, 3), limit, table, upstream_grad)
     return (upstream_grad[None], weight_grad[None])

time: 168 us -> 165 us (0.982)
  local copies, waits for them, and re-layouts: 13.4 us -> 18 us
  waiting for transfers between devices: 74.7 us -> 71.4 us
  starting transfers between devices: 33.8 us -> 30.7 us
    ppermute x21, waiting for transfers between devices: 74.7 us -> 71.4 us  [send(): return lax.ppermute(shard, AXES, pairs)]
    ppermute x21, starting transfers between devices: 33.8 us -> 30.7 us  [send(): return lax.ppermute(shard, AXES, pairs)]
    unnamed x12 -> x32, local copies, waits for them, and re-layouts: 0.82 us -> 3.7 us
  transfers between devices with their start and end apart: 21 -> 21, of which waited for: 9 -> 9; matrix products, arithmetic and copies ran while one was open for 10% -> 13% of each run, Pallas kernels for 20% -> 20%
where the time goes in v5:
time: 165 us
  waiting for transfers between devices  71.4 us (43%)
  Pallas kernels  34.1 us (21%)
  starting transfers between devices  30.7 us (19%)
  local copies, waits for them, and re-layouts  18 us (11%)
  other arithmetic  9.37 us (6%)
    ppermute x21, waiting for transfers between devices, send(): return lax.ppermute(shard, AXES, pairs)  71.4 us
    ppermute x21, starting transfers between devices, send(): return lax.ppermute(shard, AXES, pairs)  30.7 us
    pallas_call x2, Pallas kernels, product(): pl.pallas_call(product_kernel, out_shape=jax.ShapeDtypeStruct((rows, colu...  17.7 us
    pallas_call x1, Pallas kernels, rotate(): pl.pallas_call(rotate_kernel, out_shape=[jax.ShapeDtypeStruct((rows, toke...  11.2 us
    dynamic_slice x2, local copies, waits for them, and re-layouts, features(): return lax.dynamic_slice_in_dim(inputs, block * rows_here, rows_here, 1)  7.88 us
    pallas_call x2, Pallas kernels, back(): pl.pallas_call(functools.partial(back_kernel, rounds), out_shape=jax.Shap...  4.55 us
    dynamic_slice x2, local copies, waits for them, and re-layouts, quarter_for(): lax.dynamic_slice_in_dim(weight, jnp.bitwise_xor(tensor, x) * quarter, qu...  4 us
    unnamed x32, local copies, waits for them, and re-layouts  3.7 us
  transfers between devices with their start and end apart: 21, of which 9 were waited for; matrix products, arithmetic and copies ran while one was open for 13% of the time, Pallas kernels for 20%

profile of v5, /device:TPU:20, one launch (start us, length us, event | category | flops | bytes accessed | tf_op | source)
XLA Modules:
  0.0 164.7 jit_solution(17055274642208544730)
XLA Ops:
  0.7 1.6 dynamic-slice_bitcast_fusion
  2.3 2.0 %collective-permute-start.2 = (bf16[768,512]{1,0:T(8,128)(2,1)S(1)}, bf16[768,512]{1,0:T(8,128)(2,1)S(1)}, u32[]{:S(2)}, u32[]{:S(2)}) collective-permute-start(bf16[768,512]{1,0:T(8,128)(2,1)S(1)} %get-tuple-element.73), channel_id=1, source_target_pairs={{0,1},{1,0},{2,3},{3,2},{4,7},{5,6},{6,5},{7,4},{8,9},{9,8},{10,11... | collective-permute-start | bytes 2359304 | tf_op jit(solution)/shard_map/ppermute | solution.py:29
  4.3 2.5 %collective-permute-start.3 = (bf16[768,512]{1,0:T(8,128)(2,1)S(1)}, bf16[768,512]{1,0:T(8,128)(2,1)}, u32[]{:S(2)}, u32[]{:S(2)}) collective-permute-start(bf16[768,512]{1,0:T(8,128)(2,1)S(1)} %get-tuple-element.72), channel_id=1, source_target_pairs={{0,3},{1,2},{2,1},{3,0},{4,5},{5,4},{6,7},{7,6},{8,11},{9,10},{10,... | collective-permute-start | bytes 2359304 | tf_op jit(solution)/shard_map/ppermute | solution.py:29
  6.8 0.8 fusion.1
  7.7 2.4 %collective-permute-start = (bf16[544,512]{1,0:T(8,128)(2,1)}, bf16[544,512]{1,0:T(8,128)(2,1)}, u32[]{:S(2)}, u32[]{:S(2)}) collective-permute-start(bf16[544,512]{1,0:T(8,128)(2,1)} %fusion.1), channel_id=1, source_target_pairs={{16,8},{17,9},{18,10},{19,11},{20,12},{21,13},{22,14},{23,15},{24,... | collective-permute-start | bytes 1671176 | tf_op jit(solution)/shard_map/ppermute | solution.py:29
  10.3 1.1 collective-permute-start.7
  11.4 2.4 %constant_dynamic-slice_fusion.1 = (bf16[768,512]{1,0:T(8,128)(2,1)}, bf16[768,512]{1,0:T(8,128)(2,1)S(1)}) fusion(bf16[3072,512]{1,0:T(8,128)(2,1)} %bitcast.33, s32[]{:T(128)S(6)} %select_n.24, s32[]{:T(128)S(6)} %select_n.23), kind=kLoop, calls=%fused_computation.20 | loop fusion | bytes 3145736 | tf_op jit(solution)/shard_map/dynamic_slice | solution.py:230
  13.9 4.0 %constant_dynamic-slice_fusion.3 = bf16[512,3072]{1,0:T(8,128)(2,1)} fusion(bf16[512,12288]{1,0:T(8,128)(2,1)} %bitcast.27, s32[]{:T(128)S(6)} %select_n.22), kind=kLoop, calls=%fused_computation.22 | loop fusion | bytes 6291460 | tf_op jit(solution)/shard_map/dynamic_slice | solution.py:221
  17.9 0.8 copy-done.3
  18.8 5.7 %collective-permute-done = bf16[544,512]{1,0:T(8,128)(2,1)} collective-permute-done((bf16[544,512]{1,0:T(8,128)(2,1)}, bf16[544,512]{1,0:T(8,128)(2,1)}, u32[]{:S(2)}, u32[]{:S(2)}) %collective-permute-start) | collective-permute-done | bytes 557088 | tf_op jit(solution)/shard_map/ppermute | solution.py:29
  24.4 0.9 copy-done.10
  25.3 2.4 %collective-permute-start.4 = (bf16[544,512]{1,0:T(8,128)(2,1)}, bf16[544,512]{1,0:T(8,128)(2,1)}, u32[]{:S(2)}, u32[]{:S(2)}) collective-permute-start(bf16[544,512]{1,0:T(8,128)(2,1)} %collective-permute-done), channel_id=1, source_target_pairs={{0,8},{1,9},{2,10},{3,11},{4,12},{5,13},{6,14},{7,15},{8,0},{9,1},... | collective-permute-start | bytes 1671176 | tf_op jit(solution)/shard_map/ppermute | solution.py:29
  27.7 2.7 %pad_maximum_fusion.1 = bf16[1664,512]{1,0:T(8,128)(2,1)} fusion(bf16[128,512]{1,0:T(8,128)(2,1)S(1)} %slice.17, bf16[768,512]{1,0:T(8,128)(2,1)} %collective-permute-done.3, bf16[768,512]{1,0:T(8,128)(2,1)} %copy-done.10), kind=kLoop, calls=%fused_computation.1 | loop fusion | flops 5111808 | bytes 3407872 | tf_op jit(solution)/shard_map/concatenate | solution.py:254
  30.5 1.9 %collective-permute-start.9 = (bf16[1664,512]{1,0:T(8,128)(2,1)}, bf16[1664,512]{1,0:T(8,128)(2,1)}, u32[]{:S(2)}, u32[]{:S(2)}) collective-permute-start(bf16[1664,512]{1,0:T(8,128)(2,1)} %pad_maximum_fusion.1), channel_id=1, source_target_pairs={{16,8},{17,9},{18,10},{19,11},{20,12},{21,13},{22,14},{23,15},{24,... | collective-permute-start | bytes 5111816 | tf_op jit(solution)/shard_map/ppermute | solution.py:29
  32.4 1.6 collective-permute-start.13
  34.0 0.7 hadamard_signs.1
  34.7 3.8 %constant_dynamic-slice_fusion = bf16[512,3072]{1,0:T(8,128)(2,1)} fusion(bf16[512,12288]{1,0:T(8,128)(2,1)} %bitcast.28, s32[]{:T(128)S(6)} %select_n.27), kind=kLoop, calls=%fused_computation.19 | loop fusion | bytes 6291460 | tf_op jit(solution)/shard_map/dynamic_slice | solution.py:221
  38.5 1.1 slice.16
  39.7 6.9 %weight_product.2 = bf16[3072,512]{1,0:T(8,128)(2,1)} custom-call(s32[1]{0:T(128)} %bitcast.8.block_ref, bf16[512,12288]{1,0:T(8,128)(2,1)} %bitcast.29, bf16[512,3072]{1,0:T(8,128)(2,1)S(1)} %collective-permute-done.5.got_ref, bf16[512,512]{1,0:T(8,128)(2,1)S(1)} %bitcast.25, bf16[512,512]{1,0:T(8,128)(2,1)S(1)} %copy-done.4), custom_call_target="tpu_custom_call" | custom-call | tf_op jit(solution)/shard_map/weight_product/pallas_call | solution.py:197
  46.6 1.1 slice.15
  48.2 1.7 %collective-permute-start.6 = (bf16[3072,512]{1,0:T(8,128)(2,1)}, bf16[3072,512]{1,0:T(8,128)(2,1)}, u32[]{:S(2)}, u32[]{:S(2)}) collective-permute-start(bf16[3072,512]{1,0:T(8,128)(2,1)} %weight_product.2), channel_id=1, source_target_pairs={{0,8},{1,9},{2,10},{3,11},{4,12},{5,13},{6,14},{7,15},{8,0},{9,1},... | collective-permute-start | bytes 9437192 | tf_op jit(solution)/shard_map/ppermute | solution.py:29
  49.9 1.1 collective-permute-start.12
  51.0 3.3 %collective-permute-done.13 = bf16[768,512]{1,0:T(8,128)(2,1)} collective-permute-done((bf16[768,512]{1,0:T(8,128)(2,1)}, bf16[768,512]{1,0:T(8,128)(2,1)}, u32[]{:S(2)}, u32[]{:S(2)}) %collective-permute-start.13) | collective-permute-done | bytes 786464 | tf_op jit(solution)/shard_map/ppermute | solution.py:29
  54.3 1.2 pad_maximum_fusion.2
  55.6 3.5 %collective-permute-start.14 = (bf16[1408,512]{1,0:T(8,128)(2,1)S(1)}, bf16[1408,512]{1,0:T(8,128)(2,1)S(1)}, u32[]{:S(2)}, u32[]{:S(2)}) collective-permute-start(bf16[1408,512]{1,0:T(8,128)(2,1)S(1)} %pad_maximum_fusion.2), channel_id=1, source_target_pairs={{16,8},{17,9},{18,10},{19,11},{20,12},{21,13},{22,14},{23,15},{24,... | collective-permute-start | bytes 4325384 | tf_op jit(solution)/shard_map/ppermute | solution.py:29
  59.1 14.5 %collective-permute-done.9.refs_3_ = bf16[1664,512]{1,0:T(8,128)(2,1)} collective-permute-done((bf16[1664,512]{1,0:T(8,128)(2,1)}, bf16[1664,512]{1,0:T(8,128)(2,1)}, u32[]{:S(2)}, u32[]{:S(2)}) %collective-permute-start.9) | collective-permute-done | bytes 1703968 | tf_op jit(solution)/shard_map/ppermute | solution.py:29
  73.6 1.2 collective-permute-done.10
  74.7 0.6 copy-done.15
  75.3 1.6 pad_maximum_fusion
  76.9 0.5 collective-permute-start.11
  77.4 1.1 collective-permute-start.15
  78.5 25.5 %collective-permute-done.14.refs_4_ = bf16[1408,512]{1,0:T(8,128)(2,1)S(1)} collective-permute-done((bf16[1408,512]{1,0:T(8,128)(2,1)S(1)}, bf16[1408,512]{1,0:T(8,128)(2,1)S(1)}, u32[]{:S(2)}, u32[]{:S(2)}) %collective-permute-start.14) | collective-permute-done | bytes 1441824 | tf_op jit(solution)/shard_map/ppermute | solution.py:29
  104.0 0.7 fusion.4
  104.7 0.9 multiply_convert_fusion.1
  105.7 1.7 %collective-permute-done.16.refs_6_ = bf16[1408,512]{1,0:T(8,128)(2,1)} collective-permute-done((bf16[1408,512]{1,0:T(8,128)(2,1)S(1)}, bf16[1408,512]{1,0:T(8,128)(2,1)}, u32[]{:S(2)}, u32[]{:S(2)}) %collective-permute-start.16) | collective-permute-done | bytes 1441824 | tf_op jit(solution)/shard_map/ppermute | solution.py:29
  107.4 1.4 copy-done.7
  108.7 11.2 %rotate.1 = (bf16[768,512]{1,0:T(8,128)(2,1)}, bf16[768,512]{1,0:T(8,128)(2,1)}, bf16[768,512]{1,0:T(8,128)(2,1)}, bf16[768,512]{1,0:T(8,128)(2,1)}) custom-call(s32[1]{0:T(128)} %bitcast.9.base_ref, bf16[2,6,128,256]{3,2,1,0:T(8,128)(2,1)S(1)} %pad_maximum_fusion.4.table_ref, bf16[1024,512]{1,0:T(8,128)(2,1)S(1)} %get-tuple-element.77.refs_0_, ...), custom_call_target="tpu_custom_call" | custom-call | tf_op jit(solution)/shard_map/rotate/pallas_call | solution.py:119
  119.9 1.7 %collective-permute-start.19 = (bf16[768,512]{1,0:T(8,128)(2,1)}, bf16[768,512]{1,0:T(8,128)(2,1)}, u32[]{:S(2)}, u32[]{:S(2)}) collective-permute-start(bf16[768,512]{1,0:T(8,128)(2,1)} %get-tuple-element.69), channel_id=1, source_target_pairs={{0,2},{1,3},{2,10},{3,11},{4,6},{5,7},{6,14},{7,15},{8,0},{9,1},{1... | collective-permute-start | bytes 2359304 | tf_op jit(solution)/shard_map/ppermute | solution.py:29
  121.6 0.9 collective-permute-start.20
  122.5 4.7 %collective-permute-start.17 = (bf16[768,512]{1,0:T(8,128)(2,1)}, bf16[768,512]{1,0:T(8,128)(2,1)S(1)}, u32[]{:S(2)}, u32[]{:S(2)}) collective-permute-start(bf16[768,512]{1,0:T(8,128)(2,1)} %get-tuple-element.64), channel_id=1, source_target_pairs={{0,10},{1,11},{2,2},{3,3},{4,14},{5,15},{6,6},{7,7},{8,8},{9,9},{1... | collective-permute-start | bytes 2359304 | tf_op jit(solution)/shard_map/ppermute | solution.py:29
  127.2 1.1 collective-permute-start.18
  128.3 0.7 slice_convert_fusion
  129.1 0.5 multiply_convert_fusion.refs_3_
  129.6 10.8 %weight_product.3 = f32[3072,512]{1,0:T(8,128)} custom-call(s32[1]{0:T(128)} %bitcast.14.block_ref, bf16[512,12288]{1,0:T(8,128)(2,1)} %bitcast.30, bf16[512,3072]{1,0:T(8,128)(2,1)} %collective-permute-done.12.got_ref, bf16[512,512]{1,0:T(8,128)(2,1)S(1)} %bitcast.26, bf16[512,512]{1,0:T(8,128)(2,1)S(1)} %copy-done.5, ...), custom_call_target="tpu_custom_call" | custom-call | tf_op jit(solution)/shard_map/weight_product/pallas_call | solution.py:197
  140.7 17.2 %collective-permute-done.20.refs_1_ = bf16[768,512]{1,0:T(8,128)(2,1)} collective-permute-done((bf16[768,512]{1,0:T(8,128)(2,1)}, bf16[768,512]{1,0:T(8,128)(2,1)}, u32[]{:S(2)}, u32[]{:S(2)}) %collective-permute-start.20) | collective-permute-done | bytes 786464 | tf_op jit(solution)/shard_map/ppermute | solution.py:29
  157.9 2.9 %rotate_back.2.refs_4_ = bf16[3072,512]{1,0:T(8,128)(2,1)} custom-call(s32[1]{0:T(128)} %bitcast.here_ref, bf16[768,512]{1,0:T(8,128)(2,1)} %collective-permute-done.19.refs_0_, bf16[768,512]{1,0:T(8,128)(2,1)} %collective-permute-done.20.refs_1_, f32[24,1,512]{2,1,0:T(1,128)S(1)} %reshape.59.refs_2_, bf16[24,128,128]{2,1,0:T(8,128)(2,1)S(1)} %multiply_convert_fusion.refs_3_), custom_call_target="tpu_custom_call" | custom-call | tf_op jit(solution)/shard_map/rotate_back/pallas_call | solution.py:157
  160.9 2.1 %collective-permute-done.18.refs_1_ = bf16[768,512]{1,0:T(8,128)(2,1)S(1)} collective-permute-done((bf16[768,512]{1,0:T(8,128)(2,1)}, bf16[768,512]{1,0:T(8,128)(2,1)S(1)}, u32[]{:S(2)}, u32[]{:S(2)}) %collective-permute-start.18) | collective-permute-done | bytes 786464 | tf_op jit(solution)/shard_map/ppermute | solution.py:29
  163.0 1.6 rotate_back.3
  (54 shorter events, 1.2 us)
Async XLA Ops:
  0.6 6.1 %copy-start.13 = (s32[1,24,512]{2,1,0:T(8,128)S(1)}, s32[1,24,512]{2,1,0:T(8,128)}, u32[]{:S(2)}) copy-start(s32[1,24,512]{2,1,0:T(8,128)} %param.10) | copy-start | bytes 147460
  0.6 6.2 %copy-start.11 = (bf16[1,512,512]{2,1,0:T(8,128)(2,1)S(1)}, bf16[1,512,512]{2,1,0:T(8,128)(2,1)}, u32[]{:S(2)}) copy-start(bf16[1,512,512]{2,1,0:T(8,128)(2,1)} %param.8) | copy-start | bytes 1572868
  0.7 9.4 %copy-start = (bf16[1,512,512]{2,1,0:T(8,128)(2,1)S(1)}, bf16[1,512,512]{2,1,0:T(8,128)(2,1)}, u32[]{:S(2)}) copy-start(bf16[1,512,512]{2,1,0:T(8,128)(2,1)} %param.7) | copy-start | bytes 1572868
  0.7 9.5 %copy-start.14 = (s32[3072]{0:T(1024)S(1)}, s32[3072]{0:T(1024)}, u32[]{:S(2)}) copy-start(s32[3072]{0:T(1024)} %param.11) | copy-start | bytes 36868
  2.3 22.2 %collective-permute-start.2 = (bf16[768,512]{1,0:T(8,128)(2,1)S(1)}, bf16[768,512]{1,0:T(8,128)(2,1)S(1)}, u32[]{:S(2)}, u32[]{:S(2)}) collective-permute-start(bf16[768,512]{1,0:T(8,128)(2,1)S(1)} %get-tuple-element.73), channel_id=1, source_target_pairs={{0,1},{1,0},{2,3},{3,2},{4,7},{5,6},{6,5},{7,4},{8,9},{9,8},{10,11... | collective-permute-start | bytes 2359304 | tf_op jit(solution)/shard_map/ppermute | solution.py:29
  4.3 20.2 %collective-permute-start.3 = (bf16[768,512]{1,0:T(8,128)(2,1)S(1)}, bf16[768,512]{1,0:T(8,128)(2,1)}, u32[]{:S(2)}, u32[]{:S(2)}) collective-permute-start(bf16[768,512]{1,0:T(8,128)(2,1)S(1)} %get-tuple-element.72), channel_id=1, source_target_pairs={{0,3},{1,2},{2,1},{3,0},{4,5},{5,4},{6,7},{7,6},{8,11},{9,10},{10,... | collective-permute-start | bytes 2359304 | tf_op jit(solution)/shard_map/ppermute | solution.py:29
  7.7 16.8 %collective-permute-start = (bf16[544,512]{1,0:T(8,128)(2,1)}, bf16[544,512]{1,0:T(8,128)(2,1)}, u32[]{:S(2)}, u32[]{:S(2)}) collective-permute-start(bf16[544,512]{1,0:T(8,128)(2,1)} %fusion.1), channel_id=1, source_target_pairs={{16,8},{17,9},{18,10},{19,11},{20,12},{21,13},{22,14},{23,15},{24,... | collective-permute-start | bytes 1671176 | tf_op jit(solution)/shard_map/ppermute | solution.py:29
  10.1 7.8 %collective-permute-start.1 = (bf16[512,512]{1,0:T(8,128)(2,1)S(1)}, bf16[512,512]{1,0:T(8,128)(2,1)S(1)}, u32[]{:S(2)}, u32[]{:S(2)}) collective-permute-start(bf16[512,512]{1,0:T(8,128)(2,1)S(1)} %bitcast.24), channel_id=1, source_target_pairs={{0,4},{1,5},{2,6},{3,7},{4,0},{5,1},{6,2},{7,3},{8,12},{9,13},{10,... | collective-permute-start | bytes 1572872 | tf_op jit(solution)/shard_map/ppermute | solution.py:29
  10.3 36.3 %collective-permute-start.7 = (s32[768]{0:T(1024)S(1)}, s32[768]{0:T(1024)S(1)}, u32[]{:S(2)}, u32[]{:S(2)}) collective-permute-start(s32[768]{0:T(1024)S(1)} %dynamic_slice.32), channel_id=1, source_target_pairs={{0,8},{1,12},{2,0},{3,4},{4,9},{5,13},{6,1},{7,5},{8,10},{9,14},{1... | collective-permute-start | bytes 9224 | tf_op jit(solution)/shard_map/ppermute | solution.py:29
  13.9 13.8 %copy-start.8 = (bf16[768,512]{1,0:T(8,128)(2,1)}, bf16[768,512]{1,0:T(8,128)(2,1)S(1)}, u32[]{:S(2)}) copy-start(bf16[768,512]{1,0:T(8,128)(2,1)S(1)} %get-tuple-element.50) | copy-start | bytes 2359300
  17.9 0.8 copy-start.3
  24.4 0.9 copy-start.10
  25.3 21.3 %collective-permute-start.4 = (bf16[544,512]{1,0:T(8,128)(2,1)}, bf16[544,512]{1,0:T(8,128)(2,1)}, u32[]{:S(2)}, u32[]{:S(2)}) collective-permute-start(bf16[544,512]{1,0:T(8,128)(2,1)} %collective-permute-done), channel_id=1, source_target_pairs={{0,8},{1,9},{2,10},{3,11},{4,12},{5,13},{6,14},{7,15},{8,0},{9,1},... | collective-permute-start | bytes 1671176 | tf_op jit(solution)/shard_map/ppermute | solution.py:29
  27.7 11.9 %collective-permute-start.5 = (bf16[512,3072]{1,0:T(8,128)(2,1)}, bf16[512,3072]{1,0:T(8,128)(2,1)S(1)}, u32[]{:S(2)}, u32[]{:S(2)}) collective-permute-start(bf16[512,3072]{1,0:T(8,128)(2,1)} %constant_dynamic-slice_fusion.3), channel_id=1, source_target_pairs={{0,4},{1,5},{2,6},{3,7},{4,0},{5,1},{6,2},{7,3},{8,12},{9,13},{10,... | collective-permute-start | bytes 9437192 | tf_op jit(solution)/shard_map/ppermute | solution.py:29
  30.5 43.1 %collective-permute-start.9 = (bf16[1664,512]{1,0:T(8,128)(2,1)}, bf16[1664,512]{1,0:T(8,128)(2,1)}, u32[]{:S(2)}, u32[]{:S(2)}) collective-permute-start(bf16[1664,512]{1,0:T(8,128)(2,1)} %pad_maximum_fusion.1), channel_id=1, source_target_pairs={{16,8},{17,9},{18,10},{19,11},{20,12},{21,13},{22,14},{23,15},{24,... | collective-permute-start | bytes 5111816 | tf_op jit(solution)/shard_map/ppermute | solution.py:29
  32.4 22.0 %collective-permute-start.13 = (bf16[768,512]{1,0:T(8,128)(2,1)}, bf16[768,512]{1,0:T(8,128)(2,1)}, u32[]{:S(2)}, u32[]{:S(2)}) collective-permute-start(bf16[768,512]{1,0:T(8,128)(2,1)} %get-tuple-element.55), channel_id=1, source_target_pairs={{0,2},{1,3},{2,0},{3,1},{4,6},{5,7},{6,4},{7,5},{8,10},{9,11},{10,... | collective-permute-start | bytes 2359304 | tf_op jit(solution)/shard_map/ppermute | solution.py:29
  34.7 4.9 %copy-start.1 = (bf16[1,512,512]{2,1,0:T(8,128)(2,1)S(1)}, bf16[1,512,512]{2,1,0:T(8,128)(2,1)}, u32[]{:S(2)}) copy-start(bf16[1,512,512]{2,1,0:T(8,128)(2,1)} %param.7) | copy-start | bytes 1572868
  34.7 4.9 %copy-start.4 = (bf16[512,512]{1,0:T(8,128)(2,1)S(1)}, bf16[512,512]{1,0:T(8,128)(2,1)}, u32[]{:S(2)}) copy-start(bf16[512,512]{1,0:T(8,128)(2,1)} %copy-done.3) | copy-start | bytes 1572868
  46.6 1.6 copy-start.9
  47.9 26.9 %collective-permute-start.8 = (bf16[1024,512]{1,0:T(8,128)(2,1)S(1)}, bf16[1024,512]{1,0:T(8,128)(2,1)S(1)}, u32[]{:S(2)}, u32[]{:S(2)}) collective-permute-start(bf16[1024,512]{1,0:T(8,128)(2,1)S(1)} %get-tuple-element.77.refs_0_), channel_id=1, source_target_pairs={{0,1},{1,0},{2,3},{3,2},{4,7},{5,6},{6,5},{7,4},{8,9},{9,8},{10,11... | collective-permute-start | bytes 3145736 | tf_op jit(solution)/shard_map/ppermute | solution.py:29
  48.2 74.3 %collective-permute-start.6 = (bf16[3072,512]{1,0:T(8,128)(2,1)}, bf16[3072,512]{1,0:T(8,128)(2,1)}, u32[]{:S(2)}, u32[]{:S(2)}) collective-permute-start(bf16[3072,512]{1,0:T(8,128)(2,1)} %weight_product.2), channel_id=1, source_target_pairs={{0,8},{1,9},{2,10},{3,11},{4,12},{5,13},{6,14},{7,15},{8,0},{9,1},... | collective-permute-start | bytes 9437192 | tf_op jit(solution)/shard_map/ppermute | solution.py:29
  49.9 57.5 %collective-permute-start.12 = (bf16[512,3072]{1,0:T(8,128)(2,1)}, bf16[512,3072]{1,0:T(8,128)(2,1)}, u32[]{:S(2)}, u32[]{:S(2)}) collective-permute-start(bf16[512,3072]{1,0:T(8,128)(2,1)} %constant_dynamic-slice_fusion), channel_id=1, source_target_pairs={{0,4},{1,5},{2,6},{3,7},{4,0},{5,1},{6,2},{7,3},{8,12},{9,13},{10,... | collective-permute-start | bytes 9437192 | tf_op jit(solution)/shard_map/ppermute | solution.py:29
  55.6 48.4 %collective-permute-start.14 = (bf16[1408,512]{1,0:T(8,128)(2,1)S(1)}, bf16[1408,512]{1,0:T(8,128)(2,1)S(1)}, u32[]{:S(2)}, u32[]{:S(2)}) collective-permute-start(bf16[1408,512]{1,0:T(8,128)(2,1)S(1)} %pad_maximum_fusion.2), channel_id=1, source_target_pairs={{16,8},{17,9},{18,10},{19,11},{20,12},{21,13},{22,14},{23,15},{24,... | collective-permute-start | bytes 4325384 | tf_op jit(solution)/shard_map/ppermute | solution.py:29
  73.6 1.2 collective-permute-start.10
  74.7 0.6 copy-start.15
  76.9 30.5 %collective-permute-start.11 = (bf16[2,1024,512]{2,1,0:T(8,128)(2,1)}, bf16[2,1024,512]{2,1,0:T(8,128)(2,1)}, u32[]{:S(2)}, u32[]{:S(2)}) collective-permute-start(bf16[2,1024,512]{2,1,0:T(8,128)(2,1)} %pad_maximum_fusion), channel_id=1, source_target_pairs={{0,3},{1,2},{2,1},{3,0},{4,5},{5,4},{6,7},{7,6},{8,11},{9,10},{10,... | collective-permute-start | bytes 6291464 | tf_op jit(solution)/shard_map/ppermute | solution.py:29
  77.4 28.2 %collective-permute-start.15 = (bf16[1664,512]{1,0:T(8,128)(2,1)}, bf16[1664,512]{1,0:T(8,128)(2,1)}, u32[]{:S(2)}, u32[]{:S(2)}) collective-permute-start(bf16[1664,512]{1,0:T(8,128)(2,1)} %collective-permute-done.9.refs_3_), channel_id=1, source_target_pairs={{0,4},{1,5},{2,6},{3,7},{4,0},{5,1},{6,2},{7,3},{8,12},{9,13},{10,... | collective-permute-start | bytes 5111816 | tf_op jit(solution)/shard_map/ppermute | solution.py:29
  104.0 3.4 %copy-start.6 = (bf16[1408,512]{1,0:T(8,128)(2,1)}, bf16[1408,512]{1,0:T(8,128)(2,1)S(1)}, u32[]{:S(2)}) copy-start(bf16[1408,512]{1,0:T(8,128)(2,1)S(1)} %collective-permute-done.14.refs_4_) | copy-start | bytes 4325380
  104.0 3.4 %collective-permute-start.16 = (bf16[1408,512]{1,0:T(8,128)(2,1)S(1)}, bf16[1408,512]{1,0:T(8,128)(2,1)}, u32[]{:S(2)}, u32[]{:S(2)}) collective-permute-start(bf16[1408,512]{1,0:T(8,128)(2,1)S(1)} %collective-permute-done.14.refs_4_), channel_id=1, source_target_pairs={{0,4},{1,5},{2,6},{3,7},{4,0},{5,1},{6,2},{7,3},{8,12},{9,13},{10,... | collective-permute-start | bytes 4325384 | tf_op jit(solution)/shard_map/ppermute | solution.py:29
  107.3 1.4 copy-start.7
  108.7 20.4 %copy-start.12 = (f32[128,128]{1,0:T(8,128)S(1)}, f32[128,128]{1,0:T(8,128)}, u32[]{:S(2)}) copy-start(f32[128,128]{1,0:T(8,128)} %hadamard_signs.1) | copy-start | bytes 196612
  108.7 20.9 %copy-start.2 = (bf16[1,512,512]{2,1,0:T(8,128)(2,1)S(1)}, bf16[1,512,512]{2,1,0:T(8,128)(2,1)}, u32[]{:S(2)}) copy-start(bf16[1,512,512]{2,1,0:T(8,128)(2,1)} %param.7) | copy-start | bytes 1572868
  108.7 20.9 %copy-start.5 = (bf16[512,512]{1,0:T(8,128)(2,1)S(1)}, bf16[512,512]{1,0:T(8,128)(2,1)}, u32[]{:S(2)}) copy-start(bf16[512,512]{1,0:T(8,128)(2,1)} %copy-done.3) | copy-start | bytes 1572868
  119.9 20.8 %collective-permute-start.19 = (bf16[768,512]{1,0:T(8,128)(2,1)}, bf16[768,512]{1,0:T(8,128)(2,1)}, u32[]{:S(2)}, u32[]{:S(2)}) collective-permute-start(bf16[768,512]{1,0:T(8,128)(2,1)} %get-tuple-element.69), channel_id=1, source_target_pairs={{0,2},{1,3},{2,10},{3,11},{4,6},{5,7},{6,14},{7,15},{8,0},{9,1},{1... | collective-permute-start | bytes 2359304 | tf_op jit(solution)/shard_map/ppermute | solution.py:29
  121.6 36.3 %collective-permute-start.20 = (bf16[768,512]{1,0:T(8,128)(2,1)}, bf16[768,512]{1,0:T(8,128)(2,1)}, u32[]{:S(2)}, u32[]{:S(2)}) collective-permute-start(bf16[768,512]{1,0:T(8,128)(2,1)} %get-tuple-element.70), channel_id=1, source_target_pairs={{0,3},{1,2},{2,11},{3,10},{4,7},{5,6},{6,15},{7,14},{8,1},{9,0},{1... | collective-permute-start | bytes 2359304 | tf_op jit(solution)/shard_map/ppermute | solution.py:29
  122.5 38.4 %collective-permute-start.17 = (bf16[768,512]{1,0:T(8,128)(2,1)}, bf16[768,512]{1,0:T(8,128)(2,1)S(1)}, u32[]{:S(2)}, u32[]{:S(2)}) collective-permute-start(bf16[768,512]{1,0:T(8,128)(2,1)} %get-tuple-element.64), channel_id=1, source_target_pairs={{0,10},{1,11},{2,2},{3,3},{4,14},{5,15},{6,6},{7,7},{8,8},{9,9},{1... | collective-permute-start | bytes 2359304 | tf_op jit(solution)/shard_map/ppermute | solution.py:29
  127.2 35.7 %collective-permute-start.18 = (bf16[768,512]{1,0:T(8,128)(2,1)}, bf16[768,512]{1,0:T(8,128)(2,1)S(1)}, u32[]{:S(2)}, u32[]{:S(2)}) collective-permute-start(bf16[768,512]{1,0:T(8,128)(2,1)} %get-tuple-element.65), channel_id=1, source_target_pairs={{0,11},{1,10},{2,3},{3,2},{4,15},{5,14},{6,7},{7,6},{8,9},{9,8},{1... | collective-permute-start | bytes 2359304 | tf_op jit(solution)/shard_map/ppermute | solution.py:29

commit v6 on v5

--- a/solution.py
+++ b/solution.py
@@ -60,19 +60,23 @@
     return lax.optimization_barrier((value, *others))[0]
 
 
-def rotated_rows(pair, rest, table_ref, grads_refs, swapped, far):
+def rotated_rows(pair, rest, table_ref, grads_refs, swapped, far, waits):
     held_ref, a_ref, b_ref = grads_refs
     rows, tokens = pair.shape[0] // 2, held_ref.shape[0] // 2
     at = slice(far * tokens, (far + 1) * tokens)
     first, second = slice(0, rows), slice(rows, 2 * rows)
     total = None
-    for weight, grads in (
-        (rest[first, :], held_ref[at, :]),
-        (pair[second if swapped else first, :], a_ref[at, :]),
-        (pair[first if swapped else second, :], b_ref[0, at, :]),
-        (rest[second, :], b_ref[1, at, :]),
+    for wait, weight, row, (grads_ref, index) in zip(
+        waits,
+        (rest, pair, pair, rest),
+        (first, second if swapped else first, first if swapped else second, second),
+        ((held_ref, (at,)), (a_ref, (at,)), (b_ref, (0, at)), (b_ref, (1, at))),
     ):
-        term = lax.dot_general(weight, grads, (((1,), (1,)), ((), ())), preferred_element_type=jnp.float32)
+        for fetch in wait:
+            fetch.wait()
+        term = lax.dot_general(
+            weight[row, :], grads_ref[index], (((1,), (1,)), ((), ())), preferred_element_type=jnp.float32
+        )
         total = term if total is None else total + term
     high = total.astype(jnp.bfloat16)
     low = (total - high.astype(jnp.float32)).astype(jnp.bfloat16)
@@ -87,10 +91,12 @@
     base = base_ref[0]
     given, outs, inside, made, come, gone = refs[:7], refs[7:11], refs[11:18], refs[18], refs[19], refs[20]
     extra = given[3].shape[0] - inside[3].shape[0]
-    moves = list(zip(given[:3], inside[:3]))
+    moves = []
     for pair, rest, pair_in, rest_in in ((*given[3:5], *inside[3:5]), (*given[5:], *inside[5:])):
-        held = pair_in.shape[0]
-        moves += [(pair.at[:held, :], pair_in), (pair.at[held:, :], rest_in.at[:extra, :]), (rest, rest_in.at[extra:, :])]
+        most = pair_in.shape[0]
+        moves += [(pair.at[most:, :], rest_in.at[:extra, :]), (rest, rest_in.at[extra:, :]), (pair.at[:most, :], pair_in)]
+    held, a, b = zip(given[:3], inside[:3])
+    moves = [held, *moves[:2], a, moves[2], b, *moves[3:]]
     fetches = [pltpu.make_async_copy(far, near, come.at[i]) for i, (far, near) in enumerate(moves)]
     for fetch in fetches:
         fetch.start()
@@ -101,9 +107,8 @@
             yield jnp.bitwise_xor(base, k) == r, pltpu.make_async_copy(made.at[k], out_ref, gone.at[k])
 
     for step, k in enumerate((0, 2, 1, 3)):
-        for fetch in {0: fetches[:6], 2: fetches[6:]}.get(step, ()):
-            fetch.wait()
-        done = rotated_rows(*weights[k % 2 * 2 : k % 2 * 2 + 2], table_ref.at[k % 2], grads, k % 2, k // 2)
+        waits = {0: (fetches[:3], fetches[3:5], fetches[5:6], ()), 2: (fetches[6:], (), (), ())}.get(step, ((),) * 4)
+        done = rotated_rows(*weights[k % 2 * 2 : k % 2 * 2 + 2], table_ref.at[k % 2], grads, k % 2, k // 2, waits)
         made[k] = done
         for here, copy in sends(k):
             pl.when(here)(copy.start)

time: 165 us -> 165 us (level)
  no operation moved by 1% of the time
where the time goes in v6:
time: 165 us; the launch traced here: 164 us
  waiting for transfers between devices  71.4 us (43%)
  Pallas kernels  33.7 us (20%)
  starting transfers between devices  30.7 us (19%)
  local copies, waits for them, and re-layouts  18 us (11%)
  other arithmetic  9.37 us (6%)
    ppermute x21, waiting for transfers between devices, send(): return lax.ppermute(shard, AXES, pairs)  71.4 us
    ppermute x21, starting transfers between devices, send(): return lax.ppermute(shard, AXES, pairs)  30.7 us
    pallas_call x2, Pallas kernels, product(): pl.pallas_call(product_kernel, out_shape=jax.ShapeDtypeStruct((rows, colu...  17.7 us
    pallas_call x1, Pallas kernels, rotate(): pl.pallas_call(rotate_kernel, out_shape=[jax.ShapeDtypeStruct((rows, toke...  10.8 us
    dynamic_slice x2, local copies, waits for them, and re-layouts, features(): return lax.dynamic_slice_in_dim(inputs, block * rows_here, rows_here, 1)  7.88 us
    pallas_call x2, Pallas kernels, back(): pl.pallas_call(functools.partial(back_kernel, rounds), out_shape=jax.Shap...  4.56 us
    dynamic_slice x2, local copies, waits for them, and re-layouts, quarter_for(): lax.dynamic_slice_in_dim(weight, jnp.bitwise_xor(tensor, x) * quarter, qu...  4 us
    unnamed x32, local copies, waits for them, and re-layouts  3.7 us
  transfers between devices with their start and end apart: 21, of which 9 were waited for; matrix products, arithmetic and copies ran while one was open for 13% of the time, Pallas kernels for 20%

profile of v6, /device:TPU:20, one launch (start us, length us, event | category | flops | bytes accessed | tf_op | source)
XLA Modules:
  0.0 164.3 jit_solution(8051873500345106543)
XLA Ops:
  0.7 1.6 dynamic-slice_bitcast_fusion
  2.3 2.0 %collective-permute-start.2 = (bf16[768,512]{1,0:T(8,128)(2,1)S(1)}, bf16[768,512]{1,0:T(8,128)(2,1)S(1)}, u32[]{:S(2)}, u32[]{:S(2)}) collective-permute-start(bf16[768,512]{1,0:T(8,128)(2,1)S(1)} %get-tuple-element.73), channel_id=1, source_target_pairs={{0,1},{1,0},{2,3},{3,2},{4,7},{5,6},{6,5},{7,4},{8,9},{9,8},{10,11... | collective-permute-start | bytes 2359304 | tf_op jit(solution)/shard_map/ppermute | solution.py:29
  4.3 2.5 %collective-permute-start.3 = (bf16[768,512]{1,0:T(8,128)(2,1)S(1)}, bf16[768,512]{1,0:T(8,128)(2,1)}, u32[]{:S(2)}, u32[]{:S(2)}) collective-permute-start(bf16[768,512]{1,0:T(8,128)(2,1)S(1)} %get-tuple-element.72), channel_id=1, source_target_pairs={{0,3},{1,2},{2,1},{3,0},{4,5},{5,4},{6,7},{7,6},{8,11},{9,10},{10,... | collective-permute-start | bytes 2359304 | tf_op jit(solution)/shard_map/ppermute | solution.py:29
  6.8 0.8 fusion.1
  7.7 2.4 %collective-permute-start = (bf16[544,512]{1,0:T(8,128)(2,1)}, bf16[544,512]{1,0:T(8,128)(2,1)}, u32[]{:S(2)}, u32[]{:S(2)}) collective-permute-start(bf16[544,512]{1,0:T(8,128)(2,1)} %fusion.1), channel_id=1, source_target_pairs={{16,8},{17,9},{18,10},{19,11},{20,12},{21,13},{22,14},{23,15},{24,... | collective-permute-start | bytes 1671176 | tf_op jit(solution)/shard_map/ppermute | solution.py:29
  10.3 1.1 collective-permute-start.7
  11.4 2.4 %constant_dynamic-slice_fusion.1 = (bf16[768,512]{1,0:T(8,128)(2,1)}, bf16[768,512]{1,0:T(8,128)(2,1)S(1)}) fusion(bf16[3072,512]{1,0:T(8,128)(2,1)} %bitcast.33, s32[]{:T(128)S(6)} %select_n.24, s32[]{:T(128)S(6)} %select_n.23), kind=kLoop, calls=%fused_computation.20 | loop fusion | bytes 3145736 | tf_op jit(solution)/shard_map/dynamic_slice | solution.py:235
  13.9 4.0 %constant_dynamic-slice_fusion.3 = bf16[512,3072]{1,0:T(8,128)(2,1)} fusion(bf16[512,12288]{1,0:T(8,128)(2,1)} %bitcast.27, s32[]{:T(128)S(6)} %select_n.22), kind=kLoop, calls=%fused_computation.22 | loop fusion | bytes 6291460 | tf_op jit(solution)/shard_map/dynamic_slice | solution.py:226
  17.9 0.8 copy-done.3
  18.8 5.7 %collective-permute-done = bf16[544,512]{1,0:T(8,128)(2,1)} collective-permute-done((bf16[544,512]{1,0:T(8,128)(2,1)}, bf16[544,512]{1,0:T(8,128)(2,1)}, u32[]{:S(2)}, u32[]{:S(2)}) %collective-permute-start) | collective-permute-done | bytes 557088 | tf_op jit(solution)/shard_map/ppermute | solution.py:29
  24.4 0.9 copy-done.10
  25.3 2.4 %collective-permute-start.4 = (bf16[544,512]{1,0:T(8,128)(2,1)}, bf16[544,512]{1,0:T(8,128)(2,1)}, u32[]{:S(2)}, u32[]{:S(2)}) collective-permute-start(bf16[544,512]{1,0:T(8,128)(2,1)} %collective-permute-done), channel_id=1, source_target_pairs={{0,8},{1,9},{2,10},{3,11},{4,12},{5,13},{6,14},{7,15},{8,0},{9,1},... | collective-permute-start | bytes 1671176 | tf_op jit(solution)/shard_map/ppermute | solution.py:29
  27.7 2.7 %pad_maximum_fusion.1 = bf16[1664,512]{1,0:T(8,128)(2,1)} fusion(bf16[128,512]{1,0:T(8,128)(2,1)S(1)} %slice.17, bf16[768,512]{1,0:T(8,128)(2,1)} %collective-permute-done.3, bf16[768,512]{1,0:T(8,128)(2,1)} %copy-done.10), kind=kLoop, calls=%fused_computation.1 | loop fusion | flops 5111808 | bytes 3407872 | tf_op jit(solution)/shard_map/concatenate | solution.py:259
  30.5 1.9 %collective-permute-start.9 = (bf16[1664,512]{1,0:T(8,128)(2,1)}, bf16[1664,512]{1,0:T(8,128)(2,1)}, u32[]{:S(2)}, u32[]{:S(2)}) collective-permute-start(bf16[1664,512]{1,0:T(8,128)(2,1)} %pad_maximum_fusion.1), channel_id=1, source_target_pairs={{16,8},{17,9},{18,10},{19,11},{20,12},{21,13},{22,14},{23,15},{24,... | collective-permute-start | bytes 5111816 | tf_op jit(solution)/shard_map/ppermute | solution.py:29
  32.4 1.6 collective-permute-start.13
  34.0 0.7 hadamard_signs.1
  34.7 3.8 %constant_dynamic-slice_fusion = bf16[512,3072]{1,0:T(8,128)(2,1)} fusion(bf16[512,12288]{1,0:T(8,128)(2,1)} %bitcast.28, s32[]{:T(128)S(6)} %select_n.27), kind=kLoop, calls=%fused_computation.19 | loop fusion | bytes 6291460 | tf_op jit(solution)/shard_map/dynamic_slice | solution.py:226
  38.5 1.1 slice.16
  39.7 6.9 %weight_product.2 = bf16[3072,512]{1,0:T(8,128)(2,1)} custom-call(s32[1]{0:T(128)} %bitcast.8.block_ref, bf16[512,12288]{1,0:T(8,128)(2,1)} %bitcast.29, bf16[512,3072]{1,0:T(8,128)(2,1)S(1)} %collective-permute-done.5.got_ref, bf16[512,512]{1,0:T(8,128)(2,1)S(1)} %bitcast.25, bf16[512,512]{1,0:T(8,128)(2,1)S(1)} %copy-done.4), custom_call_target="tpu_custom_call" | custom-call | tf_op jit(solution)/shard_map/weight_product/pallas_call | solution.py:202
  46.6 1.1 slice.15
  48.2 1.7 %collective-permute-start.6 = (bf16[3072,512]{1,0:T(8,128)(2,1)}, bf16[3072,512]{1,0:T(8,128)(2,1)}, u32[]{:S(2)}, u32[]{:S(2)}) collective-permute-start(bf16[3072,512]{1,0:T(8,128)(2,1)} %weight_product.2), channel_id=1, source_target_pairs={{0,8},{1,9},{2,10},{3,11},{4,12},{5,13},{6,14},{7,15},{8,0},{9,1},... | collective-permute-start | bytes 9437192 | tf_op jit(solution)/shard_map/ppermute | solution.py:29
  49.9 1.1 collective-permute-start.12
  51.0 3.3 %collective-permute-done.13 = bf16[768,512]{1,0:T(8,128)(2,1)} collective-permute-done((bf16[768,512]{1,0:T(8,128)(2,1)}, bf16[768,512]{1,0:T(8,128)(2,1)}, u32[]{:S(2)}, u32[]{:S(2)}) %collective-permute-start.13) | collective-permute-done | bytes 786464 | tf_op jit(solution)/shard_map/ppermute | solution.py:29
  54.3 1.2 pad_maximum_fusion.2
  55.6 3.5 %collective-permute-start.14 = (bf16[1408,512]{1,0:T(8,128)(2,1)S(1)}, bf16[1408,512]{1,0:T(8,128)(2,1)S(1)}, u32[]{:S(2)}, u32[]{:S(2)}) collective-permute-start(bf16[1408,512]{1,0:T(8,128)(2,1)S(1)} %pad_maximum_fusion.2), channel_id=1, source_target_pairs={{16,8},{17,9},{18,10},{19,11},{20,12},{21,13},{22,14},{23,15},{24,... | collective-permute-start | bytes 4325384 | tf_op jit(solution)/shard_map/ppermute | solution.py:29
  59.1 14.5 %collective-permute-done.9.refs_3_ = bf16[1664,512]{1,0:T(8,128)(2,1)} collective-permute-done((bf16[1664,512]{1,0:T(8,128)(2,1)}, bf16[1664,512]{1,0:T(8,128)(2,1)}, u32[]{:S(2)}, u32[]{:S(2)}) %collective-permute-start.9) | collective-permute-done | bytes 1703968 | tf_op jit(solution)/shard_map/ppermute | solution.py:29
  73.6 1.2 collective-permute-done.10
  74.7 0.6 copy-done.15
  75.3 1.6 pad_maximum_fusion
  76.9 0.5 collective-permute-start.11
  77.4 1.1 collective-permute-start.15
  78.5 25.5 %collective-permute-done.14.refs_4_ = bf16[1408,512]{1,0:T(8,128)(2,1)S(1)} collective-permute-done((bf16[1408,512]{1,0:T(8,128)(2,1)S(1)}, bf16[1408,512]{1,0:T(8,128)(2,1)S(1)}, u32[]{:S(2)}, u32[]{:S(2)}) %collective-permute-start.14) | collective-permute-done | bytes 1441824 | tf_op jit(solution)/shard_map/ppermute | solution.py:29
  104.0 0.7 fusion.4
  104.7 0.9 multiply_convert_fusion.1
  105.7 1.7 %collective-permute-done.16.refs_6_ = bf16[1408,512]{1,0:T(8,128)(2,1)} collective-permute-done((bf16[1408,512]{1,0:T(8,128)(2,1)S(1)}, bf16[1408,512]{1,0:T(8,128)(2,1)}, u32[]{:S(2)}, u32[]{:S(2)}) %collective-permute-start.16) | collective-permute-done | bytes 1441824 | tf_op jit(solution)/shard_map/ppermute | solution.py:29
  107.4 1.4 copy-done.7
  108.7 10.8 %rotate.1 = (bf16[768,512]{1,0:T(8,128)(2,1)}, bf16[768,512]{1,0:T(8,128)(2,1)}, bf16[768,512]{1,0:T(8,128)(2,1)}, bf16[768,512]{1,0:T(8,128)(2,1)}) custom-call(s32[1]{0:T(128)} %bitcast.9.base_ref, bf16[2,6,128,256]{3,2,1,0:T(8,128)(2,1)S(1)} %pad_maximum_fusion.4.table_ref, bf16[1024,512]{1,0:T(8,128)(2,1)S(1)} %get-tuple-element.77.refs_0_, ...), custom_call_target="tpu_custom_call" | custom-call | tf_op jit(solution)/shard_map/rotate/pallas_call | solution.py:124
  119.5 1.7 %collective-permute-start.19 = (bf16[768,512]{1,0:T(8,128)(2,1)}, bf16[768,512]{1,0:T(8,128)(2,1)}, u32[]{:S(2)}, u32[]{:S(2)}) collective-permute-start(bf16[768,512]{1,0:T(8,128)(2,1)} %get-tuple-element.69), channel_id=1, source_target_pairs={{0,2},{1,3},{2,10},{3,11},{4,6},{5,7},{6,14},{7,15},{8,0},{9,1},{1... | collective-permute-start | bytes 2359304 | tf_op jit(solution)/shard_map/ppermute | solution.py:29
  121.1 0.9 collective-permute-start.20
  122.1 4.7 %collective-permute-start.17 = (bf16[768,512]{1,0:T(8,128)(2,1)}, bf16[768,512]{1,0:T(8,128)(2,1)S(1)}, u32[]{:S(2)}, u32[]{:S(2)}) collective-permute-start(bf16[768,512]{1,0:T(8,128)(2,1)} %get-tuple-element.64), channel_id=1, source_target_pairs={{0,10},{1,11},{2,2},{3,3},{4,14},{5,15},{6,6},{7,7},{8,8},{9,9},{1... | collective-permute-start | bytes 2359304 | tf_op jit(solution)/shard_map/ppermute | solution.py:29
  126.8 1.1 collective-permute-start.18
  127.8 0.7 slice_convert_fusion
  128.6 0.5 multiply_convert_fusion.refs_3_
  129.1 10.8 %weight_product.3 = f32[3072,512]{1,0:T(8,128)} custom-call(s32[1]{0:T(128)} %bitcast.14.block_ref, bf16[512,12288]{1,0:T(8,128)(2,1)} %bitcast.30, bf16[512,3072]{1,0:T(8,128)(2,1)} %collective-permute-done.12.got_ref, bf16[512,512]{1,0:T(8,128)(2,1)S(1)} %bitcast.26, bf16[512,512]{1,0:T(8,128)(2,1)S(1)} %copy-done.5, ...), custom_call_target="tpu_custom_call" | custom-call | tf_op jit(solution)/shard_map/weight_product/pallas_call | solution.py:202
  140.2 17.2 %collective-permute-done.20.refs_1_ = bf16[768,512]{1,0:T(8,128)(2,1)} collective-permute-done((bf16[768,512]{1,0:T(8,128)(2,1)}, bf16[768,512]{1,0:T(8,128)(2,1)}, u32[]{:S(2)}, u32[]{:S(2)}) %collective-permute-start.20) | collective-permute-done | bytes 786464 | tf_op jit(solution)/shard_map/ppermute | solution.py:29
  157.5 3.0 %rotate_back.2.refs_4_ = bf16[3072,512]{1,0:T(8,128)(2,1)} custom-call(s32[1]{0:T(128)} %bitcast.here_ref, bf16[768,512]{1,0:T(8,128)(2,1)} %collective-permute-done.19.refs_0_, bf16[768,512]{1,0:T(8,128)(2,1)} %collective-permute-done.20.refs_1_, f32[24,1,512]{2,1,0:T(1,128)S(1)} %reshape.59.refs_2_, bf16[24,128,128]{2,1,0:T(8,128)(2,1)S(1)} %multiply_convert_fusion.refs_3_), custom_call_target="tpu_custom_call" | custom-call | tf_op jit(solution)/shard_map/rotate_back/pallas_call | solution.py:162
  160.5 2.0 %collective-permute-done.18.refs_1_ = bf16[768,512]{1,0:T(8,128)(2,1)S(1)} collective-permute-done((bf16[768,512]{1,0:T(8,128)(2,1)}, bf16[768,512]{1,0:T(8,128)(2,1)S(1)}, u32[]{:S(2)}, u32[]{:S(2)}) %collective-permute-start.18) | collective-permute-done | bytes 786464 | tf_op jit(solution)/shard_map/ppermute | solution.py:29
  162.5 1.6 rotate_back.3
  (54 shorter events, 1.2 us)
Async XLA Ops:
  0.6 6.1 %copy-start.13 = (s32[1,24,512]{2,1,0:T(8,128)S(1)}, s32[1,24,512]{2,1,0:T(8,128)}, u32[]{:S(2)}) copy-start(s32[1,24,512]{2,1,0:T(8,128)} %param.10) | copy-start | bytes 147460
  0.6 6.2 %copy-start.11 = (bf16[1,512,512]{2,1,0:T(8,128)(2,1)S(1)}, bf16[1,512,512]{2,1,0:T(8,128)(2,1)}, u32[]{:S(2)}) copy-start(bf16[1,512,512]{2,1,0:T(8,128)(2,1)} %param.8) | copy-start | bytes 1572868
  0.7 9.4 %copy-start = (bf16[1,512,512]{2,1,0:T(8,128)(2,1)S(1)}, bf16[1,512,512]{2,1,0:T(8,128)(2,1)}, u32[]{:S(2)}) copy-start(bf16[1,512,512]{2,1,0:T(8,128)(2,1)} %param.7) | copy-start | bytes 1572868
  0.7 9.5 %copy-start.14 = (s32[3072]{0:T(1024)S(1)}, s32[3072]{0:T(1024)}, u32[]{:S(2)}) copy-start(s32[3072]{0:T(1024)} %param.11) | copy-start | bytes 36868
  2.3 22.2 %collective-permute-start.2 = (bf16[768,512]{1,0:T(8,128)(2,1)S(1)}, bf16[768,512]{1,0:T(8,128)(2,1)S(1)}, u32[]{:S(2)}, u32[]{:S(2)}) collective-permute-start(bf16[768,512]{1,0:T(8,128)(2,1)S(1)} %get-tuple-element.73), channel_id=1, source_target_pairs={{0,1},{1,0},{2,3},{3,2},{4,7},{5,6},{6,5},{7,4},{8,9},{9,8},{10,11... | collective-permute-start | bytes 2359304 | tf_op jit(solution)/shard_map/ppermute | solution.py:29
  4.3 20.2 %collective-permute-start.3 = (bf16[768,512]{1,0:T(8,128)(2,1)S(1)}, bf16[768,512]{1,0:T(8,128)(2,1)}, u32[]{:S(2)}, u32[]{:S(2)}) collective-permute-start(bf16[768,512]{1,0:T(8,128)(2,1)S(1)} %get-tuple-element.72), channel_id=1, source_target_pairs={{0,3},{1,2},{2,1},{3,0},{4,5},{5,4},{6,7},{7,6},{8,11},{9,10},{10,... | collective-permute-start | bytes 2359304 | tf_op jit(solution)/shard_map/ppermute | solution.py:29
  7.7 16.8 %collective-permute-start = (bf16[544,512]{1,0:T(8,128)(2,1)}, bf16[544,512]{1,0:T(8,128)(2,1)}, u32[]{:S(2)}, u32[]{:S(2)}) collective-permute-start(bf16[544,512]{1,0:T(8,128)(2,1)} %fusion.1), channel_id=1, source_target_pairs={{16,8},{17,9},{18,10},{19,11},{20,12},{21,13},{22,14},{23,15},{24,... | collective-permute-start | bytes 1671176 | tf_op jit(solution)/shard_map/ppermute | solution.py:29
  10.1 7.8 %collective-permute-start.1 = (bf16[512,512]{1,0:T(8,128)(2,1)S(1)}, bf16[512,512]{1,0:T(8,128)(2,1)S(1)}, u32[]{:S(2)}, u32[]{:S(2)}) collective-permute-start(bf16[512,512]{1,0:T(8,128)(2,1)S(1)} %bitcast.24), channel_id=1, source_target_pairs={{0,4},{1,5},{2,6},{3,7},{4,0},{5,1},{6,2},{7,3},{8,12},{9,13},{10,... | collective-permute-start | bytes 1572872 | tf_op jit(solution)/shard_map/ppermute | solution.py:29
  10.3 36.3 %collective-permute-start.7 = (s32[768]{0:T(1024)S(1)}, s32[768]{0:T(1024)S(1)}, u32[]{:S(2)}, u32[]{:S(2)}) collective-permute-start(s32[768]{0:T(1024)S(1)} %dynamic_slice.32), channel_id=1, source_target_pairs={{0,8},{1,12},{2,0},{3,4},{4,9},{5,13},{6,1},{7,5},{8,10},{9,14},{1... | collective-permute-start | bytes 9224 | tf_op jit(solution)/shard_map/ppermute | solution.py:29
  13.9 13.8 %copy-start.8 = (bf16[768,512]{1,0:T(8,128)(2,1)}, bf16[768,512]{1,0:T(8,128)(2,1)S(1)}, u32[]{:S(2)}) copy-start(bf16[768,512]{1,0:T(8,128)(2,1)S(1)} %get-tuple-element.50) | copy-start | bytes 2359300
  17.9 0.8 copy-start.3
  24.4 0.9 copy-start.10
  25.3 21.3 %collective-permute-start.4 = (bf16[544,512]{1,0:T(8,128)(2,1)}, bf16[544,512]{1,0:T(8,128)(2,1)}, u32[]{:S(2)}, u32[]{:S(2)}) collective-permute-start(bf16[544,512]{1,0:T(8,128)(2,1)} %collective-permute-done), channel_id=1, source_target_pairs={{0,8},{1,9},{2,10},{3,11},{4,12},{5,13},{6,14},{7,15},{8,0},{9,1},... | collective-permute-start | bytes 1671176 | tf_op jit(solution)/shard_map/ppermute | solution.py:29
  27.7 11.9 %collective-permute-start.5 = (bf16[512,3072]{1,0:T(8,128)(2,1)}, bf16[512,3072]{1,0:T(8,128)(2,1)S(1)}, u32[]{:S(2)}, u32[]{:S(2)}) collective-permute-start(bf16[512,3072]{1,0:T(8,128)(2,1)} %constant_dynamic-slice_fusion.3), channel_id=1, source_target_pairs={{0,4},{1,5},{2,6},{3,7},{4,0},{5,1},{6,2},{7,3},{8,12},{9,13},{10,... | collective-permute-start | bytes 9437192 | tf_op jit(solution)/shard_map/ppermute | solution.py:29
  30.5 43.1 %collective-permute-start.9 = (bf16[1664,512]{1,0:T(8,128)(2,1)}, bf16[1664,512]{1,0:T(8,128)(2,1)}, u32[]{:S(2)}, u32[]{:S(2)}) collective-permute-start(bf16[1664,512]{1,0:T(8,128)(2,1)} %pad_maximum_fusion.1), channel_id=1, source_target_pairs={{16,8},{17,9},{18,10},{19,11},{20,12},{21,13},{22,14},{23,15},{24,... | collective-permute-start | bytes 5111816 | tf_op jit(solution)/shard_map/ppermute | solution.py:29
  32.4 22.0 %collective-permute-start.13 = (bf16[768,512]{1,0:T(8,128)(2,1)}, bf16[768,512]{1,0:T(8,128)(2,1)}, u32[]{:S(2)}, u32[]{:S(2)}) collective-permute-start(bf16[768,512]{1,0:T(8,128)(2,1)} %get-tuple-element.55), channel_id=1, source_target_pairs={{0,2},{1,3},{2,0},{3,1},{4,6},{5,7},{6,4},{7,5},{8,10},{9,11},{10,... | collective-permute-start | bytes 2359304 | tf_op jit(solution)/shard_map/ppermute | solution.py:29
  34.7 4.9 %copy-start.1 = (bf16[1,512,512]{2,1,0:T(8,128)(2,1)S(1)}, bf16[1,512,512]{2,1,0:T(8,128)(2,1)}, u32[]{:S(2)}) copy-start(bf16[1,512,512]{2,1,0:T(8,128)(2,1)} %param.7) | copy-start | bytes 1572868
  34.7 4.9 %copy-start.4 = (bf16[512,512]{1,0:T(8,128)(2,1)S(1)}, bf16[512,512]{1,0:T(8,128)(2,1)}, u32[]{:S(2)}) copy-start(bf16[512,512]{1,0:T(8,128)(2,1)} %copy-done.3) | copy-start | bytes 1572868
  46.6 1.6 copy-start.9
  47.9 26.9 %collective-permute-start.8 = (bf16[1024,512]{1,0:T(8,128)(2,1)S(1)}, bf16[1024,512]{1,0:T(8,128)(2,1)S(1)}, u32[]{:S(2)}, u32[]{:S(2)}) collective-permute-start(bf16[1024,512]{1,0:T(8,128)(2,1)S(1)} %get-tuple-element.77.refs_0_), channel_id=1, source_target_pairs={{0,1},{1,0},{2,3},{3,2},{4,7},{5,6},{6,5},{7,4},{8,9},{9,8},{10,11... | collective-permute-start | bytes 3145736 | tf_op jit(solution)/shard_map/ppermute | solution.py:29
  48.2 73.9 %collective-permute-start.6 = (bf16[3072,512]{1,0:T(8,128)(2,1)}, bf16[3072,512]{1,0:T(8,128)(2,1)}, u32[]{:S(2)}, u32[]{:S(2)}) collective-permute-start(bf16[3072,512]{1,0:T(8,128)(2,1)} %weight_product.2), channel_id=1, source_target_pairs={{0,8},{1,9},{2,10},{3,11},{4,12},{5,13},{6,14},{7,15},{8,0},{9,1},... | collective-permute-start | bytes 9437192 | tf_op jit(solution)/shard_map/ppermute | solution.py:29
  49.9 57.5 %collective-permute-start.12 = (bf16[512,3072]{1,0:T(8,128)(2,1)}, bf16[512,3072]{1,0:T(8,128)(2,1)}, u32[]{:S(2)}, u32[]{:S(2)}) collective-permute-start(bf16[512,3072]{1,0:T(8,128)(2,1)} %constant_dynamic-slice_fusion), channel_id=1, source_target_pairs={{0,4},{1,5},{2,6},{3,7},{4,0},{5,1},{6,2},{7,3},{8,12},{9,13},{10,... | collective-permute-start | bytes 9437192 | tf_op jit(solution)/shard_map/ppermute | solution.py:29
  55.6 48.4 %collective-permute-start.14 = (bf16[1408,512]{1,0:T(8,128)(2,1)S(1)}, bf16[1408,512]{1,0:T(8,128)(2,1)S(1)}, u32[]{:S(2)}, u32[]{:S(2)}) collective-permute-start(bf16[1408,512]{1,0:T(8,128)(2,1)S(1)} %pad_maximum_fusion.2), channel_id=1, source_target_pairs={{16,8},{17,9},{18,10},{19,11},{20,12},{21,13},{22,14},{23,15},{24,... | collective-permute-start | bytes 4325384 | tf_op jit(solution)/shard_map/ppermute | solution.py:29
  73.6 1.2 collective-permute-start.10
  74.7 0.6 copy-start.15
  76.9 30.5 %collective-permute-start.11 = (bf16[2,1024,512]{2,1,0:T(8,128)(2,1)}, bf16[2,1024,512]{2,1,0:T(8,128)(2,1)}, u32[]{:S(2)}, u32[]{:S(2)}) collective-permute-start(bf16[2,1024,512]{2,1,0:T(8,128)(2,1)} %pad_maximum_fusion), channel_id=1, source_target_pairs={{0,3},{1,2},{2,1},{3,0},{4,5},{5,4},{6,7},{7,6},{8,11},{9,10},{10,... | collective-permute-start | bytes 6291464 | tf_op jit(solution)/shard_map/ppermute | solution.py:29
  77.4 28.2 %collective-permute-start.15 = (bf16[1664,512]{1,0:T(8,128)(2,1)}, bf16[1664,512]{1,0:T(8,128)(2,1)}, u32[]{:S(2)}, u32[]{:S(2)}) collective-permute-start(bf16[1664,512]{1,0:T(8,128)(2,1)} %collective-permute-done.9.refs_3_), channel_id=1, source_target_pairs={{0,4},{1,5},{2,6},{3,7},{4,0},{5,1},{6,2},{7,3},{8,12},{9,13},{10,... | collective-permute-start | bytes 5111816 | tf_op jit(solution)/shard_map/ppermute | solution.py:29
  104.0 3.4 %copy-start.6 = (bf16[1408,512]{1,0:T(8,128)(2,1)}, bf16[1408,512]{1,0:T(8,128)(2,1)S(1)}, u32[]{:S(2)}) copy-start(bf16[1408,512]{1,0:T(8,128)(2,1)S(1)} %collective-permute-done.14.refs_4_) | copy-start | bytes 4325380
  104.0 3.4 %collective-permute-start.16 = (bf16[1408,512]{1,0:T(8,128)(2,1)S(1)}, bf16[1408,512]{1,0:T(8,128)(2,1)}, u32[]{:S(2)}, u32[]{:S(2)}) collective-permute-start(bf16[1408,512]{1,0:T(8,128)(2,1)S(1)} %collective-permute-done.14.refs_4_), channel_id=1, source_target_pairs={{0,4},{1,5},{2,6},{3,7},{4,0},{5,1},{6,2},{7,3},{8,12},{9,13},{10,... | collective-permute-start | bytes 4325384 | tf_op jit(solution)/shard_map/ppermute | solution.py:29
  107.3 1.4 copy-start.7
  108.7 19.9 %copy-start.12 = (f32[128,128]{1,0:T(8,128)S(1)}, f32[128,128]{1,0:T(8,128)}, u32[]{:S(2)}) copy-start(f32[128,128]{1,0:T(8,128)} %hadamard_signs.1) | copy-start | bytes 196612
  108.7 20.4 %copy-start.2 = (bf16[1,512,512]{2,1,0:T(8,128)(2,1)S(1)}, bf16[1,512,512]{2,1,0:T(8,128)(2,1)}, u32[]{:S(2)}) copy-start(bf16[1,512,512]{2,1,0:T(8,128)(2,1)} %param.7) | copy-start | bytes 1572868
  108.7 20.4 %copy-start.5 = (bf16[512,512]{1,0:T(8,128)(2,1)S(1)}, bf16[512,512]{1,0:T(8,128)(2,1)}, u32[]{:S(2)}) copy-start(bf16[512,512]{1,0:T(8,128)(2,1)} %copy-done.3) | copy-start | bytes 1572868
  119.5 20.8 %collective-permute-start.19 = (bf16[768,512]{1,0:T(8,128)(2,1)}, bf16[768,512]{1,0:T(8,128)(2,1)}, u32[]{:S(2)}, u32[]{:S(2)}) collective-permute-start(bf16[768,512]{1,0:T(8,128)(2,1)} %get-tuple-element.69), channel_id=1, source_target_pairs={{0,2},{1,3},{2,10},{3,11},{4,6},{5,7},{6,14},{7,15},{8,0},{9,1},{1... | collective-permute-start | bytes 2359304 | tf_op jit(solution)/shard_map/ppermute | solution.py:29
  121.1 36.3 %collective-permute-start.20 = (bf16[768,512]{1,0:T(8,128)(2,1)}, bf16[768,512]{1,0:T(8,128)(2,1)}, u32[]{:S(2)}, u32[]{:S(2)}) collective-permute-start(bf16[768,512]{1,0:T(8,128)(2,1)} %get-tuple-element.70), channel_id=1, source_target_pairs={{0,3},{1,2},{2,11},{3,10},{4,7},{5,6},{6,15},{7,14},{8,1},{9,0},{1... | collective-permute-start | bytes 2359304 | tf_op jit(solution)/shard_map/ppermute | solution.py:29
  122.1 38.4 %collective-permute-start.17 = (bf16[768,512]{1,0:T(8,128)(2,1)}, bf16[768,512]{1,0:T(8,128)(2,1)S(1)}, u32[]{:S(2)}, u32[]{:S(2)}) collective-permute-start(bf16[768,512]{1,0:T(8,128)(2,1)} %get-tuple-element.64), channel_id=1, source_target_pairs={{0,10},{1,11},{2,2},{3,3},{4,14},{5,15},{6,6},{7,7},{8,8},{9,9},{1... | collective-permute-start | bytes 2359304 | tf_op jit(solution)/shard_map/ppermute | solution.py:29
  126.8 35.7 %collective-permute-start.18 = (bf16[768,512]{1,0:T(8,128)(2,1)}, bf16[768,512]{1,0:T(8,128)(2,1)S(1)}, u32[]{:S(2)}, u32[]{:S(2)}) collective-permute-start(bf16[768,512]{1,0:T(8,128)(2,1)} %get-tuple-element.65), channel_id=1, source_target_pairs={{0,11},{1,10},{2,3},{3,2},{4,15},{5,14},{6,7},{7,6},{8,9},{9,8},{1... | collective-permute-start | bytes 2359304 | tf_op jit(solution)/shard_map/ppermute | solution.py:29
